TPU v7x, 32 devices: a whole 2x2x4 slice. The times are simulated.
32 devices in a mesh: gx: 4 (over y, core), gy: 8 (over z, x).
Axes of the slice: x: 2, y: 2, z: 4, core: 2. Of those that a mesh axis runs over, the one named last changes fastest.
Arguments:
- right_side: float32 [2, 64, 256, 256], P(None, 'gx', 'gy'), may hold values from -11 to 11
- coupling_from: float32 [64, 256, 256], P('gx', 'gy'), may hold values from 0.6 to 1.4
- coupling_to: float32 [64, 256, 256], P('gx', 'gy'), may hold values from 0.6 to 1.4
- mass_real: float32 [64, 256, 256], P('gx', 'gy'), may hold values from 0.9 to 1.2
- damping: float32 [64, 256, 256], P('gx', 'gy'), may hold values from 0.1 to 0.6
Outputs:
- solution: float32 [2, 64, 256, 256], P(None, 'gx', 'gy')
- residual: float32 [2, 64, 256, 256], P(None, 'gx', 'gy')
All inputs are finite; a program needn't handle non-finite values.
Results may differ from a plain program's by a relative error of at most 0.0003.
Values sent between devices are 32-bit elements; how exact they have to be, the bound alone decides.
No kernel may reach another device: no remote copies, remote signals or barrier semaphores. Data moves between devices by JAX's collectives and lax.ppermute only.
A program may use at most 64 MiB of HBM per device.

v0:
```python
import jax
import jax.numpy as jnp
from jax import lax
from jax.sharding import PartitionSpec as P

ITERS = 2


OMEGA = 0.8
EPSILON = 1e-06


def with_halo(shard, sides, width):
    for axis, dim in sides:
        peers, length = (lax.axis_size(axis), shard.shape[dim])
        up = [(i, (i + 1) % peers) for i in range(peers - 1)]
        down = [(j, i) for i, j in up]
        last = lax.slice_in_dim(shard, length - width, length, axis=dim)
        initial = lax.slice_in_dim(shard, 0, width, axis=dim)
        before = lax.ppermute(last, axis, up)
        after = lax.ppermute(initial, axis, down)
        shard = jnp.concatenate([before, shard, after], axis=dim)
    return shard


def neighbours_valid(extended):
    along_x = extended[:, :-2] + 2.0 * extended[:, 1:-1] + extended[:, 2:]
    along_y = along_x[:, :, :-2] + 2.0 * along_x[:, :, 1:-1] + along_x[:, :, 2:]
    padded = jnp.pad(along_y, ((0, 0), (0, 0), (0, 0), (1, 1)))
    total = padded[:, :, :, :-2] + 2.0 * along_y + padded[:, :, :, 2:]
    center = extended[:, 1:-1, 1:-1]
    return (total - 8.0 * center) / 160.0


def complex_mul(real_part, imag_part, field):
    return jnp.stack(
        [real_part * field[0] - imag_part * field[1], real_part * field[1] + imag_part * field[0]]
    )


def complex_div(numer, denom):
    scale = denom[0] * denom[0] + denom[1] * denom[1]
    return (
        (numer[0] * denom[0] + numer[1] * denom[1]) / scale,
        (numer[1] * denom[0] - numer[0] * denom[1]) / scale,
    )


def local_product(left, right):
    return (
        jnp.sum(left[0] * right[0] + left[1] * right[1]),
        jnp.sum(left[0] * right[1] - left[1] * right[0]),
    )


def local(right_side, coupling_from, coupling_to, mass_real, damping):
    shift_im = damping + 0.5 * mass_real
    modulus = mass_real * mass_real + shift_im * shift_im
    inv_re = mass_real / modulus
    inv_im = -shift_im / modulus

    def precond_apply(source):
        first = OMEGA * complex_mul(inv_re, inv_im, source)
        rim_first = with_halo(coupling_from * first, (("gx", 1), ("gy", 2)), 1)
        applied = complex_mul(mass_real, shift_im, first) - coupling_to * neighbours_valid(
            rim_first
        )
        second = first + OMEGA * complex_mul(inv_re, inv_im, source - applied)
        rim_second = with_halo(coupling_from * second, (("gx", 1), ("gy", 2)), 1)
        image = complex_mul(mass_real, damping, second) - coupling_to * neighbours_valid(rim_second)
        return (second, image)

    solution = jnp.zeros_like(right_side)
    residual = right_side
    direction = right_side
    rho = lax.psum(local_product(right_side, residual), ("gx", "gy"))
    for step in range(ITERS):
        dhat, image = precond_apply(direction)
        denom = lax.psum(local_product(right_side, image), ("gx", "gy"))
        alpha = complex_div(rho, denom)
        half = residual - complex_mul(alpha[0], alpha[1], image)
        hhat, second_image = precond_apply(half)
        prod_local = local_product(second_image, half)
        norm_local = jnp.sum(second_image[0] * second_image[0] + second_image[1] * second_image[1])
        pair = lax.psum((prod_local[0], prod_local[1], norm_local), ("gx", "gy"))
        norm_tt = pair[2] + EPSILON
        omega = (pair[0] / norm_tt, pair[1] / norm_tt)
        solution = (
            solution + complex_mul(alpha[0], alpha[1], dhat) + complex_mul(omega[0], omega[1], hhat)
        )
        residual = half - complex_mul(omega[0], omega[1], second_image)
        if step + 1 < ITERS:
            rho_next = lax.psum(local_product(right_side, residual), ("gx", "gy"))
            ratio = complex_div(rho_next, rho)
            factor = complex_div(alpha, omega)
            beta = (
                ratio[0] * factor[0] - ratio[1] * factor[1],
                ratio[0] * factor[1] + ratio[1] * factor[0],
            )
            direction = residual + complex_mul(
                beta[0], beta[1], direction - complex_mul(omega[0], omega[1], image)
            )
            rho = rho_next
    return (solution, residual)


def solution(mesh):
    return jax.shard_map(
        local,
        mesh=mesh,
        in_specs=(
            P(None, "gx", "gy", None),
            P("gx", "gy", None),
            P("gx", "gy", None),
            P("gx", "gy", None),
            P("gx", "gy", None),
        ),
        out_specs=(P(None, "gx", "gy", None), P(None, "gx", "gy", None)),
        check_vma=False,
    )
```

profile of v0, /device:TPU:0, one launch (start us, length us, event | category | flops | bytes accessed | tf_op | source)
XLA Modules:
  0.0 419.5 jit_solution(12997510342528725631)
XLA Ops:
  7.6 3.7 collective-permute-done.1
  16.4 4.2 %collective-permute-done.3 = f32[2,18,1,256]{3,2,1,0:T(1,128)S(1)} collective-permute-done((f32[2,18,1,256]{3,2,1,0:T(1,128)S(1)}, f32[2,18,1,256]{3,2,1,0:T(1,128)S(1)}, u32[]{:S(2)}, u32[]{:S(2)}) %collective-permute-start.3) | collective-permute-done | bytes 36896 | tf_op jit(solution)/shard_map/ppermute | solution.py:21
  23.3 3.4 collective-permute-start.4
  30.8 4.4 %collective-permute-start.6 = (f32[2,18,1,256]{3,2,1,0:T(1,128)S(1)}, f32[2,18,1,256]{3,2,1,0:T(1,128)S(1)}, u32[]{:S(2)}, u32[]{:S(2)}) collective-permute-start(f32[2,18,1,256]{3,2,1,0:T(1,128)S(1)} %get-tuple-element.83), channel_id=1, source_target_pairs={{0,1},{1,2},{2,3},{3,4},{4,5},{5,6},{6,7},{8,9},{9,10},{10,11},{11... | collective-permute-start | bytes 110600 | tf_op jit(solution)/shard_map/ppermute | solution.py:20
  36.8 4.2 %collective-permute-done.7 = f32[2,18,1,256]{3,2,1,0:T(1,128)S(1)} collective-permute-done((f32[2,18,1,256]{3,2,1,0:T(1,128)S(1)}, f32[2,18,1,256]{3,2,1,0:T(1,128)S(1)}, u32[]{:S(2)}, u32[]{:S(2)}) %collective-permute-start.7) | collective-permute-done | bytes 36896 | tf_op jit(solution)/shard_map/ppermute | solution.py:21
  44.4 42.1 %all-reduce.12 = (f32[]{:T(128)}, f32[]{:T(128)}, f32[]{:T(128)}, f32[]{:T(128)}) all-reduce(f32[]{:T(128)} %get-tuple-element.14, f32[]{:T(128)} %get-tuple-element.11, f32[]{:T(128)} %get-tuple-element.15, f32[]{:T(128)} %get-tuple-element.10), channel_id=1, replica_groups=mesh['gx'=4,'gy'=8] {'gx','gy'}, use_global_device_ids=true, to_apply=%region_5.6 | all-reduce | flops 4 | bytes 32 | tf_op jit(solution)/shard_map/psum | solution.py:76
  100.1 4.6 %collective-permute-done.9 = f32[2,1,32,256]{3,2,1,0:T(8,128)S(1)} collective-permute-done((f32[2,1,32,256]{3,2,1,0:T(8,128)S(1)}, f32[2,1,32,256]{3,2,1,0:T(8,128)S(1)}, u32[]{:S(2)}, u32[]{:S(2)}) %collective-permute-start.9) | collective-permute-done | bytes 65568 | tf_op jit(solution)/shard_map/ppermute | solution.py:21
  108.8 4.2 %collective-permute-done.11 = f32[2,18,1,256]{3,2,1,0:T(1,128)S(1)} collective-permute-done((f32[2,18,1,256]{3,2,1,0:T(1,128)S(1)}, f32[2,18,1,256]{3,2,1,0:T(1,128)S(1)}, u32[]{:S(2)}, u32[]{:S(2)}) %collective-permute-start.11) | collective-permute-done | bytes 36896 | tf_op jit(solution)/shard_map/ppermute | solution.py:21
  117.6 3.4 collective-permute-start.12
  126.2 4.0 collective-permute-start.14
  138.9 42.3 %all-reduce.11 = (f32[]{:T(128)}, f32[]{:T(128)}, f32[]{:T(128)}) all-reduce(f32[]{:T(128)} %get-tuple-element.9, f32[]{:T(128)} %get-tuple-element.13, f32[]{:T(128)} %get-tuple-element.8), channel_id=1, replica_groups=mesh['gx'=4,'gy'=8] {'gx','gy'}, use_global_device_ids=true, to_apply=%region_13.14 | all-reduce | flops 3 | bytes 24 | tf_op jit(solution)/shard_map/psum | solution.py:85
  187.9 39.8 %all-reduce.10 = (f32[]{:T(128)}, f32[]{:T(128)}) all-reduce(f32[]{:T(128)} %get-tuple-element.7, f32[]{:T(128)} %get-tuple-element.6), channel_id=1, replica_groups=mesh['gx'=4,'gy'=8] {'gx','gy'}, use_global_device_ids=true, to_apply=%region_15.16 | all-reduce | flops 2 | bytes 16 | tf_op jit(solution)/shard_map/psum | solution.py:93
  241.4 4.6 %collective-permute-done.17 = f32[2,1,32,256]{3,2,1,0:T(8,128)S(1)} collective-permute-done((f32[2,1,32,256]{3,2,1,0:T(8,128)S(1)}, f32[2,1,32,256]{3,2,1,0:T(8,128)S(1)}, u32[]{:S(2)}, u32[]{:S(2)}) %collective-permute-start.17) | collective-permute-done | bytes 65568 | tf_op jit(solution)/shard_map/ppermute | solution.py:21
  250.5 4.6 %collective-permute-done.19 = f32[2,18,1,256]{3,2,1,0:T(1,128)S(1)} collective-permute-done((f32[2,18,1,256]{3,2,1,0:T(1,128)S(1)}, f32[2,18,1,256]{3,2,1,0:T(1,128)S(1)}, u32[]{:S(2)}, u32[]{:S(2)}) %collective-permute-start.19) | collective-permute-done | bytes 36896 | tf_op jit(solution)/shard_map/ppermute | solution.py:21
  258.1 3.7 collective-permute-start.20
  265.6 4.8 %collective-permute-start.22 = (f32[2,18,1,256]{3,2,1,0:T(1,128)S(1)}, f32[2,18,1,256]{3,2,1,0:T(1,128)S(1)}, u32[]{:S(2)}, u32[]{:S(2)}) collective-permute-start(f32[2,18,1,256]{3,2,1,0:T(1,128)S(1)} %get-tuple-element.75), channel_id=1, source_target_pairs={{0,1},{1,2},{2,3},{3,4},{4,5},{5,6},{6,7},{8,9},{9,10},{10,11},{11... | collective-permute-start | bytes 110600 | tf_op jit(solution)/shard_map/ppermute | solution.py:20
  272.1 4.2 %collective-permute-done.23 = f32[2,18,1,256]{3,2,1,0:T(1,128)S(1)} collective-permute-done((f32[2,18,1,256]{3,2,1,0:T(1,128)S(1)}, f32[2,18,1,256]{3,2,1,0:T(1,128)S(1)}, u32[]{:S(2)}, u32[]{:S(2)}) %collective-permute-start.23) | collective-permute-done | bytes 36896 | tf_op jit(solution)/shard_map/ppermute | solution.py:21
  279.5 41.0 %all-reduce.9 = (f32[]{:T(128)}, f32[]{:T(128)}) all-reduce(f32[]{:T(128)} %get-tuple-element.5, f32[]{:T(128)} %get-tuple-element.4), channel_id=1, replica_groups=mesh['gx'=4,'gy'=8] {'gx','gy'}, use_global_device_ids=true, to_apply=%region_19.20 | all-reduce | flops 2 | bytes 16 | tf_op jit(solution)/shard_map/psum | solution.py:79
  335.2 3.4 collective-permute-done.25
  343.5 4.1 collective-permute-done.27
  350.6 3.4 collective-permute-start.28
  358.2 3.8 collective-permute-start.30
  363.6 4.2 %collective-permute-done.31 = f32[2,18,1,256]{3,2,1,0:T(1,128)S(1)} collective-permute-done((f32[2,18,1,256]{3,2,1,0:T(1,128)S(1)}, f32[2,18,1,256]{3,2,1,0:T(1,128)S(1)}, u32[]{:S(2)}, u32[]{:S(2)}) %collective-permute-start.31) | collective-permute-done | bytes 36896 | tf_op jit(solution)/shard_map/ppermute | solution.py:21
  370.1 40.6 %all-reduce.8 = (f32[]{:T(128)}, f32[]{:T(128)}, f32[]{:T(128)}) all-reduce(f32[]{:T(128)} %get-tuple-element.3, f32[]{:T(128)} %get-tuple-element.12, f32[]{:T(128)} %get-tuple-element.2), channel_id=1, replica_groups=mesh['gx'=4,'gy'=8] {'gx','gy'}, use_global_device_ids=true, to_apply=%region_27.28 | all-reduce | flops 3 | bytes 24 | tf_op jit(solution)/shard_map/psum | solution.py:85
  (257 shorter events, 108.2 us)
Async XLA Ops:
  6.0 5.3 %collective-permute-start.1 = (f32[2,1,32,256]{3,2,1,0:T(8,128)S(1)}, f32[2,1,32,256]{3,2,1,0:T(8,128)S(1)}, u32[]{:S(2)}, u32[]{:S(2)}) collective-permute-start(f32[2,1,32,256]{3,2,1,0:T(8,128)S(1)} %get-tuple-element.130), channel_id=1, source_target_pairs={{8,0},{16,8},{24,16},{9,1},{17,9},{25,17},{10,2},{18,10},{26,18},{... | collective-permute-start | bytes 196616 | tf_op jit(solution)/shard_map/ppermute | solution.py:21
  11.4 5.0 %collective-permute-start.2 = (f32[2,18,1,256]{3,2,1,0:T(1,128)S(1)}, f32[2,18,1,256]{3,2,1,0:T(1,128)S(1)}, u32[]{:S(2)}, u32[]{:S(2)}) collective-permute-start(f32[2,18,1,256]{3,2,1,0:T(1,128)S(1)} %get-tuple-element.85), channel_id=1, source_target_pairs={{0,1},{1,2},{2,3},{3,4},{4,5},{5,6},{6,7},{8,9},{9,10},{10,11},{11... | collective-permute-start | bytes 110600 | tf_op jit(solution)/shard_map/ppermute | solution.py:20
  14.8 5.9 %collective-permute-start.3 = (f32[2,18,1,256]{3,2,1,0:T(1,128)S(1)}, f32[2,18,1,256]{3,2,1,0:T(1,128)S(1)}, u32[]{:S(2)}, u32[]{:S(2)}) collective-permute-start(f32[2,18,1,256]{3,2,1,0:T(1,128)S(1)} %get-tuple-element.86), channel_id=1, source_target_pairs={{1,0},{2,1},{3,2},{4,3},{5,4},{6,5},{7,6},{9,8},{10,9},{11,10},{12... | collective-permute-start | bytes 110600 | tf_op jit(solution)/shard_map/ppermute | solution.py:21
  23.3 4.7 %collective-permute-start.4 = (f32[2,1,32,256]{3,2,1,0:T(8,128)S(1)}, f32[2,1,32,256]{3,2,1,0:T(8,128)S(1)}, u32[]{:S(2)}, u32[]{:S(2)}) collective-permute-start(f32[2,1,32,256]{3,2,1,0:T(8,128)S(1)} %get-tuple-element.125), channel_id=1, source_target_pairs={{0,8},{8,16},{16,24},{1,9},{9,17},{17,25},{2,10},{10,18},{18,26},{... | collective-permute-start | bytes 196616 | tf_op jit(solution)/shard_map/ppermute | solution.py:20
  30.8 6.0 %collective-permute-start.6 = (f32[2,18,1,256]{3,2,1,0:T(1,128)S(1)}, f32[2,18,1,256]{3,2,1,0:T(1,128)S(1)}, u32[]{:S(2)}, u32[]{:S(2)}) collective-permute-start(f32[2,18,1,256]{3,2,1,0:T(1,128)S(1)} %get-tuple-element.83), channel_id=1, source_target_pairs={{0,1},{1,2},{2,3},{3,4},{4,5},{5,6},{6,7},{8,9},{9,10},{10,11},{11... | collective-permute-start | bytes 110600 | tf_op jit(solution)/shard_map/ppermute | solution.py:20
  35.2 5.9 %collective-permute-start.7 = (f32[2,18,1,256]{3,2,1,0:T(1,128)S(1)}, f32[2,18,1,256]{3,2,1,0:T(1,128)S(1)}, u32[]{:S(2)}, u32[]{:S(2)}) collective-permute-start(f32[2,18,1,256]{3,2,1,0:T(1,128)S(1)} %get-tuple-element.84), channel_id=1, source_target_pairs={{1,0},{2,1},{3,2},{4,3},{5,4},{6,5},{7,6},{9,8},{10,9},{11,10},{12... | collective-permute-start | bytes 110600 | tf_op jit(solution)/shard_map/ppermute | solution.py:21
  98.8 5.9 %collective-permute-start.9 = (f32[2,1,32,256]{3,2,1,0:T(8,128)S(1)}, f32[2,1,32,256]{3,2,1,0:T(8,128)S(1)}, u32[]{:S(2)}, u32[]{:S(2)}) collective-permute-start(f32[2,1,32,256]{3,2,1,0:T(8,128)S(1)} %get-tuple-element.120), channel_id=1, source_target_pairs={{8,0},{16,8},{24,16},{9,1},{17,9},{25,17},{10,2},{18,10},{26,18},{... | collective-permute-start | bytes 196616 | tf_op jit(solution)/shard_map/ppermute | solution.py:21
  104.7 4.1 collective-permute-start.10
  107.2 5.9 %collective-permute-start.11 = (f32[2,18,1,256]{3,2,1,0:T(1,128)S(1)}, f32[2,18,1,256]{3,2,1,0:T(1,128)S(1)}, u32[]{:S(2)}, u32[]{:S(2)}) collective-permute-start(f32[2,18,1,256]{3,2,1,0:T(1,128)S(1)} %get-tuple-element.82), channel_id=1, source_target_pairs={{1,0},{2,1},{3,2},{4,3},{5,4},{6,5},{7,6},{9,8},{10,9},{11,10},{12... | collective-permute-start | bytes 110600 | tf_op jit(solution)/shard_map/ppermute | solution.py:21
  117.6 7.2 %collective-permute-start.12 = (f32[2,1,32,256]{3,2,1,0:T(8,128)S(1)}, f32[2,1,32,256]{3,2,1,0:T(8,128)S(1)}, u32[]{:S(2)}, u32[]{:S(2)}) collective-permute-start(f32[2,1,32,256]{3,2,1,0:T(8,128)S(1)} %get-tuple-element.115), channel_id=1, source_target_pairs={{0,8},{8,16},{16,24},{1,9},{9,17},{17,25},{2,10},{10,18},{18,26},{... | collective-permute-start | bytes 196616 | tf_op jit(solution)/shard_map/ppermute | solution.py:20
  126.2 6.8 %collective-permute-start.14 = (f32[2,18,1,256]{3,2,1,0:T(1,128)S(1)}, f32[2,18,1,256]{3,2,1,0:T(1,128)S(1)}, u32[]{:S(2)}, u32[]{:S(2)}) collective-permute-start(f32[2,18,1,256]{3,2,1,0:T(1,128)S(1)} %get-tuple-element.79), channel_id=1, source_target_pairs={{0,1},{1,2},{2,3},{3,4},{4,5},{5,6},{6,7},{8,9},{9,10},{10,11},{11... | collective-permute-start | bytes 110600 | tf_op jit(solution)/shard_map/ppermute | solution.py:20
  130.2 5.9 %collective-permute-start.15 = (f32[2,18,1,256]{3,2,1,0:T(1,128)S(1)}, f32[2,18,1,256]{3,2,1,0:T(1,128)S(1)}, u32[]{:S(2)}, u32[]{:S(2)}) collective-permute-start(f32[2,18,1,256]{3,2,1,0:T(1,128)S(1)} %get-tuple-element.80), channel_id=1, source_target_pairs={{1,0},{2,1},{3,2},{4,3},{5,4},{6,5},{7,6},{9,8},{10,9},{11,10},{12... | collective-permute-start | bytes 110600 | tf_op jit(solution)/shard_map/ppermute | solution.py:21
  240.1 5.9 %collective-permute-start.17 = (f32[2,1,32,256]{3,2,1,0:T(8,128)S(1)}, f32[2,1,32,256]{3,2,1,0:T(8,128)S(1)}, u32[]{:S(2)}, u32[]{:S(2)}) collective-permute-start(f32[2,1,32,256]{3,2,1,0:T(8,128)S(1)} %get-tuple-element.106), channel_id=1, source_target_pairs={{8,0},{16,8},{24,16},{9,1},{17,9},{25,17},{10,2},{18,10},{26,18},{... | collective-permute-start | bytes 196616 | tf_op jit(solution)/shard_map/ppermute | solution.py:21
  246.0 4.5 %collective-permute-start.18 = (f32[2,18,1,256]{3,2,1,0:T(1,128)S(1)}, f32[2,18,1,256]{3,2,1,0:T(1,128)S(1)}, u32[]{:S(2)}, u32[]{:S(2)}) collective-permute-start(f32[2,18,1,256]{3,2,1,0:T(1,128)S(1)} %get-tuple-element.77), channel_id=1, source_target_pairs={{0,1},{1,2},{2,3},{3,4},{4,5},{5,6},{6,7},{8,9},{9,10},{10,11},{11... | collective-permute-start | bytes 110600 | tf_op jit(solution)/shard_map/ppermute | solution.py:20
  248.9 6.3 %collective-permute-start.19 = (f32[2,18,1,256]{3,2,1,0:T(1,128)S(1)}, f32[2,18,1,256]{3,2,1,0:T(1,128)S(1)}, u32[]{:S(2)}, u32[]{:S(2)}) collective-permute-start(f32[2,18,1,256]{3,2,1,0:T(1,128)S(1)} %get-tuple-element.78), channel_id=1, source_target_pairs={{1,0},{2,1},{3,2},{4,3},{5,4},{6,5},{7,6},{9,8},{10,9},{11,10},{12... | collective-permute-start | bytes 110600 | tf_op jit(solution)/shard_map/ppermute | solution.py:21
  258.1 6.2 %collective-permute-start.20 = (f32[2,1,32,256]{3,2,1,0:T(8,128)S(1)}, f32[2,1,32,256]{3,2,1,0:T(8,128)S(1)}, u32[]{:S(2)}, u32[]{:S(2)}) collective-permute-start(f32[2,1,32,256]{3,2,1,0:T(8,128)S(1)} %get-tuple-element.101), channel_id=1, source_target_pairs={{0,8},{8,16},{16,24},{1,9},{9,17},{17,25},{2,10},{10,18},{18,26},{... | collective-permute-start | bytes 196616 | tf_op jit(solution)/shard_map/ppermute | solution.py:20
  265.6 6.4 %collective-permute-start.22 = (f32[2,18,1,256]{3,2,1,0:T(1,128)S(1)}, f32[2,18,1,256]{3,2,1,0:T(1,128)S(1)}, u32[]{:S(2)}, u32[]{:S(2)}) collective-permute-start(f32[2,18,1,256]{3,2,1,0:T(1,128)S(1)} %get-tuple-element.75), channel_id=1, source_target_pairs={{0,1},{1,2},{2,3},{3,4},{4,5},{5,6},{6,7},{8,9},{9,10},{10,11},{11... | collective-permute-start | bytes 110600 | tf_op jit(solution)/shard_map/ppermute | solution.py:20
  270.4 5.9 %collective-permute-start.23 = (f32[2,18,1,256]{3,2,1,0:T(1,128)S(1)}, f32[2,18,1,256]{3,2,1,0:T(1,128)S(1)}, u32[]{:S(2)}, u32[]{:S(2)}) collective-permute-start(f32[2,18,1,256]{3,2,1,0:T(1,128)S(1)} %get-tuple-element.76), channel_id=1, source_target_pairs={{1,0},{2,1},{3,2},{4,3},{5,4},{6,5},{7,6},{9,8},{10,9},{11,10},{12... | collective-permute-start | bytes 110600 | tf_op jit(solution)/shard_map/ppermute | solution.py:21
  332.6 6.0 %collective-permute-start.25 = (f32[2,1,32,256]{3,2,1,0:T(8,128)S(1)}, f32[2,1,32,256]{3,2,1,0:T(8,128)S(1)}, u32[]{:S(2)}, u32[]{:S(2)}) collective-permute-start(f32[2,1,32,256]{3,2,1,0:T(8,128)S(1)} %get-tuple-element.96), channel_id=1, source_target_pairs={{8,0},{16,8},{24,16},{9,1},{17,9},{25,17},{10,2},{18,10},{26,18},{... | collective-permute-start | bytes 196616 | tf_op jit(solution)/shard_map/ppermute | solution.py:21
  338.7 4.8 %collective-permute-start.26 = (f32[2,18,1,256]{3,2,1,0:T(1,128)S(1)}, f32[2,18,1,256]{3,2,1,0:T(1,128)S(1)}, u32[]{:S(2)}, u32[]{:S(2)}) collective-permute-start(f32[2,18,1,256]{3,2,1,0:T(1,128)S(1)} %get-tuple-element.73), channel_id=1, source_target_pairs={{0,1},{1,2},{2,3},{3,4},{4,5},{5,6},{6,7},{8,9},{9,10},{10,11},{11... | collective-permute-start | bytes 110600 | tf_op jit(solution)/shard_map/ppermute | solution.py:20
  341.7 5.9 %collective-permute-start.27 = (f32[2,18,1,256]{3,2,1,0:T(1,128)S(1)}, f32[2,18,1,256]{3,2,1,0:T(1,128)S(1)}, u32[]{:S(2)}, u32[]{:S(2)}) collective-permute-start(f32[2,18,1,256]{3,2,1,0:T(1,128)S(1)} %get-tuple-element.74), channel_id=1, source_target_pairs={{1,0},{2,1},{3,2},{4,3},{5,4},{6,5},{7,6},{9,8},{10,9},{11,10},{12... | collective-permute-start | bytes 110600 | tf_op jit(solution)/shard_map/ppermute | solution.py:21
  350.6 5.9 %collective-permute-start.28 = (f32[2,1,32,256]{3,2,1,0:T(8,128)S(1)}, f32[2,1,32,256]{3,2,1,0:T(8,128)S(1)}, u32[]{:S(2)}, u32[]{:S(2)}) collective-permute-start(f32[2,1,32,256]{3,2,1,0:T(8,128)S(1)} %get-tuple-element.91), channel_id=1, source_target_pairs={{0,8},{8,16},{16,24},{1,9},{9,17},{17,25},{2,10},{10,18},{18,26},{... | collective-permute-start | bytes 196616 | tf_op jit(solution)/shard_map/ppermute | solution.py:20
  358.2 5.4 %collective-permute-start.30 = (f32[2,18,1,256]{3,2,1,0:T(1,128)S(1)}, f32[2,18,1,256]{3,2,1,0:T(1,128)S(1)}, u32[]{:S(2)}, u32[]{:S(2)}) collective-permute-start(f32[2,18,1,256]{3,2,1,0:T(1,128)S(1)} %get-tuple-element.71), channel_id=1, source_target_pairs={{0,1},{1,2},{2,3},{3,4},{4,5},{5,6},{6,7},{8,9},{9,10},{10,11},{11... | collective-permute-start | bytes 110600 | tf_op jit(solution)/shard_map/ppermute | solution.py:20
  362.0 5.9 %collective-permute-start.31 = (f32[2,18,1,256]{3,2,1,0:T(1,128)S(1)}, f32[2,18,1,256]{3,2,1,0:T(1,128)S(1)}, u32[]{:S(2)}, u32[]{:S(2)}) collective-permute-start(f32[2,18,1,256]{3,2,1,0:T(1,128)S(1)} %get-tuple-element.72), channel_id=1, source_target_pairs={{1,0},{2,1},{3,2},{4,3},{5,4},{6,5},{7,6},{9,8},{10,9},{11,10},{12... | collective-permute-start | bytes 110600 | tf_op jit(solution)/shard_map/ppermute | solution.py:21
  (66 other events, 294.3 us)
where the time goes:
time: 422 us; the launch traced here: 419 us
  blocking collectives  206 us (49%)
  starting transfers between devices  70.2 us (17%)
  waiting for transfers between devices  55.9 us (13%)
  other arithmetic  46.7 us (11%)
  between operations  28.4 us (7%)
  local copies, waits for them, and re-layouts  12.4 us (3%)
    psum x2, blocking collectives, local(): pair = lax.psum((prod_local[0], prod_local[1], norm_local), ('gx', 'gy'))  82.9 us
    ppermute x16, waiting for transfers between devices, with_halo(): after = lax.ppermute(initial, axis, down)  55.1 us
    ppermute x16, starting transfers between devices, with_halo(): before = lax.ppermute(last, axis, up)  49.2 us
    psum x1, blocking collectives, local(): rho = lax.psum(local_product(right_side, residual), ('gx', 'gy'))  42.1 us
    psum x1, blocking collectives, local(): denom = lax.psum(local_product(right_side, image), ('gx', 'gy'))  41 us
    psum x1, blocking collectives, local(): rho_next = lax.psum(local_product(right_side, residual), ('gx', 'gy'))  39.8 us
    ppermute x16, starting transfers between devices, with_halo(): after = lax.ppermute(initial, axis, down)  21 us
    sub x10, other arithmetic, complex_mul(): real_part * field[0] - imag_part * field[1]  13.2 us
  transfers between devices with their start and end apart: 32, of which 22 were waited for; matrix products, arithmetic and copies ran while one was open for 2% of the time, Pallas kernels for 0%

commit v1 on v0

v1 whole, which is shorter than its diff:
```python
import jax
import jax.numpy as jnp
from jax import lax
from jax.experimental import pallas as pl
from jax.experimental.pallas import tpu as pltpu
from jax.sharding import PartitionSpec as P

OMEGA = 0.8
EPSILON = 1e-06
H = 4
AXES = ("gx", "gy")
F32 = jnp.float32
LIMIT = 48 * 1024 * 1024


def vmem(n):
    return [pl.BlockSpec(memory_space=pltpu.VMEM)] * n


def cmul(a, b):
    return (a[0] * b[0] - a[1] * b[1], a[0] * b[1] + a[1] * b[0])


def cconj(a):
    return (a[0], -a[1])


def cadd(a, b):
    return (a[0] + b[0], a[1] + b[1])


def csub(a, b):
    return (a[0] - b[0], a[1] - b[1])


def cdiv(n, d):
    scale = d[0] * d[0] + d[1] * d[1]
    return (
        (n[0] * d[0] + n[1] * d[1]) / scale,
        (n[1] * d[0] - n[0] * d[1]) / scale,
    )


def smooth_yz(plane):
    rows, lanes = plane.shape
    y = plane + plane + pltpu.roll(plane, 1, 0) + pltpu.roll(plane, rows - 1, 0)
    lane = lax.broadcasted_iota(jnp.int32, plane.shape, 1)
    up = jnp.where(lane == 0, 0.0, pltpu.roll(y, 1, 1))
    down = jnp.where(lane == lanes - 1, 0.0, pltpu.roll(y, lanes - 1, 1))
    return y + y + up + down


def weighted(ref, i):
    out = []
    for part in range(2):
        mid = ref[part, i]
        total = smooth_yz(ref[part, i - 1] + mid + mid + ref[part, i + 1])
        out.append((total - 8.0 * mid) * (1.0 / 160.0))
    return tuple(out)


def coefficients(c, mr, d):
    shift = d + 0.5 * mr
    mod = mr * mr + shift * shift
    den = mod * c
    inv = 1.0 / jnp.where(den == 0.0, 1.0, den)
    k = OMEGA * c * c * inv
    rc = mod * inv
    return (k * mr, -(k * shift)), (rc * mr, rc * d)


def half_step(u_ref, p_ref, w_ref, lo, hi):
    def body(i, carry):
        pw = cmul((p_ref[0, i], p_ref[1, i]), weighted(u_ref, i))
        w_ref[0, i] = 1.2 * u_ref[0, i] + pw[0]
        w_ref[1, i] = 1.2 * u_ref[1, i] + pw[1]
        return carry

    lax.fori_loop(lo, hi, body, 0)


def image_plane(w_ref, n_ref, i):
    nw = cmul((n_ref[0, i], n_ref[1, i]), (w_ref[0, i], w_ref[1, i]))
    return csub(nw, weighted(w_ref, i))


def total_of(ref):
    rows = ref[...].reshape(ref.shape[0], ref.shape[-1])
    tot = jnp.sum(rows, axis=0, keepdims=True)
    lane = lax.broadcasted_iota(jnp.int32, tot.shape, 1)
    return lambda k: jnp.sum(jnp.where(lane == k, tot, 0.0), axis=1, keepdims=True)


def pack_lanes(values):
    lane = lax.broadcasted_iota(jnp.int32, (1, 128), 1)
    row = jnp.zeros((1, 128), F32)
    for k, v in enumerate(values):
        s = jnp.sum(jnp.sum(v, axis=0, keepdims=True), axis=1, keepdims=True)
        row = jnp.where(lane == k, s, row)
    return row


def fold(x):
    rows, lanes = x.shape
    out = None
    for a in range(0, rows, 8):
        for b in range(0, lanes, 128):
            t = x[a : a + 8, b : b + 128]
            out = t if out is None else out + t
    return out


def shift_kernel(b_ref, cf_ref, ct_ref, mr_ref, d_ref, out_ref, u_ref, w_ref, p_ref, n_ref):
    nx, ny, nz = cf_ref.shape
    zero = jnp.zeros((ny + 8, nz), F32)
    for ref in (u_ref, w_ref):
        for part in range(2):
            ref[part, 0] = zero
            ref[part, nx + 1] = zero

    pad = jnp.zeros((8, nz), F32)

    def ext(x):
        return jnp.concatenate([x, pad], axis=0)

    def fill(i, carry):
        ct = ct_ref[i]
        r = 1.0 / ct
        p, n = coefficients(cf_ref[i] * ct, mr_ref[i], d_ref[i])
        u = cmul(p, (b_ref[0, i] * r, b_ref[1, i] * r))
        for part in range(2):
            p_ref[part, i + 1] = ext(p[part])
            n_ref[part, i + 1] = ext(n[part])
            u_ref[part, i + 1] = ext(u[part])
        return carry

    lax.fori_loop(0, nx, fill, 0)
    half_step(u_ref, p_ref, w_ref, 1, nx + 1)

    def dots(i, acc):
        y = image_plane(w_ref, n_ref, i + 1)
        ct = ct_ref[i]
        yr, yi = y[0][:ny] * ct, y[1][:ny] * ct
        br, bi = b_ref[0, i], b_ref[1, i]
        return (
            acc[0] + fold(br * yr + bi * yi),
            acc[1] + fold(br * yi - bi * yr),
            acc[2] + fold(br * br + bi * bi),
        )

    acc = lax.fori_loop(0, nx, dots, (jnp.zeros((8, 128), F32),) * 3)
    row = pack_lanes(acc)
    for k in range(out_ref.shape[0]):
        out_ref[k] = row


def local_shift(b, cf, ct, mr, d, peers):
    nx, ny, nz = cf.shape
    big = pltpu.VMEM((2, nx + 2, ny + 8, nz), F32)
    return pl.pallas_call(
        shift_kernel,
        out_shape=jax.ShapeDtypeStruct((peers, 1, 128), F32),
        in_specs=vmem(5),
        out_specs=pl.BlockSpec(memory_space=pltpu.VMEM),
        scratch_shapes=[big] * 4,
        compiler_params=pltpu.CompilerParams(vmem_limit_bytes=LIMIT),
    )(b, cf, ct, mr, d)


def pack_pair(first, second, top):
    sub = lax.broadcasted_iota(jnp.int32, first.shape, 0)
    rolled = pltpu.roll(second, 4, 0)
    if top:
        return jnp.where(sub < 4, first, rolled)
    return jnp.where(sub < 4, rolled, first)


def unpack_pair(right, left):
    sub = lax.broadcasted_iota(jnp.int32, right.shape, 0)
    first = jnp.where(sub < 4, right, left)
    second = pltpu.roll(jnp.where(sub < 4, left, right), 4, 0)
    return first, second


def pack_first_kernel(xl_ref, xr_ref, b_ref, cf_ref, ct_ref, mr_ref, d_ref, top_ref, bot_ref):
    nx, ny, _ = cf_ref.shape

    def own(rows):
        def get(i):
            ct = ct_ref[i, rows]
            r = 1.0 / ct
            return (
                b_ref[0, i, rows] * r,
                b_ref[1, i, rows] * r,
                cf_ref[i, rows] * ct,
                mr_ref[i, rows],
                d_ref[i, rows],
            )

        return get

    def halo(ref, rows):
        return lambda i: tuple(ref[f, i, rows] for f in range(5))

    for out_ref, rows, top in ((top_ref, pl.ds(0, 8), True), (bot_ref, pl.ds(ny - 8, 8), False)):

        def run(get, count, base):
            def body(j, carry):
                a, b = get(2 * j), get(2 * j + 1)
                plane = base + 2 * j
                out_ref[plane] = pack_pair(a[0], a[1], top)
                out_ref[plane + 1] = pack_pair(b[0], b[1], top)
                for f in range(3):
                    at = (nx + 2 * H) + f * (nx + 2 * H) // 2 + base // 2 + j
                    out_ref[at] = pack_pair(a[2 + f], b[2 + f], top)
                return carry

            lax.fori_loop(0, count // 2, body, 0)

        run(halo(xl_ref, rows), H, 0)
        run(own(rows), nx, H)
        run(halo(xr_ref, rows), H, H + nx)


def pack_later_kernel(xl_ref, xr_ref, v_ref, top_ref, bot_ref):
    nx, ny = v_ref.shape[1:3]
    for out_ref, rows, top in ((top_ref, pl.ds(0, 8), True), (bot_ref, pl.ds(ny - 8, 8), False)):
        for ref, count, base in ((xl_ref, H, 0), (v_ref, nx, H), (xr_ref, H, H + nx)):

            def body(i, carry):
                out_ref[base + i] = pack_pair(ref[0, i, rows], ref[1, i, rows], top)
                return carry

            lax.fori_loop(0, count, body, 0)


def first_kernel(
    th_ref, xl_ref, xr_ref, yl_ref, yr_ref, b_ref, cf_ref, ct_ref, mr_ref, d_ref,
    p_ref, n_ref, w0_ref, w1_ref, v1_ref, v2_ref, sl_ref, sr_ref,
    u_ref, w_ref, v_ref,
):
    nx, ny, nz = cf_ref.shape
    planes = nx + 2 * H
    th = shift_from(th_ref)

    def own(i):
        ct = ct_ref[i]
        r = 1.0 / ct
        return (b_ref[0, i] * r, b_ref[1, i] * r, cf_ref[i] * ct, mr_ref[i], d_ref[i])

    def halo(ref):
        return lambda i: tuple(ref[f, i] for f in range(5))

    def run(get, count, base):
        def body(j, carry):
            plane = base + 2 * j
            tails = []
            for k in range(2):
                tails.append(list(unpack_pair(yr_ref[plane + k], yl_ref[plane + k])))
            for f in range(3):
                at = planes + f * planes // 2 + base // 2 + j
                a, b = unpack_pair(yr_ref[at], yl_ref[at])
                tails[0].append(a)
                tails[1].append(b)
            for k in range(2):
                body_rows = get(2 * j + k)
                vr, vi, c, mr, d = (
                    jnp.concatenate([body_rows[f], tails[k][f]], axis=0) for f in range(5)
                )
                p, n = coefficients(c, mr, d)
                u = cmul(p, (vr, vi))
                v_ref[0, plane + k], v_ref[1, plane + k] = vr, vi
                for part in range(2):
                    p_ref[part, plane + k] = p[part]
                    n_ref[part, plane + k] = n[part]
                    u_ref[part, plane + k] = u[part]
            return carry

        lax.fori_loop(0, count // 2, body, 0)

    run(halo(xl_ref), H, 0)
    run(own, nx, H)
    run(halo(xr_ref), H, H + nx)

    half_step(u_ref, p_ref, w_ref, 1, planes - 1)

    def second(i, carry):
        y = csub(image_plane(w_ref, n_ref, i), cmul(th, (v_ref[0, i], v_ref[1, i])))
        u = cmul((p_ref[0, i], p_ref[1, i]), y)
        for part in range(2):
            v_ref[part, i] = y[part]
            u_ref[part, i] = u[part]
        return carry

    lax.fori_loop(2, planes - 2, second, 0)

    def keep(i, carry):
        for part in range(2):
            w0_ref[part, i] = w_ref[part, i + H, pl.ds(0, ny)]
            v1_ref[part, i] = v_ref[part, i + H, pl.ds(0, ny)]
        return carry

    lax.fori_loop(0, nx, keep, 0)
    half_step(u_ref, p_ref, w_ref, 3, planes - 3)

    def last(i, carry):
        at = i + H
        y = csub(image_plane(w_ref, n_ref, at), cmul(th, (v_ref[0, at], v_ref[1, at])))
        for part in range(2):
            v2_ref[part, i] = y[part][:ny]
            w1_ref[part, i] = w_ref[part, at, pl.ds(0, ny)]
        return carry

    lax.fori_loop(0, nx, last, 0)
    for part in range(2):
        for i in range(H):
            sl_ref[part, i] = v2_ref[part, i]
            sr_ref[part, i] = v2_ref[part, nx - H + i]


def shift_from(th_ref):
    pick = total_of(th_ref)
    den = pick(2)
    safe = jnp.where(den > 0.0, den, 1.0)
    return (
        jnp.where(den > 0.0, pick(0) / safe, 0.72),
        jnp.where(den > 0.0, pick(1) / safe, -0.28),
    )


def second_kernel(
    th_ref, xl_ref, xr_ref, yl_ref, yr_ref, p_ref, n_ref, b_ref, ct_ref, v1_ref, v2_ref,
    w2_ref, w3_ref, v3_ref, v4_ref, out_ref,
    u_ref, w_ref, v_ref,
):
    nx, ny, nz = ct_ref.shape
    planes = nx + 2 * H
    th = shift_from(th_ref)

    for ref, count, base in ((xl_ref, H, 0), (v2_ref, nx, H), (xr_ref, H, H + nx)):

        def fill(i, carry):
            at = base + i
            tail = unpack_pair(yr_ref[at], yl_ref[at])
            v = tuple(jnp.concatenate([ref[part, i], tail[part]], axis=0) for part in range(2))
            u = cmul((p_ref[0, at], p_ref[1, at]), v)
            for part in range(2):
                v_ref[part, at] = v[part]
                u_ref[part, at] = u[part]
            return carry

        lax.fori_loop(0, count, fill, 0)

    half_step(u_ref, p_ref, w_ref, 1, planes - 1)

    def second(i, carry):
        y = csub(image_plane(w_ref, n_ref, i), cmul(th, (v_ref[0, i], v_ref[1, i])))
        u = cmul((p_ref[0, i], p_ref[1, i]), y)
        for part in range(2):
            v_ref[part, i] = y[part]
            u_ref[part, i] = u[part]
        return carry

    lax.fori_loop(2, planes - 2, second, 0)

    def keep(i, carry):
        for part in range(2):
            w2_ref[part, i] = w_ref[part, i + H, pl.ds(0, ny)]
            v3_ref[part, i] = v_ref[part, i + H, pl.ds(0, ny)]
        return carry

    lax.fori_loop(0, nx, keep, 0)
    half_step(u_ref, p_ref, w_ref, 3, planes - 3)

    def last(i, carry):
        at = i + H
        y = csub(image_plane(w_ref, n_ref, at), cmul(th, (v_ref[0, at], v_ref[1, at])))
        for part in range(2):
            v4_ref[part, i] = y[part][:ny]
            w3_ref[part, i] = w_ref[part, at, pl.ds(0, ny)]
        return carry

    lax.fori_loop(0, nx, last, 0)

    def dots(i, acc):
        acc = list(acc)
        for a in range(0, ny, 8):
            rows = pl.ds(a, 8)
            ct = ct_ref[i, rows]
            vs = [(b_ref[0, i, rows], b_ref[1, i, rows])]
            for ref in (v1_ref, v2_ref, v3_ref, v4_ref):
                vs.append((ct * ref[0, i, rows], ct * ref[1, i, rows]))
            k = 0
            for left in range(5):
                for right in range(left, 5):
                    (lr, li), (rr, ri) = vs[left], vs[right]
                    acc[k] = acc[k] + fold(lr * rr + li * ri)
                    k += 1
                    if right > left:
                        acc[k] = acc[k] + fold(lr * ri - li * rr)
                        k += 1
        return tuple(acc)

    acc = lax.fori_loop(0, nx, dots, (jnp.zeros((8, 128), F32),) * 25)
    row = pack_lanes(acc)
    for k in range(out_ref.shape[0]):
        out_ref[k] = row


def recurrences(th, gram):
    def inner(x, y):
        total = None
        for i, xi in enumerate(x):
            part = None
            for j, yj in enumerate(y):
                t = cmul(gram(i, j), yj)
                part = t if part is None else cadd(part, t)
            t = cmul(cconj(xi), part)
            total = t if total is None else cadd(total, t)
        return total

    def apply(x):
        scaled = [cmul(th, c) for c in x]
        return [scaled[0]] + [cadd(x[k], scaled[k + 1]) for k in range(len(x) - 1)] + [x[-1]]

    def lincomb(x, s, y):
        out = []
        for k in range(max(len(x), len(y))):
            a = x[k] if k < len(x) else None
            b = cmul(s, y[k]) if k < len(y) else None
            out.append(b if a is None else a if b is None else cadd(a, b))
        return out

    def neg(s):
        return (-s[0], -s[1])

    one = (jnp.ones((1, 1), F32), jnp.zeros((1, 1), F32))
    residual, direction, shadow, answer = [one], [one], [one], []
    rho = inner(shadow, residual)
    for step in range(2):
        image = apply(direction)
        alpha = cdiv(rho, inner(shadow, image))
        half = lincomb(residual, neg(alpha), image)
        second = apply(half)
        prod = inner(second, half)
        norm = inner(second, second)[0] + EPSILON
        omega = (prod[0] / norm, prod[1] / norm)
        answer = lincomb(lincomb(answer, alpha, direction), omega, half)
        residual = lincomb(half, neg(omega), second)
        if step == 0:
            rho_next = inner(shadow, residual)
            beta = cmul(cdiv(rho_next, rho), cdiv(alpha, omega))
            direction = lincomb(residual, beta, lincomb(direction, neg(omega), image))
            rho = rho_next
    return answer, residual


def final_kernel(
    th_ref, g_ref, b_ref, cf_ref, ct_ref,
    w0_ref, w1_ref, w2_ref, w3_ref, v1_ref, v2_ref, v3_ref, v4_ref,
    sol_ref, res_ref,
):
    nx = cf_ref.shape[0]
    th = shift_from(th_ref)
    pick = total_of(g_ref)
    entries, k = {}, 0
    for left in range(5):
        for right in range(left, 5):
            if right > left:
                entries[left, right] = (pick(k), pick(k + 1))
                entries[right, left] = cconj(entries[left, right])
                k += 2
            else:
                entries[left, right] = (pick(k), jnp.zeros((1, 1), F32))
                k += 1
    answer, residual = recurrences(th, lambda i, j: entries[i, j])

    def body(i, carry):
        acc = None
        for c, ref in zip(answer, (w0_ref, w1_ref, w2_ref, w3_ref)):
            t = cmul(c, (ref[0, i], ref[1, i]))
            acc = t if acc is None else cadd(acc, t)
        inv = 1.0 / cf_ref[i]
        sol_ref[0, i] = acc[0] * inv
        sol_ref[1, i] = acc[1] * inv
        acc = None
        for c, ref in zip(residual[1:], (v1_ref, v2_ref, v3_ref, v4_ref)):
            t = cmul(c, (ref[0, i], ref[1, i]))
            acc = t if acc is None else cadd(acc, t)
        ct = ct_ref[i]
        t = cmul(residual[0], (b_ref[0, i], b_ref[1, i]))
        res_ref[0, i] = acc[0] * ct + t[0]
        res_ref[1, i] = acc[1] * ct + t[1]
        return carry

    lax.fori_loop(0, nx, body, 0)


def call(kernel, outs, scratch, *args):
    return pl.pallas_call(
        kernel,
        out_shape=[jax.ShapeDtypeStruct(s, F32) for s in outs],
        in_specs=vmem(len(args)),
        out_specs=vmem(len(outs)),
        scratch_shapes=[pltpu.VMEM(s, F32) for s in scratch],
        compiler_params=pltpu.CompilerParams(vmem_limit_bytes=LIMIT),
    )(*args)


def both_ways(to_lower, to_upper, axis):
    n = lax.axis_size(axis)
    up = [(i, i + 1) for i in range(n - 1)]
    down = [(i + 1, i) for i in range(n - 1)]
    return lax.ppermute(to_upper, axis, up), lax.ppermute(to_lower, axis, down)


def local(b, cf, ct, mr, d):
    nx, ny, nz = cf.shape
    peers = lax.axis_size("gx") * lax.axis_size("gy")
    planes = nx + 2 * H
    own = (2, nx, ny, nz)
    ext = (2, planes, ny + 2 * H, nz)

    def edge(s):
        return jnp.concatenate(
            [b[:, s] / ct[s], (cf[s] * ct[s])[None], mr[s][None], d[s][None]], axis=0
        )

    xl, xr = both_ways(edge(slice(0, H)), edge(slice(nx - H, nx)), "gx")
    th = local_shift(b, cf, ct, mr, d, peers)
    th = lax.all_to_all(th, AXES, 0, 0)
    count = planes + 3 * planes // 2
    top, bot = call(pack_first_kernel, [(count, 8, nz)] * 2, [], xl, xr, b, cf, ct, mr, d)
    yl, yr = both_ways(top, bot, "gy")
    p, n, w0, w1, v1, v2, sl, sr = call(
        first_kernel,
        [ext, ext, own, own, own, own, (2, H, ny, nz), (2, H, ny, nz)],
        [ext, ext, ext],
        th, xl, xr, yl, yr, b, cf, ct, mr, d,
    )
    xl, xr = both_ways(sl, sr, "gx")
    top, bot = call(pack_later_kernel, [(planes, 8, nz)] * 2, [], xl, xr, v2)
    yl, yr = both_ways(top, bot, "gy")
    w2, w3, v3, v4, g = call(
        second_kernel,
        [own, own, own, own, (peers, 1, 128)],
        [ext, ext, ext],
        th, xl, xr, yl, yr, p, n, b, ct, v1, v2,
    )
    g = lax.all_to_all(g, AXES, 0, 0)
    sol, res = call(
        final_kernel, [own, own], [], th, g, b, cf, ct, w0, w1, w2, w3, v1, v2, v3, v4
    )
    return sol, res


def solution(mesh):
    field, coef = P(None, "gx", "gy", None), P("gx", "gy", None)
    return jax.shard_map(
        local,
        mesh=mesh,
        in_specs=(field, coef, coef, coef, coef),
        out_specs=(field, field),
        check_vma=False,
    )
```

time: 422 us -> 116 us (0.27)
  blocking collectives: 206 us -> 35.3 us
  starting transfers between devices: 70.2 us -> 15.4 us
  other arithmetic: 46.7 us -> 1.32 us
  Pallas kernels: 0 us -> 43.9 us
  waiting for transfers between devices: 55.9 us -> 13.5 us
  between operations: 28.4 us -> 0.85 us
  local copies, waits for them, and re-layouts: 12.4 us -> 5.44 us
    psum x5 -> x0, blocking collectives: 206 us -> none  [the longest x2 82.9 us: local(): pair = lax.psum((prod_local[0], prod_local[1], norm_local), ('gx', 'gy'))]
    ppermute x32 -> x8, starting transfers between devices: 70.2 us -> 15.4 us  [the longest x4 10.2 us: both_ways(): lax.ppermute(to_upper, axis, up)]
    pallas_call x0 -> x6, Pallas kernels: none -> 43.9 us  [the longest x5 38.9 us: call(): pl.pallas_call(kernel, out_shape=[jax.ShapeDtypeStruct(s, F32) for s in o...]
    ppermute x32 -> x8, waiting for transfers between devices: 55.9 us -> 13.5 us  [the longest x4 11.4 us: both_ways(): lax.ppermute(to_lower, axis, down)]
    all_to_all x0 -> x2, blocking collectives: none -> 35.3 us  [the longest x1 20.7 us: local(): th = lax.all_to_all(th, AXES, 0, 0)]
    sub x23 -> x0, other arithmetic: 23.9 us -> none  [the longest x10 13.2 us: complex_mul(): real_part * field[0] - imag_part * field[1]]
    unnamed x116 -> x22, local copies, waits for them, and re-layouts: 12.3 us -> 4.21 us
    another operation x17 -> x0, other arithmetic: 6.55 us -> none  [complex_mul(): jnp.stack([real_part * field[0] - imag_part * field[1], real_part * field...]
  transfers between devices with their start and end apart: 32 -> 8, of which waited for: 22 -> 5; matrix products, arithmetic and copies ran while one was open for 2% -> 0% of each run, Pallas kernels for 0% -> 4%
where the time goes in v1:
time: 116 us
  Pallas kernels  43.9 us (38%)
  blocking collectives  35.3 us (30%)
  starting transfers between devices  15.4 us (13%)
  waiting for transfers between devices  13.5 us (12%)
  local copies, waits for them, and re-layouts  5.44 us (5%)
  other arithmetic  1.32 us (1%)
    pallas_call x5, Pallas kernels, call(): pl.pallas_call(kernel, out_shape=[jax.ShapeDtypeStruct(s, F32) for s in o...  38.9 us
    all_to_all x1, blocking collectives, local(): th = lax.all_to_all(th, AXES, 0, 0)  20.7 us
    all_to_all x1, blocking collectives, local(): g = lax.all_to_all(g, AXES, 0, 0)  14.5 us
    ppermute x4, waiting for transfers between devices, both_ways(): lax.ppermute(to_lower, axis, down)  11.4 us
    ppermute x4, starting transfers between devices, both_ways(): lax.ppermute(to_upper, axis, up)  10.2 us
    ppermute x4, starting transfers between devices, both_ways(): lax.ppermute(to_lower, axis, down)  5.17 us
    pallas_call x1, Pallas kernels, local_shift(): pl.pallas_call(shift_kernel, out_shape=jax.ShapeDtypeStruct((peers, 1, 12...  4.96 us
    unnamed x22, local copies, waits for them, and re-layouts  4.21 us
  transfers between devices with their start and end apart: 8, of which 5 were waited for; matrix products, arithmetic and copies ran while one was open for 0% of the time, Pallas kernels for 4%

profile of v1, /device:TPU:0, one launch (start us, length us, event | category | flops | bytes accessed | tf_op | source)
XLA Modules:
  0.0 115.7 jit_solution(11899853103556837699)
XLA Ops:
  0.6 1.2 %slice_bitcast_fusion = (f32[1,4,32,256]{3,2,1,0:T(8,128)S(1)}, f32[1,4,32,256]{3,2,1,0:T(8,128)S(1)}, f32[1,4,32,256]{3,2,1,0:T(8,128)S(1)}, f32[1,4,32,256]{3,2,1,0:T(8,128)S(1)}) fusion(f32[16,32,256]{2,1,0:T(8,128)} %d_ref.5, f32[16,32,256]{2,1,0:T(8,128)} %mr_ref.5), kind=kLoop, calls=%fused_computation.4 | loop fusion | bytes 1048576 | tf_op jit(solution)/shard_map/broadcast_in_dim | solution.py:526
  1.9 1.1 multiply_bitcast_fusion
  3.2 2.5 %collective-permute-start = (f32[5,4,32,256]{3,2,1,0:T(8,128)S(1)}, f32[5,4,32,256]{3,2,1,0:T(8,128)S(1)}, u32[]{:S(2)}, u32[]{:S(2)}) collective-permute-start(f32[5,4,32,256]{3,2,1,0:T(8,128)S(1)} %pad_maximum_fusion), channel_id=1, source_target_pairs={{0,8},{8,16},{16,24},{1,9},{9,17},{17,25},{2,10},{10,18},{18,26},{... | collective-permute-start | bytes 1966088 | tf_op jit(solution)/shard_map/ppermute | solution.py:514
  5.8 1.3 %collective-permute-start.1 = (f32[5,4,32,256]{3,2,1,0:T(8,128)S(1)}, f32[5,4,32,256]{3,2,1,0:T(8,128)S(1)}, u32[]{:S(2)}, u32[]{:S(2)}) collective-permute-start(f32[5,4,32,256]{3,2,1,0:T(8,128)S(1)} %pad_maximum_fusion.1), channel_id=1, source_target_pairs={{8,0},{16,8},{24,16},{9,1},{17,9},{25,17},{10,2},{18,10},{26,18},{... | collective-permute-start | bytes 1966088 | tf_op jit(solution)/shard_map/ppermute | solution.py:514
  7.4 4.5 %collective-permute-done.1.xr_ref = f32[5,4,32,256]{3,2,1,0:T(8,128)S(1)} collective-permute-done((f32[5,4,32,256]{3,2,1,0:T(8,128)S(1)}, f32[5,4,32,256]{3,2,1,0:T(8,128)S(1)}, u32[]{:S(2)}, u32[]{:S(2)}) %collective-permute-start.1) | collective-permute-done | bytes 655392 | tf_op jit(solution)/shard_map/ppermute | solution.py:514
  12.2 3.4 %collective-permute-start.2 = (f32[60,8,256]{2,1,0:T(8,128)S(1)}, f32[60,8,256]{2,1,0:T(8,128)S(1)}, u32[]{:S(2)}, u32[]{:S(2)}) collective-permute-start(f32[60,8,256]{2,1,0:T(8,128)S(1)} %get-tuple-element.19), channel_id=1, source_target_pairs={{0,1},{1,2},{2,3},{3,4},{4,5},{5,6},{6,7},{8,9},{9,10},{10,11},{11... | collective-permute-start | bytes 1474568 | tf_op jit(solution)/shard_map/ppermute | solution.py:514
  15.7 1.3 %collective-permute-start.3 = (f32[60,8,256]{2,1,0:T(8,128)S(1)}, f32[60,8,256]{2,1,0:T(8,128)S(1)}, u32[]{:S(2)}, u32[]{:S(2)}) collective-permute-start(f32[60,8,256]{2,1,0:T(8,128)S(1)} %get-tuple-element.20), channel_id=1, source_target_pairs={{1,0},{2,1},{3,2},{4,3},{5,4},{6,5},{7,6},{9,8},{10,9},{11,10},{12... | collective-permute-start | bytes 1474568 | tf_op jit(solution)/shard_map/ppermute | solution.py:514
  17.0 5.0 %shard_map.68 = f32[32,1,128]{2,1,0:T(1,128)S(1)} custom-call(f32[2,16,32,256]{3,2,1,0:T(8,128)S(1)} %copy-done, f32[16,32,256]{2,1,0:T(8,128)S(1)} %copy-done.3, f32[16,32,256]{2,1,0:T(8,128)S(1)} %copy-done.2, f32[16,32,256]{2,1,0:T(8,128)S(1)} %copy-done.5, f32[16,32,256]{2,1,0:T(8,128)S(1)} %copy-done.6), custom_call_target="tpu_custom_call" | custom-call | tf_op jit(solution)/shard_map/pallas_call | solution.py:160
  21.9 20.7 %all_to_all.10.th_ref = f32[32,1,128]{2,1,0:T(1,128)S(1)} all-to-all(f32[32,1,128]{2,1,0:T(1,128)S(1)} %shard_map.68), channel_id=1, replica_groups=mesh['gx'=4,'gy'=8] {'gx','gy'}, dimensions={0} | all-to-all | bytes 32768 | tf_op jit(solution)/shard_map/all_to_all | solution.py:531
  42.7 16.1 %shard_map.70 = (f32[2,24,40,256]{3,2,1,0:T(8,128)}, f32[2,24,40,256]{3,2,1,0:T(8,128)}, f32[2,16,32,256]{3,2,1,0:T(8,128)S(1)}, f32[2,16,32,256]{3,2,1,0:T(8,12...) custom-call(f32[32,1,128]{2,1,0:T(1,128)S(1)} %all_to_all.10.th_ref,, ...), custom_call_target="tpu_custom_call" | custom-call | tf_op jit(solution)/shard_map/pallas_call | solution.py:500
  58.8 1.7 %collective-permute-start.4 = (f32[2,4,32,256]{3,2,1,0:T(8,128)S(1)}, f32[2,4,32,256]{3,2,1,0:T(8,128)S(1)}, u32[]{:S(2)}, u32[]{:S(2)}) collective-permute-start(f32[2,4,32,256]{3,2,1,0:T(8,128)S(1)} %get-tuple-element.21), channel_id=1, source_target_pairs={{0,8},{8,16},{16,24},{1,9},{9,17},{17,25},{2,10},{10,18},{18,26},{... | collective-permute-start | bytes 786440 | tf_op jit(solution)/shard_map/ppermute | solution.py:514
  60.5 1.3 %collective-permute-start.5 = (f32[2,4,32,256]{3,2,1,0:T(8,128)S(1)}, f32[2,4,32,256]{3,2,1,0:T(8,128)S(1)}, u32[]{:S(2)}, u32[]{:S(2)}) collective-permute-start(f32[2,4,32,256]{3,2,1,0:T(8,128)S(1)} %get-tuple-element.22), channel_id=1, source_target_pairs={{8,0},{16,8},{24,16},{9,1},{17,9},{25,17},{10,2},{18,10},{26,18},{... | collective-permute-start | bytes 786440 | tf_op jit(solution)/shard_map/ppermute | solution.py:514
  61.8 2.5 %collective-permute-done.5.xr_ref = f32[2,4,32,256]{3,2,1,0:T(8,128)S(1)} collective-permute-done((f32[2,4,32,256]{3,2,1,0:T(8,128)S(1)}, f32[2,4,32,256]{3,2,1,0:T(8,128)S(1)}, u32[]{:S(2)}, u32[]{:S(2)}) %collective-permute-start.5) | collective-permute-done | bytes 262176 | tf_op jit(solution)/shard_map/ppermute | solution.py:514
  64.3 1.2 %copy-done.4 = f32[2,16,32,256]{3,2,1,0:T(8,128)S(1)} copy-done((f32[2,16,32,256]{3,2,1,0:T(8,128)S(1)}, f32[2,16,32,256]{3,2,1,0:T(8,128)}, u32[]{:S(2)}) %copy-start.4) | copy-done | bytes 1048600
  65.9 2.5 %collective-permute-start.6 = (f32[24,8,256]{2,1,0:T(8,128)S(1)}, f32[24,8,256]{2,1,0:T(8,128)S(1)}, u32[]{:S(2)}, u32[]{:S(2)}) collective-permute-start(f32[24,8,256]{2,1,0:T(8,128)S(1)} %get-tuple-element.24), channel_id=1, source_target_pairs={{0,1},{1,2},{2,3},{3,4},{4,5},{5,6},{6,7},{8,9},{9,10},{10,11},{11... | collective-permute-start | bytes 589832 | tf_op jit(solution)/shard_map/ppermute | solution.py:514
  68.4 1.3 %collective-permute-start.7 = (f32[24,8,256]{2,1,0:T(8,128)S(1)}, f32[24,8,256]{2,1,0:T(8,128)S(1)}, u32[]{:S(2)}, u32[]{:S(2)}) collective-permute-start(f32[24,8,256]{2,1,0:T(8,128)S(1)} %get-tuple-element.25), channel_id=1, source_target_pairs={{1,0},{2,1},{3,2},{4,3},{5,4},{6,5},{7,6},{9,8},{10,9},{11,10},{12... | collective-permute-start | bytes 589832 | tf_op jit(solution)/shard_map/ppermute | solution.py:514
  69.7 1.9 %collective-permute-done.6.yl_ref = f32[24,8,256]{2,1,0:T(8,128)S(1)} collective-permute-done((f32[24,8,256]{2,1,0:T(8,128)S(1)}, f32[24,8,256]{2,1,0:T(8,128)S(1)}, u32[]{:S(2)}, u32[]{:S(2)}) %collective-permute-start.6) | collective-permute-done | bytes 196640 | tf_op jit(solution)/shard_map/ppermute | solution.py:514
  71.6 4.4 %collective-permute-done.7.yr_ref = f32[24,8,256]{2,1,0:T(8,128)S(1)} collective-permute-done((f32[24,8,256]{2,1,0:T(8,128)S(1)}, f32[24,8,256]{2,1,0:T(8,128)S(1)}, u32[]{:S(2)}, u32[]{:S(2)}) %collective-permute-start.7) | collective-permute-done | bytes 196640 | tf_op jit(solution)/shard_map/ppermute | solution.py:514
  76.0 16.7 %shard_map.72 = (f32[2,16,32,256]{3,2,1,0:T(8,128)S(1)}, f32[2,16,32,256]{3,2,1,0:T(8,128)S(1)}, f32[2,16,32,256]{3,2,1,0:T(8,128)S(1)}, f32[2,16,32,256]{3,2,1,0:T(8,128)S(1)}, f32[32,1,128]{2,1,0:T(1,128)S(1)}) custom-call(f32[32,1,128]{2,1,0:T(1,128)S(1)} %all_to_all.10.th_ref, f32[2,4,32,256]{3,2,1,0:T(8,128)S(1)} %collective-permute-done.4.xl_ref, ...), custom_call_target="tpu_custom_call" | custom-call | tf_op jit(solution)/shard_map/pallas_call | solution.py:500
  92.7 1.0 copy-done.8
  93.7 1.0 copy-done.9
  94.7 1.0 copy-done.10
  95.6 14.5 %all_to_all.11.g_ref = f32[32,1,128]{2,1,0:T(1,128)S(1)} all-to-all(f32[32,1,128]{2,1,0:T(1,128)S(1)} %get-tuple-element.29), channel_id=1, replica_groups=mesh['gx'=4,'gy'=8] {'gx','gy'}, dimensions={0} | all-to-all | bytes 32768 | tf_op jit(solution)/shard_map/all_to_all | solution.py:550
  110.2 5.5 %shard_map.73 = (f32[2,16,32,256]{3,2,1,0:T(8,128)}, f32[2,16,32,256]{3,2,1,0:T(8,128)}) custom-call(f32[32,1,128]{2,1,0:T(1,128)S(1)} %all_to_all.10.th_ref, f32[32,1,128]{2,1,0:T(1,128)S(1)} %all_to_all.11.g_ref, f32[2,16,32,256]{3,2,1,0:T(8,128)S(1)} %copy-done.1, f32[16,32,256]{2,1,0:T(8,128)S(1)} %copy-done.3, f32[16,32,256]{2,1,0:T(8,128)S(1)} %copy-done.2, ...), custom_call_target="tpu_custom_call" | custom-call | tf_op jit(solution)/shard_map/pallas_call | solution.py:500
  (27 shorter events, 1.1 us)
Async XLA Ops:
  0.6 2.4 %copy-start = (f32[2,16,32,256]{3,2,1,0:T(8,128)S(1)}, f32[2,16,32,256]{3,2,1,0:T(8,128)}, u32[]{:S(2)}) copy-start(f32[2,16,32,256]{3,2,1,0:T(8,128)} %b_ref.9) | copy-start | bytes 3145732
  3.0 8.9 %copy-start.2 = (f32[16,32,256]{2,1,0:T(8,128)S(1)}, f32[16,32,256]{2,1,0:T(8,128)}, u32[]{:S(2)}) copy-start(f32[16,32,256]{2,1,0:T(8,128)} %ct_ref.9) | copy-start | bytes 1572868
  3.0 8.9 %copy-start.3 = (f32[16,32,256]{2,1,0:T(8,128)S(1)}, f32[16,32,256]{2,1,0:T(8,128)}, u32[]{:S(2)}) copy-start(f32[16,32,256]{2,1,0:T(8,128)} %cf_ref.7) | copy-start | bytes 1572868
  3.1 8.9 %copy-start.5 = (f32[16,32,256]{2,1,0:T(8,128)S(1)}, f32[16,32,256]{2,1,0:T(8,128)}, u32[]{:S(2)}) copy-start(f32[16,32,256]{2,1,0:T(8,128)} %mr_ref.5) | copy-start | bytes 1572868
  3.1 8.8 %copy-start.6 = (f32[16,32,256]{2,1,0:T(8,128)S(1)}, f32[16,32,256]{2,1,0:T(8,128)}, u32[]{:S(2)}) copy-start(f32[16,32,256]{2,1,0:T(8,128)} %d_ref.5) | copy-start | bytes 1572868
  3.2 4.2 %collective-permute-start = (f32[5,4,32,256]{3,2,1,0:T(8,128)S(1)}, f32[5,4,32,256]{3,2,1,0:T(8,128)S(1)}, u32[]{:S(2)}, u32[]{:S(2)}) collective-permute-start(f32[5,4,32,256]{3,2,1,0:T(8,128)S(1)} %pad_maximum_fusion), channel_id=1, source_target_pairs={{0,8},{8,16},{16,24},{1,9},{9,17},{17,25},{2,10},{10,18},{18,26},{... | collective-permute-start | bytes 1966088 | tf_op jit(solution)/shard_map/ppermute | solution.py:514
  5.8 6.1 %collective-permute-start.1 = (f32[5,4,32,256]{3,2,1,0:T(8,128)S(1)}, f32[5,4,32,256]{3,2,1,0:T(8,128)S(1)}, u32[]{:S(2)}, u32[]{:S(2)}) collective-permute-start(f32[5,4,32,256]{3,2,1,0:T(8,128)S(1)} %pad_maximum_fusion.1), channel_id=1, source_target_pairs={{8,0},{16,8},{24,16},{9,1},{17,9},{25,17},{10,2},{18,10},{26,18},{... | collective-permute-start | bytes 1966088 | tf_op jit(solution)/shard_map/ppermute | solution.py:514
  12.2 30.4 %collective-permute-start.2 = (f32[60,8,256]{2,1,0:T(8,128)S(1)}, f32[60,8,256]{2,1,0:T(8,128)S(1)}, u32[]{:S(2)}, u32[]{:S(2)}) collective-permute-start(f32[60,8,256]{2,1,0:T(8,128)S(1)} %get-tuple-element.19), channel_id=1, source_target_pairs={{0,1},{1,2},{2,3},{3,4},{4,5},{5,6},{6,7},{8,9},{9,10},{10,11},{11... | collective-permute-start | bytes 1474568 | tf_op jit(solution)/shard_map/ppermute | solution.py:514
  15.7 27.0 %collective-permute-start.3 = (f32[60,8,256]{2,1,0:T(8,128)S(1)}, f32[60,8,256]{2,1,0:T(8,128)S(1)}, u32[]{:S(2)}, u32[]{:S(2)}) collective-permute-start(f32[60,8,256]{2,1,0:T(8,128)S(1)} %get-tuple-element.20), channel_id=1, source_target_pairs={{1,0},{2,1},{3,2},{4,3},{5,4},{6,5},{7,6},{9,8},{10,9},{11,10},{12... | collective-permute-start | bytes 1474568 | tf_op jit(solution)/shard_map/ppermute | solution.py:514
  58.8 3.1 %collective-permute-start.4 = (f32[2,4,32,256]{3,2,1,0:T(8,128)S(1)}, f32[2,4,32,256]{3,2,1,0:T(8,128)S(1)}, u32[]{:S(2)}, u32[]{:S(2)}) collective-permute-start(f32[2,4,32,256]{3,2,1,0:T(8,128)S(1)} %get-tuple-element.21), channel_id=1, source_target_pairs={{0,8},{8,16},{16,24},{1,9},{9,17},{17,25},{2,10},{10,18},{18,26},{... | collective-permute-start | bytes 786440 | tf_op jit(solution)/shard_map/ppermute | solution.py:514
  60.5 3.8 %collective-permute-start.5 = (f32[2,4,32,256]{3,2,1,0:T(8,128)S(1)}, f32[2,4,32,256]{3,2,1,0:T(8,128)S(1)}, u32[]{:S(2)}, u32[]{:S(2)}) collective-permute-start(f32[2,4,32,256]{3,2,1,0:T(8,128)S(1)} %get-tuple-element.22), channel_id=1, source_target_pairs={{8,0},{16,8},{24,16},{9,1},{17,9},{25,17},{10,2},{18,10},{26,18},{... | collective-permute-start | bytes 786440 | tf_op jit(solution)/shard_map/ppermute | solution.py:514
  64.3 1.2 %copy-start.4 = (f32[2,16,32,256]{3,2,1,0:T(8,128)S(1)}, f32[2,16,32,256]{3,2,1,0:T(8,128)}, u32[]{:S(2)}) copy-start(f32[2,16,32,256]{3,2,1,0:T(8,128)} %get-tuple-element.23.v_ref.v2_ref) | copy-start | bytes 3145732
  65.9 5.7 %collective-permute-start.6 = (f32[24,8,256]{2,1,0:T(8,128)S(1)}, f32[24,8,256]{2,1,0:T(8,128)S(1)}, u32[]{:S(2)}, u32[]{:S(2)}) collective-permute-start(f32[24,8,256]{2,1,0:T(8,128)S(1)} %get-tuple-element.24), channel_id=1, source_target_pairs={{0,1},{1,2},{2,3},{3,4},{4,5},{5,6},{6,7},{8,9},{9,10},{10,11},{11... | collective-permute-start | bytes 589832 | tf_op jit(solution)/shard_map/ppermute | solution.py:514
  68.4 7.6 %collective-permute-start.7 = (f32[24,8,256]{2,1,0:T(8,128)S(1)}, f32[24,8,256]{2,1,0:T(8,128)S(1)}, u32[]{:S(2)}, u32[]{:S(2)}) collective-permute-start(f32[24,8,256]{2,1,0:T(8,128)S(1)} %get-tuple-element.25), channel_id=1, source_target_pairs={{1,0},{2,1},{3,2},{4,3},{5,4},{6,5},{7,6},{9,8},{10,9},{11,10},{12... | collective-permute-start | bytes 589832 | tf_op jit(solution)/shard_map/ppermute | solution.py:514
  76.0 34.2 %copy-start.1 = (f32[2,16,32,256]{3,2,1,0:T(8,128)S(1)}, f32[2,16,32,256]{3,2,1,0:T(8,128)}, u32[]{:S(2)}) copy-start(f32[2,16,32,256]{3,2,1,0:T(8,128)} %b_ref.9) | copy-start | bytes 3145732
  76.0 34.2 %copy-start.7 = (f32[2,16,32,256]{3,2,1,0:T(8,128)S(1)}, f32[2,16,32,256]{3,2,1,0:T(8,128)}, u32[]{:S(2)}) copy-start(f32[2,16,32,256]{3,2,1,0:T(8,128)} %get-tuple-element.31.w1_ref) | copy-start | bytes 3145732
  92.7 1.0 copy-start.8
  93.7 1.0 copy-start.9
  94.6 1.0 copy-start.10

commit v2 on v0

v2 whole, which is shorter than its diff:
```python
import jax
import jax.numpy as jnp
from jax import lax
from jax.experimental import pallas as pl
from jax.experimental.pallas import tpu as pltpu
from jax.sharding import PartitionSpec as P

OMEGA = 0.8
EPSILON = 1e-06
H = 4
AXES = ("gx", "gy")
F32 = jnp.float32
LIMIT = 24 * 1024 * 1024
SHIFTS = ((0.72, -0.28), (0.55, -0.2))


def vmem(n):
    return [pl.BlockSpec(memory_space=pltpu.VMEM)] * n


def cmul(a, b):
    return (a[0] * b[0] - a[1] * b[1], a[0] * b[1] + a[1] * b[0])


def cconj(a):
    return (a[0], -a[1])


def cadd(a, b):
    return (a[0] + b[0], a[1] + b[1])


def csub(a, b):
    return (a[0] - b[0], a[1] - b[1])


def cdiv(n, d):
    scale = d[0] * d[0] + d[1] * d[1]
    return (
        (n[0] * d[0] + n[1] * d[1]) / scale,
        (n[1] * d[0] - n[0] * d[1]) / scale,
    )


def smooth_yz(plane):
    rows, lanes = plane.shape
    y = plane + plane + pltpu.roll(plane, 1, 0) + pltpu.roll(plane, rows - 1, 0)
    lane = lax.broadcasted_iota(jnp.int32, plane.shape, 1)
    up = jnp.where(lane == 0, 0.0, pltpu.roll(y, 1, 1))
    down = jnp.where(lane == lanes - 1, 0.0, pltpu.roll(y, lanes - 1, 1))
    return y + y + up + down


def weighted(ref, i):
    out = []
    for part in range(2):
        mid = ref[part, i]
        total = smooth_yz(ref[part, i - 1] + mid + mid + ref[part, i + 1])
        out.append((total - 8.0 * mid) * (1.0 / 160.0))
    return tuple(out)


def coefficients(c, mr, d):
    shift = d + 0.5 * mr
    mod = mr * mr + shift * shift
    den = mod * c
    inv = 1.0 / jnp.where(den == 0.0, 1.0, den)
    k = OMEGA * c * c * inv
    rc = mod * inv
    return (k * mr, -(k * shift)), (rc * mr, rc * d)


def half_step(u_ref, p_ref, w_ref, lo, hi):
    def body(i, carry):
        pw = cmul((p_ref[0, i], p_ref[1, i]), weighted(u_ref, i))
        w_ref[0, i] = 1.2 * u_ref[0, i] + pw[0]
        w_ref[1, i] = 1.2 * u_ref[1, i] + pw[1]
        return carry

    lax.fori_loop(lo, hi, body, 0, unroll=2)


def image(w_ref, n_ref, v_ref, th, i, at):
    w = (w_ref[0, i], w_ref[1, i])
    nw = cmul((n_ref[0, i], n_ref[1, i]), w)
    rows = v_ref.shape[2]
    v = cmul(th, (v_ref[0, at], v_ref[1, at]))
    y = csub(nw, weighted(w_ref, i))
    return csub((y[0][:rows], y[1][:rows]), v)


def apply_wide(w_ref, n_ref, v_ref, p_ref, th, next_ref, u_ref, lo, hi):
    def body(i, carry):
        y = image(w_ref, n_ref, v_ref, th, i, i)
        u = cmul((p_ref[0, i], p_ref[1, i]), y)
        for part in range(2):
            next_ref[part, i] = y[part]
            u_ref[part, i] = u[part]
        return carry

    lax.fori_loop(lo, hi, body, 0, unroll=2)


def apply_own(w_ref, n_ref, v_ref, th, next_ref):
    nx, ny = next_ref.shape[1:3]

    def body(i, carry):
        y = image(w_ref, n_ref, v_ref, th, i + H, i + H)
        for part in range(2):
            next_ref[part, i] = y[part][:ny]
        return carry

    lax.fori_loop(0, nx, body, 0, unroll=2)


def total_of(ref):
    rows = ref[...].reshape(ref.shape[0], ref.shape[-1])
    tot = jnp.sum(rows, axis=0, keepdims=True)
    lane = lax.broadcasted_iota(jnp.int32, tot.shape, 1)
    return lambda k: jnp.sum(jnp.where(lane == k, tot, 0.0), axis=1, keepdims=True)


def pack_lanes(values):
    lane = lax.broadcasted_iota(jnp.int32, (1, 128), 1)
    row = jnp.zeros((1, 128), F32)
    for k, v in enumerate(values):
        s = jnp.sum(jnp.sum(v, axis=0, keepdims=True), axis=1, keepdims=True)
        row = jnp.where(lane == k, s, row)
    return row


def fold(x):
    out = x[:, :128]
    for b in range(128, x.shape[1], 128):
        out = out + x[:, b : b + 128]
    return out


def pairs_of(rights):
    return [(left, right) for right in rights for left in range(right + 1)]


def gram_rows(fields, ct_ref, pairs, out_ref):
    nx, ny, _ = ct_ref.shape
    used = sorted({k for pair in pairs for k in pair})
    count = sum(1 if left == right else 2 for left, right in pairs)

    def body(i, acc):
        acc = list(acc)
        for a in range(0, ny, 8):
            rows = pl.ds(a, 8)
            ct = ct_ref[i, rows]
            vs = {}
            for k in used:
                ref, base, scaled = fields[k]
                v = (ref[0, i + base, rows], ref[1, i + base, rows])
                vs[k] = (ct * v[0], ct * v[1]) if scaled else v
            k = 0
            for left, right in pairs:
                (lr, li), (rr, ri) = vs[left], vs[right]
                acc[k] = acc[k] + fold(lr * rr + li * ri)
                k += 1
                if right > left:
                    acc[k] = acc[k] + fold(lr * ri - li * rr)
                    k += 1
        return tuple(acc)

    acc = lax.fori_loop(0, nx, body, (jnp.zeros((8, 128), F32),) * count)
    row = pack_lanes(acc)
    for k in range(out_ref.shape[0]):
        out_ref[k] = row


def gram_entries(ref, pairs, entries):
    pick = total_of(ref)
    k = 0
    for left, right in pairs:
        if left == right:
            entries[left, right] = (pick(k), jnp.zeros((1, 1), F32))
            k += 1
        else:
            entries[left, right] = (pick(k), pick(k + 1))
            entries[right, left] = cconj(entries[left, right])
            k += 2
    return entries


def later_shift(entries):
    den = entries[0, 0][0]
    safe = jnp.where(den > 0.0, den, 1.0)
    num = entries[0, 1]
    return (SHIFTS[0][0] + num[0] / safe, SHIFTS[0][1] + num[1] / safe)


EARLY = pairs_of((0, 1, 2))
LATE = pairs_of((3, 4))


def pack_pair(first, second, top):
    sub = lax.broadcasted_iota(jnp.int32, first.shape, 0)
    rolled = pltpu.roll(second, 4, 0)
    if top:
        return jnp.where(sub < 4, first, rolled)
    return jnp.where(sub < 4, rolled, first)


def unpack_pair(right, left):
    sub = lax.broadcasted_iota(jnp.int32, right.shape, 0)
    first = jnp.where(sub < 4, right, left)
    second = pltpu.roll(jnp.where(sub < 4, left, right), 4, 0)
    return first, second


def own_values(b_ref, cf_ref, ct_ref, mr_ref, d_ref):
    def get(i, rows):
        ct = ct_ref[i, rows]
        r = 1.0 / ct
        return (
            b_ref[0, i, rows] * r,
            b_ref[1, i, rows] * r,
            cf_ref[i, rows] * ct,
            mr_ref[i, rows],
            d_ref[i, rows],
        )

    return get


def edges_kernel(b_ref, cf_ref, ct_ref, mr_ref, d_ref, lo_ref, hi_ref, top_ref, bot_ref):
    nx, ny, _ = cf_ref.shape
    get = own_values(b_ref, cf_ref, ct_ref, mr_ref, d_ref)
    for out_ref, base in ((lo_ref, 0), (hi_ref, nx - H)):
        for i in range(H):
            for f, value in enumerate(get(base + i, pl.ds(0, ny))):
                out_ref[f, i] = value
    for out_ref, rows, top in ((top_ref, pl.ds(0, 8), True), (bot_ref, pl.ds(ny - 8, 8), False)):

        def body(j, carry):
            a, b = get(2 * j, rows), get(2 * j + 1, rows)
            out_ref[2 * j] = pack_pair(a[0], a[1], top)
            out_ref[2 * j + 1] = pack_pair(b[0], b[1], top)
            for f in range(3):
                out_ref[nx + f * nx // 2 + j] = pack_pair(a[2 + f], b[2 + f], top)
            return carry

        lax.fori_loop(0, nx // 2, body, 0, unroll=2)


def corners_kernel(yl_ref, yr_ref, lo_ref, hi_ref):
    count = yl_ref.shape[0]
    nx = count * 2 // 5
    for k, ref in enumerate((yl_ref, yr_ref)):
        for out_ref, base in ((lo_ref, 0), (hi_ref, nx - H)):
            for i in range(H):
                out_ref[k, i] = ref[base + i]
            for f in range(3):
                for j in range(H // 2):
                    at = nx + f * nx // 2 + base // 2 + j
                    out_ref[k, H + f * H // 2 + j] = ref[at]


def store_fields(refs, plane, rows, v, c, mr, d):
    p_ref, n_ref, u_ref, v_ref = refs
    p, n = coefficients(c, mr, d)
    u = cmul(p, v)
    for part in range(2):
        p_ref[part, plane, rows] = p[part]
        n_ref[part, plane, rows] = n[part]
        u_ref[part, plane, rows] = u[part]
        v_ref[part, plane, rows] = v[part]


def own_kernel(b_ref, cf_ref, ct_ref, mr_ref, d_ref, p_ref, n_ref, u_ref, v_ref):
    nx, ny, _ = cf_ref.shape
    get = own_values(b_ref, cf_ref, ct_ref, mr_ref, d_ref)
    rows = pl.ds(0, ny)

    def body(i, carry):
        vr, vi, c, mr, d = get(i, rows)
        store_fields((p_ref, n_ref, u_ref, v_ref), i + H, rows, (vr, vi), c, mr, d)
        return carry

    lax.fori_loop(0, nx, body, 0, unroll=2)


def tails(refs, left, right, ny, fields, coefs, planes):
    rows = pl.ds(ny, 8)
    v = [unpack_pair(right(k), left(k)) for k in fields]
    c = [unpack_pair(right(k), left(k)) for k in coefs]
    for k in range(2):
        store_fields(refs, planes[k], rows, v[k], c[0][k], c[1][k], c[2][k])


def sides_kernel(xl_ref, xr_ref, yl_ref, yr_ref, *refs):
    refs = refs[4:]
    ny = xl_ref.shape[2]
    nx = refs[0].shape[1] - 2 * H
    rows = pl.ds(0, ny)
    for ref, base in ((xl_ref, 0), (xr_ref, nx + H)):

        def body(i, carry):
            vr, vi, c, mr, d = (ref[f, i] for f in range(5))
            store_fields(refs, base + i, rows, (vr, vi), c, mr, d)
            return carry

        lax.fori_loop(0, H, body, 0, unroll=2)

    def body(j, carry):
        coefs = [nx + f * nx // 2 + j for f in range(3)]
        at = (H + 2 * j, H + 2 * j + 1)
        tails(
            refs, lambda k: yl_ref[k], lambda k: yr_ref[k], ny, (2 * j, 2 * j + 1), coefs, at
        )
        return carry

    lax.fori_loop(0, nx // 2, body, 0, unroll=2)


def first_kernel(cl_ref, cr_ref, *refs):
    (p_ref, n_ref, u_ref, v_ref), rest = refs[4:8], refs[8:]
    w0_ref, w1_ref, v1_ref, v2_ref, sl_ref, sr_ref = rest
    nx, ny = v2_ref.shape[1:3]
    planes = nx + 2 * H
    for ref, base in ((cl_ref, 0), (cr_ref, nx + H)):
        for j in range(H // 2):
            coefs = [H + f * H // 2 + j for f in range(3)]
            at = (base + 2 * j, base + 2 * j + 1)
            tails(
                (p_ref, n_ref, u_ref, v_ref), lambda k: ref[0, k], lambda k: ref[1, k],
                ny, (2 * j, 2 * j + 1), coefs, at,
            )
    half_step(u_ref, p_ref, w0_ref, 1, planes - 1)
    apply_wide(w0_ref, n_ref, v_ref, p_ref, SHIFTS[0], v1_ref, u_ref, 2, planes - 2)
    half_step(u_ref, p_ref, w1_ref, 3, planes - 3)
    apply_own(w1_ref, n_ref, v1_ref, SHIFTS[1], v2_ref)
    for part in range(2):
        for i in range(H):
            sl_ref[part, i] = v2_ref[part, i]
            sr_ref[part, i] = v2_ref[part, nx - H + i]


def pack_kernel(xl_ref, xr_ref, v_ref, top_ref, bot_ref):
    nx, ny = v_ref.shape[1:3]
    for out_ref, rows, top in ((top_ref, pl.ds(0, 8), True), (bot_ref, pl.ds(ny - 8, 8), False)):
        for ref, count, base in ((xl_ref, H, 0), (v_ref, nx, H), (xr_ref, H, H + nx)):

            def body(i, carry):
                out_ref[base + i] = pack_pair(ref[0, i, rows], ref[1, i, rows], top)
                return carry

            lax.fori_loop(0, count, body, 0, unroll=2)


def early_kernel(b_ref, ct_ref, v1_ref, v2_ref, out_ref):
    fields = ((b_ref, 0, False), (v1_ref, H, True), (v2_ref, 0, True))
    gram_rows(fields, ct_ref, EARLY, out_ref)


def second_kernel(
    e_ref, xl_ref, xr_ref, yl_ref, yr_ref, p_ref, n_ref, b_ref, ct_ref, v1_ref, v2_ref,
    w2_ref, w3_ref, v3_ref, v4_ref, out_ref,
    u_ref, v_ref,
):
    nx, ny, _ = ct_ref.shape
    planes = nx + 2 * H
    th = later_shift(gram_entries(e_ref, EARLY[:2], {}))

    for ref, count, base in ((xl_ref, H, 0), (v2_ref, nx, H), (xr_ref, H, H + nx)):

        def fill(i, carry):
            at = base + i
            tail = unpack_pair(yr_ref[at], yl_ref[at])
            v = tuple(jnp.concatenate([ref[part, i], tail[part]], axis=0) for part in range(2))
            u = cmul((p_ref[0, at], p_ref[1, at]), v)
            for part in range(2):
                v_ref[part, at] = v[part]
                u_ref[part, at] = u[part]
            return carry

        lax.fori_loop(0, count, fill, 0, unroll=2)

    half_step(u_ref, p_ref, w2_ref, 1, planes - 1)
    apply_wide(w2_ref, n_ref, v_ref, p_ref, th, v3_ref, u_ref, 2, planes - 2)
    half_step(u_ref, p_ref, w3_ref, 3, planes - 3)
    apply_own(w3_ref, n_ref, v3_ref, th, v4_ref)
    fields = (
        (b_ref, 0, False), (v1_ref, H, True), (v2_ref, 0, True), (v3_ref, H, True),
        (v4_ref, 0, True),
    )
    gram_rows(fields, ct_ref, LATE, out_ref)


def recurrences(shifts, gram):
    def inner(x, y):
        total = None
        for i, xi in enumerate(x):
            part = None
            for j, yj in enumerate(y):
                t = cmul(gram[i, j], yj)
                part = t if part is None else cadd(part, t)
            t = cmul(cconj(xi), part)
            total = t if total is None else cadd(total, t)
        return total

    def apply(x):
        scaled = [cmul(th, c) for th, c in zip(shifts, x)]
        return [scaled[0]] + [cadd(x[k], scaled[k + 1]) for k in range(len(x) - 1)] + [x[-1]]

    def lincomb(x, s, y):
        out = []
        for k in range(max(len(x), len(y))):
            a = x[k] if k < len(x) else None
            b = cmul(s, y[k]) if k < len(y) else None
            out.append(b if a is None else a if b is None else cadd(a, b))
        return out

    def neg(s):
        return (-s[0], -s[1])

    one = (jnp.ones((1, 1), F32), jnp.zeros((1, 1), F32))
    residual, direction, shadow, answer = [one], [one], [one], []
    rho = inner(shadow, residual)
    for step in range(2):
        image = apply(direction)
        alpha = cdiv(rho, inner(shadow, image))
        half = lincomb(residual, neg(alpha), image)
        second = apply(half)
        prod = inner(second, half)
        norm = inner(second, second)[0] + EPSILON
        omega = (prod[0] / norm, prod[1] / norm)
        answer = lincomb(lincomb(answer, alpha, direction), omega, half)
        residual = lincomb(half, neg(omega), second)
        if step == 0:
            rho_next = inner(shadow, residual)
            beta = cmul(cdiv(rho_next, rho), cdiv(alpha, omega))
            direction = lincomb(residual, beta, lincomb(direction, neg(omega), image))
            rho = rho_next
    return answer, residual


def final_kernel(
    e_ref, g_ref, b_ref, cf_ref, ct_ref,
    w0_ref, w1_ref, w2_ref, w3_ref, v1_ref, v2_ref, v3_ref, v4_ref,
    sol_ref, res_ref,
):
    nx, ny, nz = cf_ref.shape
    entries = gram_entries(g_ref, LATE, gram_entries(e_ref, EARLY, {}))
    th = later_shift(entries)
    answer, residual = recurrences(SHIFTS + (th, th), entries)

    def spread(c):
        return tuple(jnp.broadcast_to(x, (8, nz)) for x in c)

    answer, residual = [spread(c) for c in answer], [spread(c) for c in residual]

    def body(i, carry):
        for a in range(0, ny, 8):
            rows = pl.ds(a, 8)
            acc = None
            for c, ref in zip(answer, (w0_ref, w1_ref, w2_ref, w3_ref)):
                t = cmul(c, (ref[0, i + H, rows], ref[1, i + H, rows]))
                acc = t if acc is None else cadd(acc, t)
            inv = 1.0 / cf_ref[i, rows]
            sol_ref[0, i, rows] = acc[0] * inv
            sol_ref[1, i, rows] = acc[1] * inv
            acc = None
            for c, ref, base in zip(residual[1:], (v1_ref, v2_ref, v3_ref, v4_ref), (H, 0, H, 0)):
                t = cmul(c, (ref[0, i + base, rows], ref[1, i + base, rows]))
                acc = t if acc is None else cadd(acc, t)
            ct = ct_ref[i, rows]
            t = cmul(residual[0], (b_ref[0, i, rows], b_ref[1, i, rows]))
            res_ref[0, i, rows] = acc[0] * ct + t[0]
            res_ref[1, i, rows] = acc[1] * ct + t[1]
        return carry

    lax.fori_loop(0, nx, body, 0)


def call(kernel, outs, scratch, *args, alias=None):
    return pl.pallas_call(
        kernel,
        out_shape=[jax.ShapeDtypeStruct(s, F32) for s in outs],
        in_specs=vmem(len(args)),
        out_specs=vmem(len(outs)),
        scratch_shapes=[pltpu.VMEM(s, F32) for s in scratch],
        input_output_aliases=alias or {},
        compiler_params=pltpu.CompilerParams(vmem_limit_bytes=LIMIT),
    )(*args)


def both_ways(to_lower, to_upper, axis):
    n = lax.axis_size(axis)
    up = [(i, i + 1) for i in range(n - 1)]
    down = [(i + 1, i) for i in range(n - 1)]
    return lax.ppermute(to_upper, axis, up), lax.ppermute(to_lower, axis, down)


def local(b, cf, ct, mr, d):
    nx, ny, nz = cf.shape
    peers = lax.axis_size("gx") * lax.axis_size("gy")
    planes = nx + 2 * H
    own = (2, nx, ny, nz)
    ext = (2, planes, ny + 2 * H, nz)
    face = (2, H, ny, nz)
    rim = (nx + 3 * nx // 2, 8, nz)
    corner = (2, H + 3 * H // 2, 8, nz)

    lo, hi, top, bot = call(
        edges_kernel, [(5, H, ny, nz), (5, H, ny, nz), rim, rim], [], b, cf, ct, mr, d
    )
    yl, yr = both_ways(top, bot, "gy")
    xl, xr = both_ways(lo, hi, "gx")
    state = call(own_kernel, [ext] * 4, [], b, cf, ct, mr, d)
    lo, hi = call(corners_kernel, [corner] * 2, [], yl, yr)
    cl, cr = both_ways(lo, hi, "gx")
    state = call(
        sides_kernel, [ext] * 4, [], xl, xr, yl, yr, *state, alias={4 + k: k for k in range(4)}
    )
    p, n, _, _, w0, w1, v1, v2, sl, sr = call(
        first_kernel, [ext] * 7 + [own, face, face], [], cl, cr, *state,
        alias={2 + k: k for k in range(4)},
    )
    xl, xr = both_ways(sl, sr, "gx")
    early = call(early_kernel, [(peers, 1, 128)], [], b, ct, v1, v2)[0]
    early = lax.all_to_all(early, AXES, 0, 0)
    top, bot = call(pack_kernel, [(planes, 8, nz)] * 2, [], xl, xr, v2)
    yl, yr = both_ways(top, bot, "gy")
    w2, w3, v3, v4, late = call(
        second_kernel, [ext, ext, ext, own, (peers, 1, 128)], [ext, ext],
        early, xl, xr, yl, yr, p, n, b, ct, v1, v2,
    )
    late = lax.all_to_all(late, AXES, 0, 0)
    return tuple(
        call(final_kernel, [own, own], [], early, late, b, cf, ct, w0, w1, w2, w3, v1, v2, v3, v4)
    )


def solution(mesh):
    field, coef = P(None, "gx", "gy", None), P("gx", "gy", None)
    return jax.shard_map(
        local,
        mesh=mesh,
        in_specs=(field, coef, coef, coef, coef),
        out_specs=(field, field),
        check_vma=False,
    )
```

time: 422 us -> 98.1 us (0.23)
  blocking collectives: 206 us -> 26.1 us
  other arithmetic: 46.7 us -> 0 us
  starting transfers between devices: 70.2 us -> 26.9 us
  waiting for transfers between devices: 55.9 us -> 16.8 us
  between operations: 28.4 us -> 0.83 us
  Pallas kernels: 0 us -> 21.6 us
  local copies, waits for them, and re-layouts: 12.4 us -> 5.39 us
    psum x5 -> x0, blocking collectives: 206 us -> none  [the longest x2 82.9 us: local(): pair = lax.psum((prod_local[0], prod_local[1], norm_local), ('gx', 'gy'))]
    ppermute x32 -> x10, starting transfers between devices: 70.2 us -> 26.9 us  [the longest x5 20.4 us: both_ways(): lax.ppermute(to_upper, axis, up)]
    ppermute x32 -> x10, waiting for transfers between devices: 55.9 us -> 16.8 us  [the longest x5 12.3 us: both_ways(): lax.ppermute(to_upper, axis, up)]
    all_to_all x0 -> x2, blocking collectives: none -> 26.1 us  [the longest x1 17.3 us: local(): early = lax.all_to_all(early, AXES, 0, 0)]
    sub x23 -> x0, other arithmetic: 23.9 us -> none  [the longest x10 13.2 us: complex_mul(): real_part * field[0] - imag_part * field[1]]
    pallas_call x0 -> x9, Pallas kernels: none -> 21.6 us  [call(): pl.pallas_call(kernel, out_shape=[jax.ShapeDtypeStruct(s, F32) for s in o...]
    unnamed x116 -> x16, local copies, waits for them, and re-layouts: 12.3 us -> 5.39 us
    another operation x17 -> x0, other arithmetic: 6.55 us -> none  [complex_mul(): jnp.stack([real_part * field[0] - imag_part * field[1], real_part * field...]
  transfers between devices with their start and end apart: 32 -> 10, of which waited for: 22 -> 3; matrix products, arithmetic and copies ran while one was open for 2% -> 0% of each run, Pallas kernels for 0% -> 2%
where the time goes in v2:
time: 98.1 us; the launch traced here: 97.5 us
  starting transfers between devices  26.9 us (27%)
  blocking collectives  26.1 us (27%)
  Pallas kernels  21.6 us (22%)
  waiting for transfers between devices  16.8 us (17%)
  local copies, waits for them, and re-layouts  5.39 us (5%)
    pallas_call x9, Pallas kernels, call(): pl.pallas_call(kernel, out_shape=[jax.ShapeDtypeStruct(s, F32) for s in o...  21.6 us
    ppermute x5, starting transfers between devices, both_ways(): lax.ppermute(to_upper, axis, up)  20.4 us
    all_to_all x1, blocking collectives, local(): early = lax.all_to_all(early, AXES, 0, 0)  17.3 us
    ppermute x5, waiting for transfers between devices, both_ways(): lax.ppermute(to_upper, axis, up)  12.3 us
    all_to_all x1, blocking collectives, local(): late = lax.all_to_all(late, AXES, 0, 0)  8.81 us
    ppermute x5, starting transfers between devices, both_ways(): lax.ppermute(to_lower, axis, down)  6.46 us
    unnamed x16, local copies, waits for them, and re-layouts  5.39 us
    ppermute x5, waiting for transfers between devices, both_ways(): lax.ppermute(to_lower, axis, down)  4.44 us
  transfers between devices with their start and end apart: 10, of which 3 were waited for; matrix products, arithmetic and copies ran while one was open for 0% of the time, Pallas kernels for 2%

profile of v2, /device:TPU:0, one launch (start us, length us, event | category | flops | bytes accessed | tf_op | source)
XLA Modules:
  0.0 97.5 jit_solution(7723112104057441947)
XLA Ops:
  0.6 1.2 %copy-done = f32[2,16,32,256]{3,2,1,0:T(8,128)S(1)} copy-done((f32[2,16,32,256]{3,2,1,0:T(8,128)S(1)}, f32[2,16,32,256]{3,2,1,0:T(8,128)}, u32[]{:S(2)}) %copy-start) | copy-done | bytes 1048600
  1.9 1.0 %copy-done.2 = f32[16,32,256]{2,1,0:T(8,128)S(1)} copy-done((f32[16,32,256]{2,1,0:T(8,128)S(1)}, f32[16,32,256]{2,1,0:T(8,128)}, u32[]{:S(2)}) %copy-start.2) | copy-done | bytes 524312
  2.9 1.0 %copy-done.4 = f32[16,32,256]{2,1,0:T(8,128)S(1)} copy-done((f32[16,32,256]{2,1,0:T(8,128)S(1)}, f32[16,32,256]{2,1,0:T(8,128)}, u32[]{:S(2)}) %copy-start.4) | copy-done | bytes 524312
  3.9 1.0 %copy-done.6 = f32[16,32,256]{2,1,0:T(8,128)S(1)} copy-done((f32[16,32,256]{2,1,0:T(8,128)S(1)}, f32[16,32,256]{2,1,0:T(8,128)}, u32[]{:S(2)}) %copy-start.6) | copy-done | bytes 524312
  5.0 1.0 %copy-done.7 = f32[16,32,256]{2,1,0:T(8,128)S(1)} copy-done((f32[16,32,256]{2,1,0:T(8,128)S(1)}, f32[16,32,256]{2,1,0:T(8,128)}, u32[]{:S(2)}) %copy-start.7) | copy-done | bytes 524312
  6.3 2.5 %collective-permute-start.4 = (f32[5,4,32,256]{3,2,1,0:T(8,128)S(1)}, f32[5,4,32,256]{3,2,1,0:T(8,128)S(1)}, u32[]{:S(2)}, u32[]{:S(2)}) collective-permute-start(f32[5,4,32,256]{3,2,1,0:T(8,128)S(1)} %get-tuple-element.35), channel_id=1, source_target_pairs={{0,8},{8,16},{16,24},{1,9},{9,17},{17,25},{2,10},{10,18},{18,26},{... | collective-permute-start | bytes 1966088 | tf_op jit(solution)/shard_map/ppermute | solution.py:495
  8.8 1.3 %collective-permute-start.5 = (f32[5,4,32,256]{3,2,1,0:T(8,128)S(1)}, f32[5,4,32,256]{3,2,1,0:T(8,128)S(1)}, u32[]{:S(2)}, u32[]{:S(2)}) collective-permute-start(f32[5,4,32,256]{3,2,1,0:T(8,128)S(1)} %get-tuple-element.36), channel_id=1, source_target_pairs={{8,0},{16,8},{24,16},{9,1},{17,9},{25,17},{10,2},{18,10},{26,18},{... | collective-permute-start | bytes 1966088 | tf_op jit(solution)/shard_map/ppermute | solution.py:495
  10.1 4.2 %collective-permute-start = (f32[40,8,256]{2,1,0:T(8,128)S(1)}, f32[40,8,256]{2,1,0:T(8,128)S(1)}, u32[]{:S(2)}, u32[]{:S(2)}) collective-permute-start(f32[40,8,256]{2,1,0:T(8,128)S(1)} %get-tuple-element.31), channel_id=1, source_target_pairs={{0,1},{1,2},{2,3},{3,4},{4,5},{5,6},{6,7},{8,9},{9,10},{10,11},{11... | collective-permute-start | bytes 983048 | tf_op jit(solution)/shard_map/ppermute | solution.py:495
  14.4 1.3 %collective-permute-start.1 = (f32[40,8,256]{2,1,0:T(8,128)S(1)}, f32[40,8,256]{2,1,0:T(8,128)S(1)}, u32[]{:S(2)}, u32[]{:S(2)}) collective-permute-start(f32[40,8,256]{2,1,0:T(8,128)S(1)} %get-tuple-element.32), channel_id=1, source_target_pairs={{1,0},{2,1},{3,2},{4,3},{5,4},{6,5},{7,6},{9,8},{10,9},{11,10},{12... | collective-permute-start | bytes 983048 | tf_op jit(solution)/shard_map/ppermute | solution.py:495
  15.7 12.3 %collective-permute-done.yl_ref = f32[40,8,256]{2,1,0:T(8,128)S(1)} collective-permute-done((f32[40,8,256]{2,1,0:T(8,128)S(1)}, f32[40,8,256]{2,1,0:T(8,128)S(1)}, u32[]{:S(2)}, u32[]{:S(2)}) %collective-permute-start) | collective-permute-done | bytes 327712 | tf_op jit(solution)/shard_map/ppermute | solution.py:495
  28.0 3.5 %collective-permute-start.2 = (f32[2,10,8,256]{3,2,1,0:T(8,128)S(1)}, f32[2,10,8,256]{3,2,1,0:T(8,128)S(1)}, u32[]{:S(2)}, u32[]{:S(2)}) collective-permute-start(f32[2,10,8,256]{3,2,1,0:T(8,128)S(1)} %get-tuple-element.33), channel_id=1, source_target_pairs={{0,8},{8,16},{16,24},{1,9},{9,17},{17,25},{2,10},{10,18},{18,26},{... | collective-permute-start | bytes 491528 | tf_op jit(solution)/shard_map/ppermute | solution.py:495
  31.5 1.3 %collective-permute-start.3 = (f32[2,10,8,256]{3,2,1,0:T(8,128)S(1)}, f32[2,10,8,256]{3,2,1,0:T(8,128)S(1)}, u32[]{:S(2)}, u32[]{:S(2)}) collective-permute-start(f32[2,10,8,256]{3,2,1,0:T(8,128)S(1)} %get-tuple-element.34), channel_id=1, source_target_pairs={{8,0},{16,8},{24,16},{9,1},{17,9},{25,17},{10,2},{18,10},{26,18},{... | collective-permute-start | bytes 491528 | tf_op jit(solution)/shard_map/ppermute | solution.py:495
  33.8 2.3 %collective-permute-done.3.cr_ref = f32[2,10,8,256]{3,2,1,0:T(8,128)S(1)} collective-permute-done((f32[2,10,8,256]{3,2,1,0:T(8,128)S(1)}, f32[2,10,8,256]{3,2,1,0:T(8,128)S(1)}, u32[]{:S(2)}, u32[]{:S(2)}) %collective-permute-start.3) | collective-permute-done | bytes 163872 | tf_op jit(solution)/shard_map/ppermute | solution.py:495
  36.2 7.3 %shard_map.72 = (f32[2,24,40,256]{3,2,1,0:T(8,128)S(1)}, f32[2,24,40,256]{3,2,1,0:T(8,128)S(1)}, f32[2,24,40,256]{3,2,1,0:T(8,128)S(1)}, f32[2,24,40,256]{3,2,1,...) custom-call(f32[2,10,8,256]{3,2,1,0:T(8,128)S(1)} %collective-permut, ...), custom_call_target="tpu_custom_call", output_to_operand_aliasing={{0}: (2, {}), {1}: (3, {}), {2}: (4, {}), {3}: (5, {})} | custom-call | tf_op jit(solution)/shard_map/pallas_call | solution.py:480
  43.5 5.8 %collective-permute-start.6 = (f32[2,4,32,256]{3,2,1,0:T(8,128)S(1)}, f32[2,4,32,256]{3,2,1,0:T(8,128)S(1)}, u32[]{:S(2)}, u32[]{:S(2)}) collective-permute-start(f32[2,4,32,256]{3,2,1,0:T(8,128)S(1)} %get-tuple-element.47), channel_id=1, source_target_pairs={{0,8},{8,16},{16,24},{1,9},{9,17},{17,25},{2,10},{10,18},{18,26},{... | collective-permute-start | bytes 786440 | tf_op jit(solution)/shard_map/ppermute | solution.py:495
  49.2 1.3 %collective-permute-start.7 = (f32[2,4,32,256]{3,2,1,0:T(8,128)S(1)}, f32[2,4,32,256]{3,2,1,0:T(8,128)S(1)}, u32[]{:S(2)}, u32[]{:S(2)}) collective-permute-start(f32[2,4,32,256]{3,2,1,0:T(8,128)S(1)} %get-tuple-element.48), channel_id=1, source_target_pairs={{8,0},{16,8},{24,16},{9,1},{17,9},{25,17},{10,2},{18,10},{26,18},{... | collective-permute-start | bytes 786440 | tf_op jit(solution)/shard_map/ppermute | solution.py:495
  50.6 2.1 %collective-permute-done.7.xr_ref = f32[2,4,32,256]{3,2,1,0:T(8,128)S(1)} collective-permute-done((f32[2,4,32,256]{3,2,1,0:T(8,128)S(1)}, f32[2,4,32,256]{3,2,1,0:T(8,128)S(1)}, u32[]{:S(2)}, u32[]{:S(2)}) %collective-permute-start.7) | collective-permute-done | bytes 262176 | tf_op jit(solution)/shard_map/ppermute | solution.py:495
  52.8 4.4 %collective-permute-start.8 = (f32[24,8,256]{2,1,0:T(8,128)S(1)}, f32[24,8,256]{2,1,0:T(8,128)S(1)}, u32[]{:S(2)}, u32[]{:S(2)}) collective-permute-start(f32[24,8,256]{2,1,0:T(8,128)S(1)} %get-tuple-element.49), channel_id=1, source_target_pairs={{0,1},{1,2},{2,3},{3,4},{4,5},{5,6},{6,7},{8,9},{9,10},{10,11},{11... | collective-permute-start | bytes 589832 | tf_op jit(solution)/shard_map/ppermute | solution.py:495
  57.2 1.3 %collective-permute-start.9 = (f32[24,8,256]{2,1,0:T(8,128)S(1)}, f32[24,8,256]{2,1,0:T(8,128)S(1)}, u32[]{:S(2)}, u32[]{:S(2)}) collective-permute-start(f32[24,8,256]{2,1,0:T(8,128)S(1)} %get-tuple-element.50), channel_id=1, source_target_pairs={{1,0},{2,1},{3,2},{4,3},{5,4},{6,5},{7,6},{9,8},{10,9},{11,10},{12... | collective-permute-start | bytes 589832 | tf_op jit(solution)/shard_map/ppermute | solution.py:495
  58.5 0.9 shard_map.73
  59.4 17.3 %all_to_all.10.e_ref = f32[32,1,128]{2,1,0:T(1,128)S(1)} all-to-all(f32[32,1,128]{2,1,0:T(1,128)S(1)} %shard_map.73), channel_id=1, replica_groups=mesh['gx'=4,'gy'=8] {'gx','gy'}, dimensions={0} | all-to-all | bytes 32768 | tf_op jit(solution)/shard_map/all_to_all | solution.py:525
  76.7 9.1 %shard_map.75 = (f32[2,24,40,256]{3,2,1,0:T(8,128)S(1)}, f32[2,24,40,256]{3,2,1,0:T(8,128)S(1)}, f32[2,24,40,256]{3,2,1,0:T(8,128)S(1)}, f32[2,16,32,256]{3,2,1,0:T(8,128)S(1)}, f32[32,1,128]{2,1,0:T(1,128)S(1)}) custom-call(f32[32,1,128]{2,1,0:T(1,128)S(1)} %all_to_all.10.e_ref, f32[2,4,32,256]{3,2,1,0:T(8,128)S(1)} %collective-permute-done.6.xl_ref, ...), custom_call_target="tpu_custom_call" | custom-call | tf_op jit(solution)/shard_map/pallas_call | solution.py:480
  85.8 8.8 %all_to_all.11.g_ref = f32[32,1,128]{2,1,0:T(1,128)S(1)} all-to-all(f32[32,1,128]{2,1,0:T(1,128)S(1)} %get-tuple-element.53), channel_id=1, replica_groups=mesh['gx'=4,'gy'=8] {'gx','gy'}, dimensions={0} | all-to-all | bytes 32768 | tf_op jit(solution)/shard_map/all_to_all | solution.py:532
  94.6 2.9 %shard_map.76 = (f32[2,16,32,256]{3,2,1,0:T(8,128)}, f32[2,16,32,256]{3,2,1,0:T(8,128)}) custom-call(f32[32,1,128]{2,1,0:T(1,128)S(1)} %all_to_all.10.e_ref, f32[32,1,128]{2,1,0:T(1,128)S(1)} %all_to_all.11.g_ref, f32[2,16,32,256]{3,2,1,0:T(8,128)S(1)} %copy-done.1, f32[16,32,256]{2,1,0:T(8,128)S(1)} %copy-done.5, f32[16,32,256]{2,1,0:T(8,128)S(1)} %copy-done.3, ...), custom_call_target="tpu_custom_call" | custom-call | tf_op jit(solution)/shard_map/pallas_call | solution.py:480
  (23 shorter events, 1.4 us)
Async XLA Ops:
  0.6 1.2 %copy-start = (f32[2,16,32,256]{3,2,1,0:T(8,128)S(1)}, f32[2,16,32,256]{3,2,1,0:T(8,128)}, u32[]{:S(2)}) copy-start(f32[2,16,32,256]{3,2,1,0:T(8,128)} %b_ref.9) | copy-start | bytes 3145732
  1.9 1.0 %copy-start.2 = (f32[16,32,256]{2,1,0:T(8,128)S(1)}, f32[16,32,256]{2,1,0:T(8,128)}, u32[]{:S(2)}) copy-start(f32[16,32,256]{2,1,0:T(8,128)} %ct_ref.9) | copy-start | bytes 1572868
  2.9 1.0 %copy-start.4 = (f32[16,32,256]{2,1,0:T(8,128)S(1)}, f32[16,32,256]{2,1,0:T(8,128)}, u32[]{:S(2)}) copy-start(f32[16,32,256]{2,1,0:T(8,128)} %cf_ref.5) | copy-start | bytes 1572868
  3.9 1.0 %copy-start.6 = (f32[16,32,256]{2,1,0:T(8,128)S(1)}, f32[16,32,256]{2,1,0:T(8,128)}, u32[]{:S(2)}) copy-start(f32[16,32,256]{2,1,0:T(8,128)} %mr_ref.3) | copy-start | bytes 1572868
  5.0 1.0 %copy-start.7 = (f32[16,32,256]{2,1,0:T(8,128)S(1)}, f32[16,32,256]{2,1,0:T(8,128)}, u32[]{:S(2)}) copy-start(f32[16,32,256]{2,1,0:T(8,128)} %d_ref.3) | copy-start | bytes 1572868
  6.0 26.8 %copy-start.1 = (f32[2,16,32,256]{3,2,1,0:T(8,128)S(1)}, f32[2,16,32,256]{3,2,1,0:T(8,128)}, u32[]{:S(2)}) copy-start(f32[2,16,32,256]{3,2,1,0:T(8,128)} %b_ref.9) | copy-start | bytes 3145732
  6.3 27.1 %collective-permute-start.4 = (f32[5,4,32,256]{3,2,1,0:T(8,128)S(1)}, f32[5,4,32,256]{3,2,1,0:T(8,128)S(1)}, u32[]{:S(2)}, u32[]{:S(2)}) collective-permute-start(f32[5,4,32,256]{3,2,1,0:T(8,128)S(1)} %get-tuple-element.35), channel_id=1, source_target_pairs={{0,8},{8,16},{16,24},{1,9},{9,17},{17,25},{2,10},{10,18},{18,26},{... | collective-permute-start | bytes 1966088 | tf_op jit(solution)/shard_map/ppermute | solution.py:495
  8.8 24.6 %collective-permute-start.5 = (f32[5,4,32,256]{3,2,1,0:T(8,128)S(1)}, f32[5,4,32,256]{3,2,1,0:T(8,128)S(1)}, u32[]{:S(2)}, u32[]{:S(2)}) collective-permute-start(f32[5,4,32,256]{3,2,1,0:T(8,128)S(1)} %get-tuple-element.36), channel_id=1, source_target_pairs={{8,0},{16,8},{24,16},{9,1},{17,9},{25,17},{10,2},{18,10},{26,18},{... | collective-permute-start | bytes 1966088 | tf_op jit(solution)/shard_map/ppermute | solution.py:495
  10.1 17.9 %collective-permute-start = (f32[40,8,256]{2,1,0:T(8,128)S(1)}, f32[40,8,256]{2,1,0:T(8,128)S(1)}, u32[]{:S(2)}, u32[]{:S(2)}) collective-permute-start(f32[40,8,256]{2,1,0:T(8,128)S(1)} %get-tuple-element.31), channel_id=1, source_target_pairs={{0,1},{1,2},{2,3},{3,4},{4,5},{5,6},{6,7},{8,9},{9,10},{10,11},{11... | collective-permute-start | bytes 983048 | tf_op jit(solution)/shard_map/ppermute | solution.py:495
  14.4 13.6 %collective-permute-start.1 = (f32[40,8,256]{2,1,0:T(8,128)S(1)}, f32[40,8,256]{2,1,0:T(8,128)S(1)}, u32[]{:S(2)}, u32[]{:S(2)}) collective-permute-start(f32[40,8,256]{2,1,0:T(8,128)S(1)} %get-tuple-element.32), channel_id=1, source_target_pairs={{1,0},{2,1},{3,2},{4,3},{5,4},{6,5},{7,6},{9,8},{10,9},{11,10},{12... | collective-permute-start | bytes 983048 | tf_op jit(solution)/shard_map/ppermute | solution.py:495
  28.0 5.8 %collective-permute-start.2 = (f32[2,10,8,256]{3,2,1,0:T(8,128)S(1)}, f32[2,10,8,256]{3,2,1,0:T(8,128)S(1)}, u32[]{:S(2)}, u32[]{:S(2)}) collective-permute-start(f32[2,10,8,256]{3,2,1,0:T(8,128)S(1)} %get-tuple-element.33), channel_id=1, source_target_pairs={{0,8},{8,16},{16,24},{1,9},{9,17},{17,25},{2,10},{10,18},{18,26},{... | collective-permute-start | bytes 491528 | tf_op jit(solution)/shard_map/ppermute | solution.py:495
  31.5 4.6 %collective-permute-start.3 = (f32[2,10,8,256]{3,2,1,0:T(8,128)S(1)}, f32[2,10,8,256]{3,2,1,0:T(8,128)S(1)}, u32[]{:S(2)}, u32[]{:S(2)}) collective-permute-start(f32[2,10,8,256]{3,2,1,0:T(8,128)S(1)} %get-tuple-element.34), channel_id=1, source_target_pairs={{8,0},{16,8},{24,16},{9,1},{17,9},{25,17},{10,2},{18,10},{26,18},{... | collective-permute-start | bytes 491528 | tf_op jit(solution)/shard_map/ppermute | solution.py:495
  36.2 22.4 %copy-start.3 = (f32[16,32,256]{2,1,0:T(8,128)S(1)}, f32[16,32,256]{2,1,0:T(8,128)}, u32[]{:S(2)}) copy-start(f32[16,32,256]{2,1,0:T(8,128)} %ct_ref.9) | copy-start | bytes 1572868
  43.5 7.1 %collective-permute-start.6 = (f32[2,4,32,256]{3,2,1,0:T(8,128)S(1)}, f32[2,4,32,256]{3,2,1,0:T(8,128)S(1)}, u32[]{:S(2)}, u32[]{:S(2)}) collective-permute-start(f32[2,4,32,256]{3,2,1,0:T(8,128)S(1)} %get-tuple-element.47), channel_id=1, source_target_pairs={{0,8},{8,16},{16,24},{1,9},{9,17},{17,25},{2,10},{10,18},{18,26},{... | collective-permute-start | bytes 786440 | tf_op jit(solution)/shard_map/ppermute | solution.py:495
  49.2 3.4 %collective-permute-start.7 = (f32[2,4,32,256]{3,2,1,0:T(8,128)S(1)}, f32[2,4,32,256]{3,2,1,0:T(8,128)S(1)}, u32[]{:S(2)}, u32[]{:S(2)}) collective-permute-start(f32[2,4,32,256]{3,2,1,0:T(8,128)S(1)} %get-tuple-element.48), channel_id=1, source_target_pairs={{8,0},{16,8},{24,16},{9,1},{17,9},{25,17},{10,2},{18,10},{26,18},{... | collective-permute-start | bytes 786440 | tf_op jit(solution)/shard_map/ppermute | solution.py:495
  52.8 23.8 %collective-permute-start.8 = (f32[24,8,256]{2,1,0:T(8,128)S(1)}, f32[24,8,256]{2,1,0:T(8,128)S(1)}, u32[]{:S(2)}, u32[]{:S(2)}) collective-permute-start(f32[24,8,256]{2,1,0:T(8,128)S(1)} %get-tuple-element.49), channel_id=1, source_target_pairs={{0,1},{1,2},{2,3},{3,4},{4,5},{5,6},{6,7},{8,9},{9,10},{10,11},{11... | collective-permute-start | bytes 589832 | tf_op jit(solution)/shard_map/ppermute | solution.py:495
  57.2 19.4 %collective-permute-start.9 = (f32[24,8,256]{2,1,0:T(8,128)S(1)}, f32[24,8,256]{2,1,0:T(8,128)S(1)}, u32[]{:S(2)}, u32[]{:S(2)}) collective-permute-start(f32[24,8,256]{2,1,0:T(8,128)S(1)} %get-tuple-element.50), channel_id=1, source_target_pairs={{1,0},{2,1},{3,2},{4,3},{5,4},{6,5},{7,6},{9,8},{10,9},{11,10},{12... | collective-permute-start | bytes 589832 | tf_op jit(solution)/shard_map/ppermute | solution.py:495
  76.7 17.9 %copy-start.5 = (f32[16,32,256]{2,1,0:T(8,128)S(1)}, f32[16,32,256]{2,1,0:T(8,128)}, u32[]{:S(2)}) copy-start(f32[16,32,256]{2,1,0:T(8,128)} %cf_ref.5) | copy-start | bytes 1572868

commit v3 on v2

v3 whole, which is shorter than its diff:
```python
import jax
import jax.numpy as jnp
from jax import lax
from jax.experimental import pallas as pl
from jax.experimental.pallas import tpu as pltpu
from jax.sharding import PartitionSpec as P

OMEGA = 0.8
EPSILON = 1e-06
H = 4
AXES = ("gx", "gy")
F32 = jnp.float32
LIMIT = 24 * 1024 * 1024
FALLBACK = (0.72, -0.28)


def vmem(n):
    return [pl.BlockSpec(memory_space=pltpu.VMEM)] * n


def cmul(a, b):
    return (a[0] * b[0] - a[1] * b[1], a[0] * b[1] + a[1] * b[0])


def cconj(a):
    return (a[0], -a[1])


def cadd(a, b):
    return (a[0] + b[0], a[1] + b[1])


def csub(a, b):
    return (a[0] - b[0], a[1] - b[1])


def cdiv(n, d):
    scale = d[0] * d[0] + d[1] * d[1]
    return (
        (n[0] * d[0] + n[1] * d[1]) / scale,
        (n[1] * d[0] - n[0] * d[1]) / scale,
    )


def smooth_yz(plane):
    rows, lanes = plane.shape
    y = plane + plane + pltpu.roll(plane, 1, 0) + pltpu.roll(plane, rows - 1, 0)
    lane = lax.broadcasted_iota(jnp.int32, plane.shape, 1)
    up = jnp.where(lane == 0, 0.0, pltpu.roll(y, 1, 1))
    down = jnp.where(lane == lanes - 1, 0.0, pltpu.roll(y, lanes - 1, 1))
    return y + y + up + down


def weighted(ref, i):
    out = []
    for part in range(2):
        mid = ref[part, i]
        total = smooth_yz(ref[part, i - 1] + mid + mid + ref[part, i + 1])
        out.append((total - 8.0 * mid) * (1.0 / 160.0))
    return tuple(out)


def coefficients(c, mr, d):
    shift = d + 0.5 * mr
    mod = mr * mr + shift * shift
    den = mod * c
    inv = 1.0 / jnp.where(den == 0.0, 1.0, den)
    k = OMEGA * c * c * inv
    rc = mod * inv
    return (k * mr, -(k * shift)), (rc * mr, rc * d)


def loop(ranges, body):
    for lo, hi in ranges:

        def step(i, carry):
            body(i)
            return carry

        lax.fori_loop(lo, hi, step, 0, unroll=2)


def half_step(u_ref, p_ref, w_ref, ranges):
    def body(i):
        pw = cmul((p_ref[0, i], p_ref[1, i]), weighted(u_ref, i))
        w_ref[0, i] = 1.2 * u_ref[0, i] + pw[0]
        w_ref[1, i] = 1.2 * u_ref[1, i] + pw[1]

    loop(ranges, body)


def image(w_ref, n_ref, i):
    nw = cmul((n_ref[0, i], n_ref[1, i]), (w_ref[0, i], w_ref[1, i]))
    return csub(nw, weighted(w_ref, i))


def advance(w_ref, n_ref, v_ref, th, next_ref, ranges, p_ref=None, u_ref=None):
    def body(i):
        y = csub(image(w_ref, n_ref, i), cmul(th, (v_ref[0, i], v_ref[1, i])))
        for part in range(2):
            next_ref[part, i] = y[part]
        if p_ref is not None:
            u = cmul((p_ref[0, i], p_ref[1, i]), y)
            for part in range(2):
                u_ref[part, i] = u[part]

    loop(ranges, body)


def inside(planes, k):
    return [(H + k, planes - H - k)]


def outside(planes, k):
    return [(k, H + k), (planes - H - k, planes - k)]


def two_applications(part_of, planes, th, p_ref, n_ref, u_ref, v_ref, w_refs, next_refs):
    half_step(u_ref, p_ref, w_refs[0], part_of(planes, 1))
    advance(w_refs[0], n_ref, v_ref, th, next_refs[0], part_of(planes, 2), p_ref, u_ref)
    half_step(u_ref, p_ref, w_refs[1], part_of(planes, 3))
    advance(w_refs[1], n_ref, next_refs[0], th, next_refs[1], part_of(planes, 4))


def total_of(ref):
    rows = ref[...].reshape(ref.shape[0], ref.shape[-1])
    tot = jnp.sum(rows, axis=0, keepdims=True)
    lane = lax.broadcasted_iota(jnp.int32, tot.shape, 1)
    return lambda k: jnp.sum(jnp.where(lane == k, tot, 0.0), axis=1, keepdims=True)


def pack_lanes(values, first=0):
    lane = lax.broadcasted_iota(jnp.int32, (1, 128), 1)
    row = jnp.zeros((1, 128), F32)
    for k, v in enumerate(values, first):
        s = jnp.sum(jnp.sum(v, axis=0, keepdims=True), axis=1, keepdims=True)
        row = jnp.where(lane == k, s, row)
    return row


def fold(x):
    out = x[:, :128]
    for b in range(128, x.shape[1], 128):
        out = out + x[:, b : b + 128]
    return out


def pairs_of(rights):
    return [(left, right) for right in rights for left in range(right + 1)]


def gram_rows(fields, ct_ref, pairs, first=0):
    nx, ny, _ = ct_ref.shape
    used = sorted({k for pair in pairs for k in pair})
    count = sum(1 if left == right else 2 for left, right in pairs)

    def body(i, acc):
        acc = list(acc)
        for a in range(0, ny, 8):
            rows = pl.ds(a, 8)
            ct = ct_ref[i, rows]
            vs = {}
            for k in used:
                ref, base, scaled = fields[k]
                v = (ref[0, i + base, rows], ref[1, i + base, rows])
                vs[k] = (ct * v[0], ct * v[1]) if scaled else v
            k = 0
            for left, right in pairs:
                (lr, li), (rr, ri) = vs[left], vs[right]
                acc[k] = acc[k] + fold(lr * rr + li * ri)
                k += 1
                if right > left:
                    acc[k] = acc[k] + fold(lr * ri - li * rr)
                    k += 1
        return tuple(acc)

    acc = lax.fori_loop(0, nx, body, (jnp.zeros((8, 128), F32),) * count)
    return pack_lanes(acc, first)


def put(row, out_ref):
    for k in range(out_ref.shape[0]):
        out_ref[k] = row


def gram_entries(pick, pairs, entries):
    k = 0
    for left, right in pairs:
        if left == right:
            entries[left, right] = (pick(k), jnp.zeros((1, 1), F32))
            k += 1
        else:
            entries[left, right] = (pick(k), pick(k + 1))
            entries[right, left] = cconj(entries[left, right])
            k += 2
    return entries


def shift_from(ref):
    pick = total_of(ref)
    den = pick(2)
    safe = jnp.where(den > 0.0, den, 1.0)
    return tuple(jnp.where(den > 0.0, pick(k) / safe, FALLBACK[k]) for k in range(2))


EARLY = pairs_of((0, 1, 2))
LATE = pairs_of((3, 4))


def pack_pair(first, second, top):
    sub = lax.broadcasted_iota(jnp.int32, first.shape, 0)
    rolled = pltpu.roll(second, 4, 0)
    if top:
        return jnp.where(sub < 4, first, rolled)
    return jnp.where(sub < 4, rolled, first)


def unpack_pair(right, left):
    sub = lax.broadcasted_iota(jnp.int32, right.shape, 0)
    first = jnp.where(sub < 4, right, left)
    second = pltpu.roll(jnp.where(sub < 4, left, right), 4, 0)
    return first, second


def own_values(b_ref, cf_ref, ct_ref, mr_ref, d_ref):
    def get(i, rows):
        ct = ct_ref[i, rows]
        r = 1.0 / ct
        return (
            b_ref[0, i, rows] * r,
            b_ref[1, i, rows] * r,
            cf_ref[i, rows] * ct,
            mr_ref[i, rows],
            d_ref[i, rows],
        )

    return get


def fetch(pairs, sems):
    copies = [pltpu.make_async_copy(a, b, sems.at[k]) for k, (a, b) in enumerate(pairs)]
    for c in copies:
        c.start()
    for c in copies:
        c.wait()


def rows_kernel(b_ref, cf_ref, ct_ref, mr_ref, d_ref, top_ref, bot_ref, *scratch):
    blocks, coefs, sems = scratch
    nx, ny, _ = cf_ref.shape
    pairs = []
    for side, at in enumerate((0, ny - 8)):
        rows = pl.ds(at, 8)
        pairs.append((b_ref.at[:, :, rows], blocks.at[side]))
        for k, ref in enumerate((cf_ref, ct_ref, mr_ref, d_ref)):
            pairs.append((ref.at[:, rows], coefs.at[side, k]))
    fetch(pairs, sems)
    for side, out_ref in enumerate((top_ref, bot_ref)):
        get = own_values(blocks.at[side], *(coefs.at[side, k] for k in range(4)))
        top = side == 0

        def body(j, carry):
            a, b = get(2 * j, pl.ds(0, 8)), get(2 * j + 1, pl.ds(0, 8))
            out_ref[2 * j] = pack_pair(a[0], a[1], top)
            out_ref[2 * j + 1] = pack_pair(b[0], b[1], top)
            for f in range(3):
                out_ref[nx + f * nx // 2 + j] = pack_pair(a[2 + f], b[2 + f], top)
            return carry

        lax.fori_loop(0, nx // 2, body, 0, unroll=2)


def planes_kernel(after_ref, b_ref, cf_ref, ct_ref, mr_ref, d_ref, lo_ref, hi_ref, *scratch):
    blocks, coefs, sems = scratch
    nx, ny, _ = cf_ref.shape
    pairs = []
    for side, at in enumerate((0, nx - H)):
        span = pl.ds(at, H)
        pairs.append((b_ref.at[:, span], blocks.at[side]))
        for k, ref in enumerate((cf_ref, ct_ref, mr_ref, d_ref)):
            pairs.append((ref.at[span], coefs.at[side, k]))
    fetch(pairs, sems)
    for side, out_ref in enumerate((lo_ref, hi_ref)):
        get = own_values(blocks.at[side], *(coefs.at[side, k] for k in range(4)))
        for i in range(H):
            for f, value in enumerate(get(i, pl.ds(0, ny))):
                out_ref[f, i] = value


def corners_kernel(yl_ref, yr_ref, lo_ref, hi_ref):
    count = yl_ref.shape[0]
    nx = count * 2 // 5
    for k, ref in enumerate((yl_ref, yr_ref)):
        for out_ref, base in ((lo_ref, 0), (hi_ref, nx - H)):
            for i in range(H):
                out_ref[k, i] = ref[base + i]
            for f in range(3):
                for j in range(H // 2):
                    at = nx + f * nx // 2 + base // 2 + j
                    out_ref[k, H + f * H // 2 + j] = ref[at]


def store_fields(refs, plane, rows, v, c, mr, d):
    p_ref, n_ref, u_ref, v_ref = refs
    p, n = coefficients(c, mr, d)
    u = cmul(p, v)
    for part in range(2):
        p_ref[part, plane, rows] = p[part]
        n_ref[part, plane, rows] = n[part]
        u_ref[part, plane, rows] = u[part]
        v_ref[part, plane, rows] = v[part]


def own_kernel(b_ref, cf_ref, ct_ref, mr_ref, d_ref, p_ref, n_ref, u_ref, v_ref, out_ref, w_ref):
    nx, ny, nz = cf_ref.shape
    get = own_values(b_ref, cf_ref, ct_ref, mr_ref, d_ref)
    rows, rest = pl.ds(0, ny), pl.ds(ny, 8)
    zero = jnp.zeros((8, nz), F32)

    def body(i):
        vr, vi, c, mr, d = get(i, rows)
        store_fields((p_ref, n_ref, u_ref, v_ref), i + H, rows, (vr, vi), c, mr, d)
        for part in range(2):
            p_ref[part, i + H, rest] = zero
            u_ref[part, i + H, rest] = zero

    loop([(0, nx)], body)
    blank = jnp.zeros((ny + 8, nz), F32)
    for ref in (u_ref, w_ref):
        for part in range(2):
            ref[part, H - 1] = blank
            ref[part, nx + H] = blank
    half_step(u_ref, p_ref, w_ref, [(H, nx + H)])

    def dots(i, acc):
        acc = list(acc)
        y = image(w_ref, n_ref, i + H)
        for a in range(0, ny, 8):
            ct = ct_ref[i, pl.ds(a, 8)]
            yr, yi = y[0][a : a + 8] * ct, y[1][a : a + 8] * ct
            br, bi = b_ref[0, i, pl.ds(a, 8)], b_ref[1, i, pl.ds(a, 8)]
            acc[0] = acc[0] + fold(br * yr + bi * yi)
            acc[1] = acc[1] + fold(br * yi - bi * yr)
            acc[2] = acc[2] + fold(br * br + bi * bi)
        return tuple(acc)

    acc = lax.fori_loop(0, nx, dots, (jnp.zeros((8, 128), F32),) * 3, unroll=2)
    put(pack_lanes(acc), out_ref)


def tails(refs, left, right, ny, fields, coefs, planes):
    rows = pl.ds(ny, 8)
    v = [unpack_pair(right(k), left(k)) for k in fields]
    c = [unpack_pair(right(k), left(k)) for k in coefs]
    for k in range(2):
        store_fields(refs, planes[k], rows, v[k], c[0][k], c[1][k], c[2][k])


def sides_kernel(th_ref, xl_ref, xr_ref, yl_ref, yr_ref, *refs):
    p_ref, n_ref, u_ref, v_ref, w0_ref, w1_ref, v1_ref, v2_ref = refs[4:]
    state = (p_ref, n_ref, u_ref, v_ref)
    ny = xl_ref.shape[2]
    planes = p_ref.shape[1]
    nx = planes - 2 * H
    rows = pl.ds(0, ny)
    for ref, base in ((xl_ref, 0), (xr_ref, nx + H)):

        def side(i):
            vr, vi, c, mr, d = (ref[f, i] for f in range(5))
            store_fields(state, base + i, rows, (vr, vi), c, mr, d)

        loop([(0, H)], side)

    def pair(j):
        coefs = [nx + f * nx // 2 + j for f in range(3)]
        at = (H + 2 * j, H + 2 * j + 1)
        own = (2 * j, 2 * j + 1)
        tails(state, lambda k: yl_ref[k], lambda k: yr_ref[k], ny, own, coefs, at)

    loop([(0, nx // 2)], pair)
    th = shift_from(th_ref)
    two_applications(inside, planes, th, *state, (w0_ref, w1_ref), (v1_ref, v2_ref))


def first_kernel(th_ref, cl_ref, cr_ref, *refs):
    p_ref, n_ref, u_ref, v_ref, w0_ref, w1_ref, v1_ref, v2_ref, top_ref, bot_ref = refs[8:]
    state = (p_ref, n_ref, u_ref, v_ref)
    planes = p_ref.shape[1]
    nx, ny = planes - 2 * H, p_ref.shape[2] - 8
    for ref, base in ((cl_ref, 0), (cr_ref, nx + H)):
        for j in range(H // 2):
            coefs = [H + f * H // 2 + j for f in range(3)]
            at = (base + 2 * j, base + 2 * j + 1)
            own = (2 * j, 2 * j + 1)
            tails(state, lambda k: ref[0, k], lambda k: ref[1, k], ny, own, coefs, at)
    th = shift_from(th_ref)
    two_applications(outside, planes, th, *state, (w0_ref, w1_ref), (v1_ref, v2_ref))
    for out_ref, rows, top in ((top_ref, pl.ds(0, 8), True), (bot_ref, pl.ds(ny - 8, 8), False)):

        def pack(i):
            a, b = v2_ref[0, i + H, rows], v2_ref[1, i + H, rows]
            out_ref[i] = pack_pair(a, b, top)

        loop([(0, nx)], pack)


def early_kernel(b_ref, ct_ref, v1_ref, v2_ref, out_ref):
    fields = ((b_ref, 0, False), (v1_ref, H, True), (v2_ref, H, True))
    put(gram_rows(fields, ct_ref, EARLY), out_ref)


def rows_back_kernel(yl_ref, yr_ref, _, v_ref, lo_ref, hi_ref):
    nx, ny = yl_ref.shape[0], v_ref.shape[2] - 8
    rows = pl.ds(ny, 8)

    def tail(i):
        for part, value in enumerate(unpack_pair(yr_ref[i], yl_ref[i])):
            v_ref[part, i + H, rows] = value

    loop([(0, nx)], tail)
    for part in range(2):
        for i in range(H):
            lo_ref[part, i] = v_ref[part, H + i]
            hi_ref[part, i] = v_ref[part, nx + i]


def inner_kernel(th_ref, p_ref, n_ref, v_ref, u_ref, w2_ref, w3_ref, v3_ref, v4_ref):
    planes = p_ref.shape[1]
    th = shift_from(th_ref)

    def fill(i):
        u = cmul((p_ref[0, i], p_ref[1, i]), (v_ref[0, i], v_ref[1, i]))
        for part in range(2):
            u_ref[part, i] = u[part]

    loop([(H, planes - H)], fill)
    two_applications(
        inside, planes, th, p_ref, n_ref, u_ref, v_ref, (w2_ref, w3_ref), (v3_ref, v4_ref)
    )


def second_kernel(th_ref, e_ref, xl_ref, xr_ref, p_ref, n_ref, b_ref, ct_ref, v1_ref, *refs):
    v2_ref, u_ref, w2_ref, w3_ref, v3_ref, v4_ref, out_ref = refs[6:]
    planes = p_ref.shape[1]
    th = shift_from(th_ref)
    for ref, base in ((xl_ref, 0), (xr_ref, planes - H)):
        for i in range(H):
            v = (ref[0, i], ref[1, i])
            u = cmul((p_ref[0, base + i], p_ref[1, base + i]), v)
            for part in range(2):
                v2_ref[part, base + i] = v[part]
                u_ref[part, base + i] = u[part]
    two_applications(
        outside, planes, th, p_ref, n_ref, u_ref, v2_ref, (w2_ref, w3_ref), (v3_ref, v4_ref)
    )
    fields = (
        (b_ref, 0, False), (v1_ref, H, True), (v2_ref, H, True), (v3_ref, H, True),
        (v4_ref, H, True),
    )
    put(e_ref[0] + gram_rows(fields, ct_ref, LATE, 9), out_ref)


def recurrences(th, gram):
    def inner(x, y):
        total = None
        for i, xi in enumerate(x):
            part = None
            for j, yj in enumerate(y):
                t = cmul(gram[i, j], yj)
                part = t if part is None else cadd(part, t)
            t = cmul(cconj(xi), part)
            total = t if total is None else cadd(total, t)
        return total

    def apply(x):
        scaled = [cmul(th, c) for c in x]
        return [scaled[0]] + [cadd(x[k], scaled[k + 1]) for k in range(len(x) - 1)] + [x[-1]]

    def lincomb(x, s, y):
        out = []
        for k in range(max(len(x), len(y))):
            a = x[k] if k < len(x) else None
            b = cmul(s, y[k]) if k < len(y) else None
            out.append(b if a is None else a if b is None else cadd(a, b))
        return out

    def neg(s):
        return (-s[0], -s[1])

    one = (jnp.ones((1, 1), F32), jnp.zeros((1, 1), F32))
    residual, direction, shadow, answer = [one], [one], [one], []
    rho = inner(shadow, residual)
    for step in range(2):
        image = apply(direction)
        alpha = cdiv(rho, inner(shadow, image))
        half = lincomb(residual, neg(alpha), image)
        second = apply(half)
        prod = inner(second, half)
        norm = inner(second, second)[0] + EPSILON
        omega = (prod[0] / norm, prod[1] / norm)
        answer = lincomb(lincomb(answer, alpha, direction), omega, half)
        residual = lincomb(half, neg(omega), second)
        if step == 0:
            rho_next = inner(shadow, residual)
            beta = cmul(cdiv(rho_next, rho), cdiv(alpha, omega))
            direction = lincomb(residual, beta, lincomb(direction, neg(omega), image))
            rho = rho_next
    return answer, residual


def final_kernel(
    th_ref, g_ref, b_ref, cf_ref, ct_ref,
    w0_ref, w1_ref, w2_ref, w3_ref, v1_ref, v2_ref, v3_ref, v4_ref,
    sol_ref, res_ref,
):
    nx, ny, nz = cf_ref.shape
    th = shift_from(th_ref)
    entries = gram_entries(total_of(g_ref), EARLY + LATE, {})
    answer, residual = recurrences(th, entries)

    def spread(c):
        return tuple(jnp.broadcast_to(x, (8, nz)) for x in c)

    answer, residual = [spread(c) for c in answer], [spread(c) for c in residual]

    def body(i, carry):
        for a in range(0, ny, 8):
            rows = pl.ds(a, 8)
            acc = None
            for c, ref in zip(answer, (w0_ref, w1_ref, w2_ref, w3_ref)):
                t = cmul(c, (ref[0, i + H, rows], ref[1, i + H, rows]))
                acc = t if acc is None else cadd(acc, t)
            inv = 1.0 / cf_ref[i, rows]
            sol_ref[0, i, rows] = acc[0] * inv
            sol_ref[1, i, rows] = acc[1] * inv
            acc = None
            for c, ref in zip(residual[1:], (v1_ref, v2_ref, v3_ref, v4_ref)):
                t = cmul(c, (ref[0, i + H, rows], ref[1, i + H, rows]))
                acc = t if acc is None else cadd(acc, t)
            ct = ct_ref[i, rows]
            t = cmul(residual[0], (b_ref[0, i, rows], b_ref[1, i, rows]))
            res_ref[0, i, rows] = acc[0] * ct + t[0]
            res_ref[1, i, rows] = acc[1] * ct + t[1]
        return carry

    lax.fori_loop(0, nx, body, 0)


def call(kernel, outs, scratch, *args, alias=None):
    return pl.pallas_call(
        kernel,
        out_shape=[jax.ShapeDtypeStruct(s, F32) for s in outs],
        in_specs=vmem(len(args)),
        out_specs=vmem(len(outs)),
        scratch_shapes=[pltpu.VMEM(s, F32) for s in scratch],
        input_output_aliases=alias or {},
        compiler_params=pltpu.CompilerParams(vmem_limit_bytes=LIMIT),
    )(*args)


def edge_call(kernel, outs, scratch, *args):
    return pl.pallas_call(
        kernel,
        out_shape=[jax.ShapeDtypeStruct(s, F32) for s in outs],
        in_specs=[pl.BlockSpec(memory_space=pl.ANY)] * len(args),
        out_specs=vmem(len(outs)),
        scratch_shapes=[pltpu.VMEM(s, F32) for s in scratch] + [pltpu.SemaphoreType.DMA((10,))],
        compiler_params=pltpu.CompilerParams(vmem_limit_bytes=LIMIT),
    )(*args)


def both_ways(to_lower, to_upper, axis):
    n = lax.axis_size(axis)
    up = [(i, i + 1) for i in range(n - 1)]
    down = [(i + 1, i) for i in range(n - 1)]
    return lax.ppermute(to_upper, axis, up), lax.ppermute(to_lower, axis, down)


def local(b, cf, ct, mr, d):
    nx, ny, nz = cf.shape
    peers = lax.axis_size("gx") * lax.axis_size("gy")
    planes = nx + 2 * H
    own = (2, nx, ny, nz)
    ext = (2, planes, ny + 2 * H, nz)
    face = (2, H, ny + 2 * H, nz)
    rim = (nx + 3 * nx // 2, 8, nz)
    corner = (2, H + 3 * H // 2, 8, nz)
    inputs = (b, cf, ct, mr, d)

    top, bot = edge_call(
        rows_kernel, [rim, rim], [(2, 2, nx, 8, nz), (2, 4, nx, 8, nz)], *inputs
    )
    yl, yr = both_ways(top, bot, "gy")
    lo, hi = edge_call(
        planes_kernel, [(5, H, ny, nz)] * 2, [(2, 2, H, ny, nz), (2, 4, H, ny, nz)], top, *inputs
    )
    xl, xr = both_ways(lo, hi, "gx")
    *state, th = call(own_kernel, [ext] * 4 + [(peers, 1, 128)], [ext], *inputs)
    th = lax.all_to_all(th, AXES, 0, 0)
    lo, hi = call(corners_kernel, [corner] * 2, [], yl, yr)
    cl, cr = both_ways(lo, hi, "gx")
    state = call(
        sides_kernel, [ext] * 8, [], th, xl, xr, yl, yr, *state,
        alias={5 + k: k for k in range(4)},
    )
    p, n, _, _, w0, w1, v1, v2, top, bot = call(
        first_kernel, [ext] * 8 + [(nx, 8, nz)] * 2, [], th, cl, cr, *state,
        alias={3 + k: k for k in range(8)},
    )
    yl, yr = both_ways(top, bot, "gy")
    early = call(early_kernel, [(1, 1, 128)], [], b, ct, v1, v2)[0]
    v2, lo, hi = call(rows_back_kernel, [ext, face, face], [], yl, yr, v2, alias={2: 0})
    xl, xr = both_ways(lo, hi, "gx")
    state = call(inner_kernel, [ext] * 5, [], th, p, n, v2)
    v2, _, w2, w3, v3, v4, gram = call(
        second_kernel, [ext] * 6 + [(peers, 1, 128)], [],
        th, early, xl, xr, p, n, b, ct, v1, v2, *state,
        alias={9 + k: k for k in range(6)},
    )
    gram = lax.all_to_all(gram, AXES, 0, 0)
    return tuple(
        call(final_kernel, [own, own], [], th, gram, b, cf, ct, w0, w1, w2, w3, v1, v2, v3, v4)
    )


def solution(mesh):
    field, coef = P(None, "gx", "gy", None), P("gx", "gy", None)
    return jax.shard_map(
        local,
        mesh=mesh,
        in_specs=(field, coef, coef, coef, coef),
        out_specs=(field, field),
        check_vma=False,
    )
```

time: 98.1 us -> 101 us (1.030)
  starting transfers between devices: 26.9 us -> 20.5 us
  Pallas kernels: 21.6 us -> 27.3 us
  blocking collectives: 26.1 us -> 29.2 us
    ppermute x5, starting transfers between devices: 20.4 us -> 14 us  [both_ways(): lax.ppermute(to_upper, axis, up)]
    pallas_call x9, Pallas kernels: 21.6 us -> 25.3 us  [call(): pl.pallas_call(kernel, out_shape=[jax.ShapeDtypeStruct(s, F32) for s in o...]
    all_to_all x2, blocking collectives: 26.1 us -> 29.2 us  [the longest x1 16.3 us: local(): th = lax.all_to_all(th, AXES, 0, 0)]
    pallas_call x0 -> x2, Pallas kernels: none -> 2.01 us  [edge_call(): pl.pallas_call(kernel, out_shape=[jax.ShapeDtypeStruct(s, F32) for s in o...]
    unnamed x16 -> x14, local copies, waits for them, and re-layouts: 5.39 us -> 5.4 us
  transfers between devices with their start and end apart: 10 -> 10, of which waited for: 3 -> 3; matrix products, arithmetic and copies ran while one was open for 0% -> 0% of each run, Pallas kernels for 2% -> 14%
where the time goes in v3:
time: 101 us; the launch traced here: 100 us
  blocking collectives  29.2 us (29%)
  Pallas kernels  27.3 us (27%)
  starting transfers between devices  20.5 us (20%)
  waiting for transfers between devices  17 us (17%)
  local copies, waits for them, and re-layouts  5.4 us (5%)
    pallas_call x9, Pallas kernels, call(): pl.pallas_call(kernel, out_shape=[jax.ShapeDtypeStruct(s, F32) for s in o...  25.3 us
    all_to_all x1, blocking collectives, local(): th = lax.all_to_all(th, AXES, 0, 0)  16.3 us
    ppermute x5, starting transfers between devices, both_ways(): lax.ppermute(to_upper, axis, up)  14 us
    ppermute x5, waiting for transfers between devices, both_ways(): lax.ppermute(to_upper, axis, up)  12.9 us
    all_to_all x1, blocking collectives, local(): gram = lax.all_to_all(gram, AXES, 0, 0)  12.9 us
    ppermute x5, starting transfers between devices, both_ways(): lax.ppermute(to_lower, axis, down)  6.46 us
    unnamed x14, local copies, waits for them, and re-layouts  5.4 us
    ppermute x5, waiting for transfers between devices, both_ways(): lax.ppermute(to_lower, axis, down)  4.14 us
  transfers between devices with their start and end apart: 10, of which 3 were waited for; matrix products, arithmetic and copies ran while one was open for 0% of the time, Pallas kernels for 14%

profile of v3, /device:TPU:0, one launch (start us, length us, event | category | flops | bytes accessed | tf_op | source)
XLA Modules:
  0.0 100.2 jit_solution(4435652286883852522)
XLA Ops:
  0.6 1.2 %copy-done = f32[2,16,32,256]{3,2,1,0:T(8,128)S(1)} copy-done((f32[2,16,32,256]{3,2,1,0:T(8,128)S(1)}, f32[2,16,32,256]{3,2,1,0:T(8,128)}, u32[]{:S(2)}) %copy-start) | copy-done | bytes 1048600
  3.9 1.0 %copy-done.5 = f32[16,32,256]{2,1,0:T(8,128)S(1)} copy-done((f32[16,32,256]{2,1,0:T(8,128)S(1)}, f32[16,32,256]{2,1,0:T(8,128)}, u32[]{:S(2)}) %copy-start.5) | copy-done | bytes 524312
  5.0 1.0 %copy-done.6 = f32[16,32,256]{2,1,0:T(8,128)S(1)} copy-done((f32[16,32,256]{2,1,0:T(8,128)S(1)}, f32[16,32,256]{2,1,0:T(8,128)}, u32[]{:S(2)}) %copy-start.6) | copy-done | bytes 524312
  6.5 1.6 %shard_map.71 = (f32[5,4,32,256]{3,2,1,0:T(8,128)S(1)}, f32[5,4,32,256]{3,2,1,0:T(8,128)S(1)}) custom-call(f32[40,8,256]{2,1,0:T(8,128)S(1)} %get-tuple-element.45.after_ref, f32[2,16,32,256]{3,2,1,0:T(8,128)S(1)} %copy-done, f32[16,32,256]{2,1,0:T(8,128)S(1)} %copy-done.4, f32[16,32,256]{2,1,0:T(8,128)S(1)} %copy-done.2, f32[16,32,256]{2,1,0:T(8,128)S(1)} %copy-done.5, ...), custom_call_target="tpu_custom_call" | custom-call | tf_op jit(solution)/shard_map/pallas_call | solution.py:562
  8.1 2.4 %collective-permute-start.4 = (f32[5,4,32,256]{3,2,1,0:T(8,128)S(1)}, f32[5,4,32,256]{3,2,1,0:T(8,128)S(1)}, u32[]{:S(2)}, u32[]{:S(2)}) collective-permute-start(f32[5,4,32,256]{3,2,1,0:T(8,128)S(1)} %get-tuple-element.48), channel_id=1, source_target_pairs={{0,8},{8,16},{16,24},{1,9},{9,17},{17,25},{2,10},{10,18},{18,26},{... | collective-permute-start | bytes 1966088 | tf_op jit(solution)/shard_map/ppermute | solution.py:576
  10.5 1.3 %collective-permute-start.5 = (f32[5,4,32,256]{3,2,1,0:T(8,128)S(1)}, f32[5,4,32,256]{3,2,1,0:T(8,128)S(1)}, u32[]{:S(2)}, u32[]{:S(2)}) collective-permute-start(f32[5,4,32,256]{3,2,1,0:T(8,128)S(1)} %get-tuple-element.49), channel_id=1, source_target_pairs={{8,0},{16,8},{24,16},{9,1},{17,9},{25,17},{10,2},{18,10},{26,18},{... | collective-permute-start | bytes 1966088 | tf_op jit(solution)/shard_map/ppermute | solution.py:576
  11.8 4.2 %collective-permute-start = (f32[40,8,256]{2,1,0:T(8,128)S(1)}, f32[40,8,256]{2,1,0:T(8,128)S(1)}, u32[]{:S(2)}, u32[]{:S(2)}) collective-permute-start(f32[40,8,256]{2,1,0:T(8,128)S(1)} %get-tuple-element.44), channel_id=1, source_target_pairs={{0,1},{1,2},{2,3},{3,4},{4,5},{5,6},{6,7},{8,9},{9,10},{10,11},{11... | collective-permute-start | bytes 983048 | tf_op jit(solution)/shard_map/ppermute | solution.py:576
  16.0 1.3 %collective-permute-start.1 = (f32[40,8,256]{2,1,0:T(8,128)S(1)}, f32[40,8,256]{2,1,0:T(8,128)S(1)}, u32[]{:S(2)}, u32[]{:S(2)}) collective-permute-start(f32[40,8,256]{2,1,0:T(8,128)S(1)} %get-tuple-element.45.after_ref), channel_id=1, source_target_pairs={{1,0},{2,1},{3,2},{4,3},{5,4},{6,5},{7,6},{9,8},{10,9},{11,10},{12... | collective-permute-start | bytes 983048 | tf_op jit(solution)/shard_map/ppermute | solution.py:576
  17.3 12.3 %collective-permute-done.yl_ref = f32[40,8,256]{2,1,0:T(8,128)S(1)} collective-permute-done((f32[40,8,256]{2,1,0:T(8,128)S(1)}, f32[40,8,256]{2,1,0:T(8,128)S(1)}, u32[]{:S(2)}, u32[]{:S(2)}) %collective-permute-start) | collective-permute-done | bytes 327712 | tf_op jit(solution)/shard_map/ppermute | solution.py:576
  29.7 3.5 %collective-permute-start.2 = (f32[2,10,8,256]{3,2,1,0:T(8,128)S(1)}, f32[2,10,8,256]{3,2,1,0:T(8,128)S(1)}, u32[]{:S(2)}, u32[]{:S(2)}) collective-permute-start(f32[2,10,8,256]{3,2,1,0:T(8,128)S(1)} %get-tuple-element.46), channel_id=1, source_target_pairs={{0,8},{8,16},{16,24},{1,9},{9,17},{17,25},{2,10},{10,18},{18,26},{... | collective-permute-start | bytes 491528 | tf_op jit(solution)/shard_map/ppermute | solution.py:576
  33.2 1.3 %collective-permute-start.3 = (f32[2,10,8,256]{3,2,1,0:T(8,128)S(1)}, f32[2,10,8,256]{3,2,1,0:T(8,128)S(1)}, u32[]{:S(2)}, u32[]{:S(2)}) collective-permute-start(f32[2,10,8,256]{3,2,1,0:T(8,128)S(1)} %get-tuple-element.47), channel_id=1, source_target_pairs={{8,0},{16,8},{24,16},{9,1},{17,9},{25,17},{10,2},{18,10},{26,18},{... | collective-permute-start | bytes 491528 | tf_op jit(solution)/shard_map/ppermute | solution.py:576
  34.5 3.5 %shard_map.68 = (f32[2,24,40,256]{3,2,1,0:T(8,128)S(1)}, f32[2,24,40,256]{3,2,1,0:T(8,128)S(1)}, f32[2,24,40,256]{3,2,1,0:T(8,128)S(1)}, f32[2,24,40,256]{3,2,1,0:T(8,128)S(1)}, f32[32,1,128]{2,1,0:T(1,128)S(1)}) custom-call(f32[2,16,32,256]{3,2,1,0:T(8,128)S(1)} %copy-done.1, f32[16,32,256]{2,1,0:T(8,128)S(1)} %copy-done.4, f32[16,32,256]{2,1,0:T(8,128)S(1)} %copy-done.2, ...), custom_call_target="tpu_custom_call" | custom-call | tf_op jit(solution)/shard_map/pallas_call | solution.py:550
  38.0 16.3 %all_to_all.10.th_ref = f32[32,1,128]{2,1,0:T(1,128)S(1)} all-to-all(f32[32,1,128]{2,1,0:T(1,128)S(1)} %get-tuple-element.43), channel_id=1, replica_groups=mesh['gx'=4,'gy'=8] {'gx','gy'}, dimensions={0} | all-to-all | bytes 32768 | tf_op jit(solution)/shard_map/all_to_all | solution.py:599
  54.3 4.9 %shard_map.72 = (f32[2,24,40,256]{3,2,1,0:T(8,128)S(1)}, f32[2,24,40,256]{3,2,1,0:T(8,128)S(1)}, f32[2,24,40,256]{3,2,1,0:T(8,128)S(1)}, f32[2,24,40,256]{3,2,1,...) custom-call(f32[32,1,128]{2,1,0:T(1,128)S(1)} %all_to_all.10.th_ref,, ...), custom_call_target="tpu_custom_call", output_to_operand_aliasing={{0}: (5, {}), {1}: (6, {}), {2}: (7, {}), {3}: (8, {})} | custom-call | tf_op jit(solution)/shard_map/pallas_call | solution.py:550
  59.3 3.4 %shard_map.73 = (f32[2,24,40,256]{3,2,1,0:T(8,128)S(1)}, f32[2,24,40,256]{3,2,1,0:T(8,128)S(1)}, f32[2,24,40,256]{3,2,1,0:T(8,128)S(1)}, f32[2,24,40,256]{3,2,1,...) custom-call(f32[32,1,128]{2,1,0:T(1,128)S(1)} %all_to_all.10.th_ref,, ...), custom_call_target="tpu_custom_call", output_to_operand_aliasing={{0}: (3, {}), {1}: (4, {}), {2}: (5, {}), {3}: (6, {}), {4}... | custom-call | tf_op jit(solution)/shard_map/pallas_call | solution.py:550
  62.7 2.5 %collective-permute-start.6 = (f32[16,8,256]{2,1,0:T(8,128)S(1)}, f32[16,8,256]{2,1,0:T(8,128)S(1)}, u32[]{:S(2)}, u32[]{:S(2)}) collective-permute-start(f32[16,8,256]{2,1,0:T(8,128)S(1)} %get-tuple-element.64), channel_id=1, source_target_pairs={{0,1},{1,2},{2,3},{3,4},{4,5},{5,6},{6,7},{8,9},{9,10},{10,11},{11... | collective-permute-start | bytes 393224 | tf_op jit(solution)/shard_map/ppermute | solution.py:576
  65.2 1.3 %collective-permute-start.7 = (f32[16,8,256]{2,1,0:T(8,128)S(1)}, f32[16,8,256]{2,1,0:T(8,128)S(1)}, u32[]{:S(2)}, u32[]{:S(2)}) collective-permute-start(f32[16,8,256]{2,1,0:T(8,128)S(1)} %get-tuple-element.65), channel_id=1, source_target_pairs={{1,0},{2,1},{3,2},{4,3},{5,4},{6,5},{7,6},{9,8},{10,9},{11,10},{12... | collective-permute-start | bytes 393224 | tf_op jit(solution)/shard_map/ppermute | solution.py:576
  68.0 4.1 %collective-permute-done.7.yr_ref = f32[16,8,256]{2,1,0:T(8,128)S(1)} collective-permute-done((f32[16,8,256]{2,1,0:T(8,128)S(1)}, f32[16,8,256]{2,1,0:T(8,128)S(1)}, u32[]{:S(2)}, u32[]{:S(2)}) %collective-permute-start.7) | collective-permute-done | bytes 131104 | tf_op jit(solution)/shard_map/ppermute | solution.py:576
  72.2 1.3 %collective-permute-start.8 = (f32[2,4,40,256]{3,2,1,0:T(8,128)S(1)}, f32[2,4,40,256]{3,2,1,0:T(8,128)S(1)}, u32[]{:S(2)}, u32[]{:S(2)}) collective-permute-start(f32[2,4,40,256]{3,2,1,0:T(8,128)S(1)} %get-tuple-element.66), channel_id=1, source_target_pairs={{0,8},{8,16},{16,24},{1,9},{9,17},{17,25},{2,10},{10,18},{18,26},{... | collective-permute-start | bytes 983048 | tf_op jit(solution)/shard_map/ppermute | solution.py:576
  73.5 1.3 %collective-permute-start.9 = (f32[2,4,40,256]{3,2,1,0:T(8,128)S(1)}, f32[2,4,40,256]{3,2,1,0:T(8,128)S(1)}, u32[]{:S(2)}, u32[]{:S(2)}) collective-permute-start(f32[2,4,40,256]{3,2,1,0:T(8,128)S(1)} %get-tuple-element.67), channel_id=1, source_target_pairs={{8,0},{16,8},{24,16},{9,1},{17,9},{25,17},{10,2},{18,10},{26,18},{... | collective-permute-start | bytes 983048 | tf_op jit(solution)/shard_map/ppermute | solution.py:576
  74.8 4.7 %shard_map.76 = (f32[2,24,40,256]{3,2,1,0:T(8,128)S(1)}, f32[2,24,40,256]{3,2,1,0:T(8,128)S(1)}, f32[2,24,40,256]{3,2,1,0:T(8,128)S(1)}, f32[2,24,40,256]{3,2,1,0:T(8,128)S(1)}, f32[2,24,40,256]{3,2,1,0:T(8,128)S(1)}) custom-call(f32[32,1,128]{2,1,0:T(1,128)S(1)} %all_to_all.10.th_ref, f32[2,24,40,256]{3,2,1,0:T(8,128)S(1)} %get-tuple-element.68.p_ref, ...), custom_call_target="tpu_custom_call" | custom-call | tf_op jit(solution)/shard_map/pallas_call | solution.py:550
  79.6 4.8 %shard_map.77 = (f32[2,24,40,256]{3,2,1,0:T(8,128)S(1)}, f32[2,24,40,256]{3,2,1,0:T(8,128)S(1)}, f32[2,24,40,256]{3,2,1,0:T(8,128)S(1)}, f32[2,24,40,256]{3,2,1,...) custom-call(f32[32,1,128]{2,1,0:T(1,128)S(1)} %all_to_all.10.th_ref,, ...), custom_call_target="tpu_custom_call", output_to_operand_aliasing={{0}: (9, {}), {1}: (10, {}), {2}: (11, {}), {3}: (12, {}), ... | custom-call | tf_op jit(solution)/shard_map/pallas_call | solution.py:550
  84.4 12.9 %all_to_all.11.g_ref = f32[32,1,128]{2,1,0:T(1,128)S(1)} all-to-all(f32[32,1,128]{2,1,0:T(1,128)S(1)} %get-tuple-element.76), channel_id=1, replica_groups=mesh['gx'=4,'gy'=8] {'gx','gy'}, dimensions={0} | all-to-all | bytes 32768 | tf_op jit(solution)/shard_map/all_to_all | solution.py:620
  97.3 2.9 %shard_map.78 = (f32[2,16,32,256]{3,2,1,0:T(8,128)}, f32[2,16,32,256]{3,2,1,0:T(8,128)}) custom-call(f32[32,1,128]{2,1,0:T(1,128)S(1)} %all_to_all.10.th_ref, f32[32,1,128]{2,1,0:T(1,128)S(1)} %all_to_all.11.g_ref, f32[2,16,32,256]{3,2,1,0:T(8,128)S(1)} %copy-done.1, f32[16,32,256]{2,1,0:T(8,128)S(1)} %copy-done.4, f32[16,32,256]{2,1,0:T(8,128)S(1)} %copy-done.3, ...), custom_call_target="tpu_custom_call" | custom-call | tf_op jit(solution)/shard_map/pallas_call | solution.py:550
  (23 shorter events, 4.1 us)
Async XLA Ops:
  0.6 1.2 %copy-start = (f32[2,16,32,256]{3,2,1,0:T(8,128)S(1)}, f32[2,16,32,256]{3,2,1,0:T(8,128)}, u32[]{:S(2)}) copy-start(f32[2,16,32,256]{3,2,1,0:T(8,128)} %b_ref.11) | copy-start | bytes 3145732
  1.9 1.0 %copy-start.2 = (f32[16,32,256]{2,1,0:T(8,128)S(1)}, f32[16,32,256]{2,1,0:T(8,128)}, u32[]{:S(2)}) copy-start(f32[16,32,256]{2,1,0:T(8,128)} %ct_ref.11) | copy-start | bytes 1572868
  2.9 1.0 %copy-start.4 = (f32[16,32,256]{2,1,0:T(8,128)S(1)}, f32[16,32,256]{2,1,0:T(8,128)}, u32[]{:S(2)}) copy-start(f32[16,32,256]{2,1,0:T(8,128)} %cf_ref.7) | copy-start | bytes 1572868
  3.9 1.0 %copy-start.5 = (f32[16,32,256]{2,1,0:T(8,128)S(1)}, f32[16,32,256]{2,1,0:T(8,128)}, u32[]{:S(2)}) copy-start(f32[16,32,256]{2,1,0:T(8,128)} %mr_ref.5) | copy-start | bytes 1572868
  5.0 1.0 %copy-start.6 = (f32[16,32,256]{2,1,0:T(8,128)S(1)}, f32[16,32,256]{2,1,0:T(8,128)}, u32[]{:S(2)}) copy-start(f32[16,32,256]{2,1,0:T(8,128)} %d_ref.5) | copy-start | bytes 1572868
  6.5 28.0 %copy-start.1 = (f32[2,16,32,256]{3,2,1,0:T(8,128)S(1)}, f32[2,16,32,256]{3,2,1,0:T(8,128)}, u32[]{:S(2)}) copy-start(f32[2,16,32,256]{3,2,1,0:T(8,128)} %b_ref.11) | copy-start | bytes 3145732
  8.1 46.3 %collective-permute-start.4 = (f32[5,4,32,256]{3,2,1,0:T(8,128)S(1)}, f32[5,4,32,256]{3,2,1,0:T(8,128)S(1)}, u32[]{:S(2)}, u32[]{:S(2)}) collective-permute-start(f32[5,4,32,256]{3,2,1,0:T(8,128)S(1)} %get-tuple-element.48), channel_id=1, source_target_pairs={{0,8},{8,16},{16,24},{1,9},{9,17},{17,25},{2,10},{10,18},{18,26},{... | collective-permute-start | bytes 1966088 | tf_op jit(solution)/shard_map/ppermute | solution.py:576
  10.5 43.9 %collective-permute-start.5 = (f32[5,4,32,256]{3,2,1,0:T(8,128)S(1)}, f32[5,4,32,256]{3,2,1,0:T(8,128)S(1)}, u32[]{:S(2)}, u32[]{:S(2)}) collective-permute-start(f32[5,4,32,256]{3,2,1,0:T(8,128)S(1)} %get-tuple-element.49), channel_id=1, source_target_pairs={{8,0},{16,8},{24,16},{9,1},{17,9},{25,17},{10,2},{18,10},{26,18},{... | collective-permute-start | bytes 1966088 | tf_op jit(solution)/shard_map/ppermute | solution.py:576
  11.8 17.9 %collective-permute-start = (f32[40,8,256]{2,1,0:T(8,128)S(1)}, f32[40,8,256]{2,1,0:T(8,128)S(1)}, u32[]{:S(2)}, u32[]{:S(2)}) collective-permute-start(f32[40,8,256]{2,1,0:T(8,128)S(1)} %get-tuple-element.44), channel_id=1, source_target_pairs={{0,1},{1,2},{2,3},{3,4},{4,5},{5,6},{6,7},{8,9},{9,10},{10,11},{11... | collective-permute-start | bytes 983048 | tf_op jit(solution)/shard_map/ppermute | solution.py:576
  16.0 13.6 %collective-permute-start.1 = (f32[40,8,256]{2,1,0:T(8,128)S(1)}, f32[40,8,256]{2,1,0:T(8,128)S(1)}, u32[]{:S(2)}, u32[]{:S(2)}) collective-permute-start(f32[40,8,256]{2,1,0:T(8,128)S(1)} %get-tuple-element.45.after_ref), channel_id=1, source_target_pairs={{1,0},{2,1},{3,2},{4,3},{5,4},{6,5},{7,6},{9,8},{10,9},{11,10},{12... | collective-permute-start | bytes 983048 | tf_op jit(solution)/shard_map/ppermute | solution.py:576
  29.7 29.6 %collective-permute-start.2 = (f32[2,10,8,256]{3,2,1,0:T(8,128)S(1)}, f32[2,10,8,256]{3,2,1,0:T(8,128)S(1)}, u32[]{:S(2)}, u32[]{:S(2)}) collective-permute-start(f32[2,10,8,256]{3,2,1,0:T(8,128)S(1)} %get-tuple-element.46), channel_id=1, source_target_pairs={{0,8},{8,16},{16,24},{1,9},{9,17},{17,25},{2,10},{10,18},{18,26},{... | collective-permute-start | bytes 491528 | tf_op jit(solution)/shard_map/ppermute | solution.py:576
  33.2 26.1 %collective-permute-start.3 = (f32[2,10,8,256]{3,2,1,0:T(8,128)S(1)}, f32[2,10,8,256]{3,2,1,0:T(8,128)S(1)}, u32[]{:S(2)}, u32[]{:S(2)}) collective-permute-start(f32[2,10,8,256]{3,2,1,0:T(8,128)S(1)} %get-tuple-element.47), channel_id=1, source_target_pairs={{8,0},{16,8},{24,16},{9,1},{17,9},{25,17},{10,2},{18,10},{26,18},{... | collective-permute-start | bytes 491528 | tf_op jit(solution)/shard_map/ppermute | solution.py:576
  62.7 5.3 %collective-permute-start.6 = (f32[16,8,256]{2,1,0:T(8,128)S(1)}, f32[16,8,256]{2,1,0:T(8,128)S(1)}, u32[]{:S(2)}, u32[]{:S(2)}) collective-permute-start(f32[16,8,256]{2,1,0:T(8,128)S(1)} %get-tuple-element.64), channel_id=1, source_target_pairs={{0,1},{1,2},{2,3},{3,4},{4,5},{5,6},{6,7},{8,9},{9,10},{10,11},{11... | collective-permute-start | bytes 393224 | tf_op jit(solution)/shard_map/ppermute | solution.py:576
  65.2 6.9 %collective-permute-start.7 = (f32[16,8,256]{2,1,0:T(8,128)S(1)}, f32[16,8,256]{2,1,0:T(8,128)S(1)}, u32[]{:S(2)}, u32[]{:S(2)}) collective-permute-start(f32[16,8,256]{2,1,0:T(8,128)S(1)} %get-tuple-element.65), channel_id=1, source_target_pairs={{1,0},{2,1},{3,2},{4,3},{5,4},{6,5},{7,6},{9,8},{10,9},{11,10},{12... | collective-permute-start | bytes 393224 | tf_op jit(solution)/shard_map/ppermute | solution.py:576
  72.2 7.3 %collective-permute-start.8 = (f32[2,4,40,256]{3,2,1,0:T(8,128)S(1)}, f32[2,4,40,256]{3,2,1,0:T(8,128)S(1)}, u32[]{:S(2)}, u32[]{:S(2)}) collective-permute-start(f32[2,4,40,256]{3,2,1,0:T(8,128)S(1)} %get-tuple-element.66), channel_id=1, source_target_pairs={{0,8},{8,16},{16,24},{1,9},{9,17},{17,25},{2,10},{10,18},{18,26},{... | collective-permute-start | bytes 983048 | tf_op jit(solution)/shard_map/ppermute | solution.py:576
  73.5 6.0 %collective-permute-start.9 = (f32[2,4,40,256]{3,2,1,0:T(8,128)S(1)}, f32[2,4,40,256]{3,2,1,0:T(8,128)S(1)}, u32[]{:S(2)}, u32[]{:S(2)}) collective-permute-start(f32[2,4,40,256]{3,2,1,0:T(8,128)S(1)} %get-tuple-element.67), channel_id=1, source_target_pairs={{8,0},{16,8},{24,16},{9,1},{17,9},{25,17},{10,2},{18,10},{26,18},{... | collective-permute-start | bytes 983048 | tf_op jit(solution)/shard_map/ppermute | solution.py:576
  74.8 4.8 %copy-start.3 = (f32[16,32,256]{2,1,0:T(8,128)S(1)}, f32[16,32,256]{2,1,0:T(8,128)}, u32[]{:S(2)}) copy-start(f32[16,32,256]{2,1,0:T(8,128)} %ct_ref.11) | copy-start | bytes 1572868

commit v4 on v3

--- a/solution.py
+++ b/solution.py
@@ -270,7 +270,7 @@
         lax.fori_loop(0, nx // 2, body, 0, unroll=2)
 
 
-def planes_kernel(after_ref, b_ref, cf_ref, ct_ref, mr_ref, d_ref, lo_ref, hi_ref, *scratch):
+def planes_kernel(b_ref, cf_ref, ct_ref, mr_ref, d_ref, lo_ref, hi_ref, *scratch):
     blocks, coefs, sems = scratch
     nx, ny, _ = cf_ref.shape
     pairs = []
@@ -287,7 +287,7 @@
                 out_ref[f, i] = value
 
 
-def corners_kernel(yl_ref, yr_ref, lo_ref, hi_ref):
+def corners_kernel(after_ref, yl_ref, yr_ref, lo_ref, hi_ref):
     count = yl_ref.shape[0]
     nx = count * 2 // 5
     for k, ref in enumerate((yl_ref, yr_ref)):
@@ -311,8 +311,14 @@
         v_ref[part, plane, rows] = v[part]
 
 
-def own_kernel(b_ref, cf_ref, ct_ref, mr_ref, d_ref, p_ref, n_ref, u_ref, v_ref, out_ref, w_ref):
+def own_kernel(
+    b_any, cf_any, ct_any, mr_any, d_any,
+    p_ref, n_ref, u_ref, v_ref, out_ref, b_ref, cf_ref, ct_ref,
+    mr_ref, d_ref, w_ref, sems,
+):
     nx, ny, nz = cf_ref.shape
+    sources = (b_any, cf_any, ct_any, mr_any, d_any)
+    fetch(list(zip(sources, (b_ref, cf_ref, ct_ref, mr_ref, d_ref))), sems)
     get = own_values(b_ref, cf_ref, ct_ref, mr_ref, d_ref)
     rows, rest = pl.ds(0, ny), pl.ds(ny, 8)
     zero = jnp.zeros((8, nz), F32)
@@ -566,7 +572,7 @@
         out_specs=vmem(len(outs)),
         scratch_shapes=[pltpu.VMEM(s, F32) for s in scratch] + [pltpu.SemaphoreType.DMA((10,))],
         compiler_params=pltpu.CompilerParams(vmem_limit_bytes=LIMIT),
-    )(*args)
+    )(*(pltpu.with_memory_space_constraint(x, pltpu.HBM) for x in args))
 
 
 def both_ways(to_lower, to_upper, axis):
@@ -592,12 +598,15 @@
     )
     yl, yr = both_ways(top, bot, "gy")
     lo, hi = edge_call(
-        planes_kernel, [(5, H, ny, nz)] * 2, [(2, 2, H, ny, nz), (2, 4, H, ny, nz)], top, *inputs
+        planes_kernel, [(5, H, ny, nz)] * 2, [(2, 2, H, ny, nz), (2, 4, H, ny, nz)], *inputs
     )
     xl, xr = both_ways(lo, hi, "gx")
-    *state, th = call(own_kernel, [ext] * 4 + [(peers, 1, 128)], [ext], *inputs)
+    *state, th, b, cf, ct = edge_call(
+        own_kernel, [ext] * 4 + [(peers, 1, 128), b.shape, cf.shape, ct.shape],
+        [mr.shape, d.shape, ext], *inputs,
+    )
     th = lax.all_to_all(th, AXES, 0, 0)
-    lo, hi = call(corners_kernel, [corner] * 2, [], yl, yr)
+    lo, hi = call(corners_kernel, [corner] * 2, [], th, yl, yr)
     cl, cr = both_ways(lo, hi, "gx")
     state = call(
         sides_kernel, [ext] * 8, [], th, xl, xr, yl, yr, *state,

time: 101 us -> 86.9 us (0.86)
  waiting for transfers between devices: 17 us -> 5.87 us
  local copies, waits for them, and re-layouts: 5.4 us -> 0 us
  Pallas kernels: 27.3 us -> 30.4 us
  starting transfers between devices: 20.5 us -> 19.4 us
    ppermute x5, waiting for transfers between devices: 12.9 us -> 1.26 us  [both_ways(): lax.ppermute(to_upper, axis, up)]
    pallas_call x2 -> x3, Pallas kernels: 2.01 us -> 8.62 us  [edge_call(): pl.pallas_call(kernel, out_shape=[jax.ShapeDtypeStruct(s, F32) for s in o...]
    unnamed x14 -> x0, local copies, waits for them, and re-layouts: 5.4 us -> none
    pallas_call x9 -> x8, Pallas kernels: 25.3 us -> 21.8 us  [call(): pl.pallas_call(kernel, out_shape=[jax.ShapeDtypeStruct(s, F32) for s in o...]
    ppermute x5, starting transfers between devices: 14 us -> 13 us  [both_ways(): lax.ppermute(to_upper, axis, up)]
  transfers between devices with their start and end apart: 10 -> 10, of which waited for: 3 -> 2; matrix products, arithmetic and copies ran while one was open for 0% -> 0% of each run, Pallas kernels for 14% -> 20%
where the time goes in v4:
time: 86.9 us; the launch traced here: 86.4 us
  Pallas kernels  30.4 us (35%)
  blocking collectives  29.9 us (34%)
  starting transfers between devices  19.4 us (22%)
  waiting for transfers between devices  5.87 us (7%)
    pallas_call x8, Pallas kernels, call(): pl.pallas_call(kernel, out_shape=[jax.ShapeDtypeStruct(s, F32) for s in o...  21.8 us
    all_to_all x1, blocking collectives, local(): th = lax.all_to_all(th, AXES, 0, 0)  16.4 us
    all_to_all x1, blocking collectives, local(): gram = lax.all_to_all(gram, AXES, 0, 0)  13.5 us
    ppermute x5, starting transfers between devices, both_ways(): lax.ppermute(to_upper, axis, up)  13 us
    pallas_call x3, Pallas kernels, edge_call(): pl.pallas_call(kernel, out_shape=[jax.ShapeDtypeStruct(s, F32) for s in o...  8.62 us
    ppermute x5, starting transfers between devices, both_ways(): lax.ppermute(to_lower, axis, down)  6.46 us
    ppermute x5, waiting for transfers between devices, both_ways(): lax.ppermute(to_lower, axis, down)  4.62 us
  transfers between devices with their start and end apart: 10, of which 2 were waited for; matrix products, arithmetic and copies ran while one was open for 0% of the time, Pallas kernels for 20%

profile of v4, /device:TPU:0, one launch (start us, length us, event | category | flops | bytes accessed | tf_op | source)
XLA Modules:
  0.0 86.4 jit_solution(2356754936122896962)
XLA Ops:
  0.6 1.6 %shard_map.71 = (f32[5,4,32,256]{3,2,1,0:T(8,128)S(1)}, f32[5,4,32,256]{3,2,1,0:T(8,128)S(1)}) custom-call(f32[2,16,32,256]{3,2,1,0:T(8,128)} %b_ref.3, f32[16,32,256]{2,1,0:T(8,128)} %cf_ref.3, f32[16,32,256]{2,1,0:T(8,128)} %ct_ref.3, f32[16,32,256]{2,1,0:T(8,128)} %mr_ref.3, f32[16,32,256]{2,1,0:T(8,128)} %d_ref.3), custom_call_target="tpu_custom_call" | custom-call | tf_op jit(solution)/shard_map/pallas_call | solution.py:568
  2.2 2.4 %collective-permute-start.4 = (f32[5,4,32,256]{3,2,1,0:T(8,128)S(1)}, f32[5,4,32,256]{3,2,1,0:T(8,128)S(1)}, u32[]{:S(2)}, u32[]{:S(2)}) collective-permute-start(f32[5,4,32,256]{3,2,1,0:T(8,128)S(1)} %get-tuple-element.53), channel_id=1, source_target_pairs={{0,8},{8,16},{16,24},{1,9},{9,17},{17,25},{2,10},{10,18},{18,26},{... | collective-permute-start | bytes 1966088 | tf_op jit(solution)/shard_map/ppermute | solution.py:582
  4.6 1.3 %collective-permute-start.5 = (f32[5,4,32,256]{3,2,1,0:T(8,128)S(1)}, f32[5,4,32,256]{3,2,1,0:T(8,128)S(1)}, u32[]{:S(2)}, u32[]{:S(2)}) collective-permute-start(f32[5,4,32,256]{3,2,1,0:T(8,128)S(1)} %get-tuple-element.54), channel_id=1, source_target_pairs={{8,0},{16,8},{24,16},{9,1},{17,9},{25,17},{10,2},{18,10},{26,18},{... | collective-permute-start | bytes 1966088 | tf_op jit(solution)/shard_map/ppermute | solution.py:582
  5.9 1.6 %shard_map.69 = (f32[40,8,256]{2,1,0:T(8,128)S(1)}, f32[40,8,256]{2,1,0:T(8,128)S(1)}) custom-call(f32[2,16,32,256]{3,2,1,0:T(8,128)} %b_ref.3, f32[16,32,256]{2,1,0:T(8,128)} %cf_ref.3, f32[16,32,256]{2,1,0:T(8,128)} %ct_ref.3, f32[16,32,256]{2,1,0:T(8,128)} %mr_ref.3, f32[16,32,256]{2,1,0:T(8,128)} %d_ref.3), custom_call_target="tpu_custom_call" | custom-call | tf_op jit(solution)/shard_map/pallas_call | solution.py:568
  7.5 4.2 %collective-permute-start = (f32[40,8,256]{2,1,0:T(8,128)S(1)}, f32[40,8,256]{2,1,0:T(8,128)S(1)}, u32[]{:S(2)}, u32[]{:S(2)}) collective-permute-start(f32[40,8,256]{2,1,0:T(8,128)S(1)} %get-tuple-element.49), channel_id=1, source_target_pairs={{0,1},{1,2},{2,3},{3,4},{4,5},{5,6},{6,7},{8,9},{9,10},{10,11},{11... | collective-permute-start | bytes 983048 | tf_op jit(solution)/shard_map/ppermute | solution.py:582
  11.8 1.3 %collective-permute-start.1 = (f32[40,8,256]{2,1,0:T(8,128)S(1)}, f32[40,8,256]{2,1,0:T(8,128)S(1)}, u32[]{:S(2)}, u32[]{:S(2)}) collective-permute-start(f32[40,8,256]{2,1,0:T(8,128)S(1)} %get-tuple-element.50), channel_id=1, source_target_pairs={{1,0},{2,1},{3,2},{4,3},{5,4},{6,5},{7,6},{9,8},{10,9},{11,10},{12... | collective-permute-start | bytes 983048 | tf_op jit(solution)/shard_map/ppermute | solution.py:582
  13.1 5.4 %shard_map.68 = (f32[2,24,40,256]{3,2,1,0:T(8,128)S(1)}, f32[2,24,40,256]{3,2,1,0:T(8,128)S(1)}, f32[2,24,40,256]{3,2,1,0:T(8,128)S(1)}, f32[2,24,40,256]{3,2,1,...) custom-call(f32[2,16,32,256]{3,2,1,0:T(8,128)} %b_ref.3, ...), custom_call_target="tpu_custom_call" | custom-call | tf_op jit(solution)/shard_map/pallas_call | solution.py:568
  18.5 16.4 %all_to_all.10.after_ref.th_ref = f32[32,1,128]{2,1,0:T(1,128)S(1)} all-to-all(f32[32,1,128]{2,1,0:T(1,128)S(1)} %get-tuple-element.46), channel_id=1, replica_groups=mesh['gx'=4,'gy'=8] {'gx','gy'}, dimensions={0} | all-to-all | bytes 32768 | tf_op jit(solution)/shard_map/all_to_all | solution.py:608
  35.0 1.8 %collective-permute-start.2 = (f32[2,10,8,256]{3,2,1,0:T(8,128)S(1)}, f32[2,10,8,256]{3,2,1,0:T(8,128)S(1)}, u32[]{:S(2)}, u32[]{:S(2)}) collective-permute-start(f32[2,10,8,256]{3,2,1,0:T(8,128)S(1)} %get-tuple-element.51), channel_id=1, source_target_pairs={{0,8},{8,16},{16,24},{1,9},{9,17},{17,25},{2,10},{10,18},{18,26},{... | collective-permute-start | bytes 491528 | tf_op jit(solution)/shard_map/ppermute | solution.py:582
  36.7 1.3 %collective-permute-start.3 = (f32[2,10,8,256]{3,2,1,0:T(8,128)S(1)}, f32[2,10,8,256]{3,2,1,0:T(8,128)S(1)}, u32[]{:S(2)}, u32[]{:S(2)}) collective-permute-start(f32[2,10,8,256]{3,2,1,0:T(8,128)S(1)} %get-tuple-element.52), channel_id=1, source_target_pairs={{8,0},{16,8},{24,16},{9,1},{17,9},{25,17},{10,2},{18,10},{26,18},{... | collective-permute-start | bytes 491528 | tf_op jit(solution)/shard_map/ppermute | solution.py:582
  38.1 5.0 %shard_map.72 = (f32[2,24,40,256]{3,2,1,0:T(8,128)S(1)}, f32[2,24,40,256]{3,2,1,0:T(8,128)S(1)}, f32[2,24,40,256]{3,2,1,0:T(8,128)S(1)}, f32[2,24,40,256]{3,2,1,...) custom-call(f32[32,1,128]{2,1,0:T(1,128)S(1)} %all_to_all.10.after_r, ...), custom_call_target="tpu_custom_call", output_to_operand_aliasing={{0}: (5, {}), {1}: (6, {}), {2}: (7, {}), {3}: (8, {})} | custom-call | tf_op jit(solution)/shard_map/pallas_call | solution.py:556
  43.0 3.4 %shard_map.73 = (f32[2,24,40,256]{3,2,1,0:T(8,128)S(1)}, f32[2,24,40,256]{3,2,1,0:T(8,128)S(1)}, f32[2,24,40,256]{3,2,1,0:T(8,128)S(1)}, f32[2,24,40,256]{3,2,1,...) custom-call(f32[32,1,128]{2,1,0:T(1,128)S(1)} %all_to_all.10.after_r, ...), custom_call_target="tpu_custom_call", output_to_operand_aliasing={{0}: (3, {}), {1}: (4, {}), {2}: (5, {}), {3}: (6, {}), {4}... | custom-call | tf_op jit(solution)/shard_map/pallas_call | solution.py:556
  46.5 2.5 %collective-permute-start.6 = (f32[16,8,256]{2,1,0:T(8,128)S(1)}, f32[16,8,256]{2,1,0:T(8,128)S(1)}, u32[]{:S(2)}, u32[]{:S(2)}) collective-permute-start(f32[16,8,256]{2,1,0:T(8,128)S(1)} %get-tuple-element.69), channel_id=1, source_target_pairs={{0,1},{1,2},{2,3},{3,4},{4,5},{5,6},{6,7},{8,9},{9,10},{10,11},{11... | collective-permute-start | bytes 393224 | tf_op jit(solution)/shard_map/ppermute | solution.py:582
  49.0 1.3 %collective-permute-start.7 = (f32[16,8,256]{2,1,0:T(8,128)S(1)}, f32[16,8,256]{2,1,0:T(8,128)S(1)}, u32[]{:S(2)}, u32[]{:S(2)}) collective-permute-start(f32[16,8,256]{2,1,0:T(8,128)S(1)} %get-tuple-element.70), channel_id=1, source_target_pairs={{1,0},{2,1},{3,2},{4,3},{5,4},{6,5},{7,6},{9,8},{10,9},{11,10},{12... | collective-permute-start | bytes 393224 | tf_op jit(solution)/shard_map/ppermute | solution.py:582
  50.3 0.9 %shard_map.74.e_ref = f32[1,1,128]{2,1,0:T(1,128)S(1)} custom-call(f32[2,16,32,256]{3,2,1,0:T(8,128)S(1)} %get-tuple-element.47.b_ref, f32[16,32,256]{2,1,0:T(8,128)S(1)} %get-tuple-element.48.ct_ref, f32[2,24,40,256]{3,2,1,0:T(8,128)S(1)} %get-tuple-element.67.v1_ref, f32[2,24,40,256]{3,2,1,0:T(8,128)S(1)} %get-tuple-element.68.v2_ref._), custom_call_target="tpu_custom_call" | custom-call | tf_op jit(solution)/shard_map/pallas_call | solution.py:556
  51.1 1.2 %collective-permute-done.6.yl_ref = f32[16,8,256]{2,1,0:T(8,128)S(1)} collective-permute-done((f32[16,8,256]{2,1,0:T(8,128)S(1)}, f32[16,8,256]{2,1,0:T(8,128)S(1)}, u32[]{:S(2)}, u32[]{:S(2)}) %collective-permute-start.6) | collective-permute-done | bytes 131104 | tf_op jit(solution)/shard_map/ppermute | solution.py:582
  52.4 4.6 %collective-permute-done.7.yr_ref = f32[16,8,256]{2,1,0:T(8,128)S(1)} collective-permute-done((f32[16,8,256]{2,1,0:T(8,128)S(1)}, f32[16,8,256]{2,1,0:T(8,128)S(1)}, u32[]{:S(2)}, u32[]{:S(2)}) %collective-permute-start.7) | collective-permute-done | bytes 131104 | tf_op jit(solution)/shard_map/ppermute | solution.py:582
  57.0 0.1 shard_map.75
  57.1 2.0 %collective-permute-start.8 = (f32[2,4,40,256]{3,2,1,0:T(8,128)S(1)}, f32[2,4,40,256]{3,2,1,0:T(8,128)S(1)}, u32[]{:S(2)}, u32[]{:S(2)}) collective-permute-start(f32[2,4,40,256]{3,2,1,0:T(8,128)S(1)} %get-tuple-element.71), channel_id=1, source_target_pairs={{0,8},{8,16},{16,24},{1,9},{9,17},{17,25},{2,10},{10,18},{18,26},{... | collective-permute-start | bytes 983048 | tf_op jit(solution)/shard_map/ppermute | solution.py:582
  59.1 1.3 %collective-permute-start.9 = (f32[2,4,40,256]{3,2,1,0:T(8,128)S(1)}, f32[2,4,40,256]{3,2,1,0:T(8,128)S(1)}, u32[]{:S(2)}, u32[]{:S(2)}) collective-permute-start(f32[2,4,40,256]{3,2,1,0:T(8,128)S(1)} %get-tuple-element.72), channel_id=1, source_target_pairs={{8,0},{16,8},{24,16},{9,1},{17,9},{25,17},{10,2},{18,10},{26,18},{... | collective-permute-start | bytes 983048 | tf_op jit(solution)/shard_map/ppermute | solution.py:582
  60.4 4.7 %shard_map.76 = (f32[2,24,40,256]{3,2,1,0:T(8,128)S(1)}, f32[2,24,40,256]{3,2,1,0:T(8,128)S(1)}, f32[2,24,40,256]{3,2,1,0:T(8,128)S(1)}, f32[2,24,40,256]{3,2,1,0:T(8,128)S(1)}, f32[2,24,40,256]{3,2,1,0:T(8,128)S(1)}) custom-call(f32[32,1,128]{2,1,0:T(1,128)S(1)} %all_to_all.10.after_ref.th_ref, f32[2,24,40,256]{3,2,1,0:T(8,128)S(1)} %get-tuple-element.73.p_ref, ...), custom_call_target="tpu_custom_call" | custom-call | tf_op jit(solution)/shard_map/pallas_call | solution.py:556
  65.2 4.8 %shard_map.77 = (f32[2,24,40,256]{3,2,1,0:T(8,128)S(1)}, f32[2,24,40,256]{3,2,1,0:T(8,128)S(1)}, f32[2,24,40,256]{3,2,1,0:T(8,128)S(1)}, f32[2,24,40,256]{3,2,1,...) custom-call(f32[32,1,128]{2,1,0:T(1,128)S(1)} %all_to_all.10.after_r, ...), custom_call_target="tpu_custom_call", output_to_operand_aliasing={{0}: (9, {}), {1}: (10, {}), {2}: (11, {}), {3}: (12, {}), ... | custom-call | tf_op jit(solution)/shard_map/pallas_call | solution.py:556
  70.0 13.5 %all_to_all.11.g_ref = f32[32,1,128]{2,1,0:T(1,128)S(1)} all-to-all(f32[32,1,128]{2,1,0:T(1,128)S(1)} %get-tuple-element.81), channel_id=1, replica_groups=mesh['gx'=4,'gy'=8] {'gx','gy'}, dimensions={0} | all-to-all | bytes 32768 | tf_op jit(solution)/shard_map/all_to_all | solution.py:629
  83.5 2.9 %shard_map.78 = (f32[2,16,32,256]{3,2,1,0:T(8,128)}, f32[2,16,32,256]{3,2,1,0:T(8,128)}) custom-call(f32[32,1,128]{2,1,0:T(1,128)S(1)} %all_to_all.10.after_ref.th_ref, f32[32,1,128]{2,1,0:T(1,128)S(1)} %all_to_all.11.g_ref, f32[2,16,32,256]{3,2,1,0:T(8,128)S(1)} %get-tuple-element.47.b_ref, f32[16,32,256]{2,1,0:T(8,128)S(1)} %get-tuple-element.82.cf_ref, ...), custom_call_target="tpu_custom_call" | custom-call | tf_op jit(solution)/shard_map/pallas_call | solution.py:556
  (9 shorter events, 0.0 us)
Async XLA Ops:
  2.2 35.8 %collective-permute-start.4 = (f32[5,4,32,256]{3,2,1,0:T(8,128)S(1)}, f32[5,4,32,256]{3,2,1,0:T(8,128)S(1)}, u32[]{:S(2)}, u32[]{:S(2)}) collective-permute-start(f32[5,4,32,256]{3,2,1,0:T(8,128)S(1)} %get-tuple-element.53), channel_id=1, source_target_pairs={{0,8},{8,16},{16,24},{1,9},{9,17},{17,25},{2,10},{10,18},{18,26},{... | collective-permute-start | bytes 1966088 | tf_op jit(solution)/shard_map/ppermute | solution.py:582
  4.6 33.4 %collective-permute-start.5 = (f32[5,4,32,256]{3,2,1,0:T(8,128)S(1)}, f32[5,4,32,256]{3,2,1,0:T(8,128)S(1)}, u32[]{:S(2)}, u32[]{:S(2)}) collective-permute-start(f32[5,4,32,256]{3,2,1,0:T(8,128)S(1)} %get-tuple-element.54), channel_id=1, source_target_pairs={{8,0},{16,8},{24,16},{9,1},{17,9},{25,17},{10,2},{18,10},{26,18},{... | collective-permute-start | bytes 1966088 | tf_op jit(solution)/shard_map/ppermute | solution.py:582
  7.5 27.4 %collective-permute-start = (f32[40,8,256]{2,1,0:T(8,128)S(1)}, f32[40,8,256]{2,1,0:T(8,128)S(1)}, u32[]{:S(2)}, u32[]{:S(2)}) collective-permute-start(f32[40,8,256]{2,1,0:T(8,128)S(1)} %get-tuple-element.49), channel_id=1, source_target_pairs={{0,1},{1,2},{2,3},{3,4},{4,5},{5,6},{6,7},{8,9},{9,10},{10,11},{11... | collective-permute-start | bytes 983048 | tf_op jit(solution)/shard_map/ppermute | solution.py:582
  11.8 23.2 %collective-permute-start.1 = (f32[40,8,256]{2,1,0:T(8,128)S(1)}, f32[40,8,256]{2,1,0:T(8,128)S(1)}, u32[]{:S(2)}, u32[]{:S(2)}) collective-permute-start(f32[40,8,256]{2,1,0:T(8,128)S(1)} %get-tuple-element.50), channel_id=1, source_target_pairs={{1,0},{2,1},{3,2},{4,3},{5,4},{6,5},{7,6},{9,8},{10,9},{11,10},{12... | collective-permute-start | bytes 983048 | tf_op jit(solution)/shard_map/ppermute | solution.py:582
  35.0 8.0 %collective-permute-start.2 = (f32[2,10,8,256]{3,2,1,0:T(8,128)S(1)}, f32[2,10,8,256]{3,2,1,0:T(8,128)S(1)}, u32[]{:S(2)}, u32[]{:S(2)}) collective-permute-start(f32[2,10,8,256]{3,2,1,0:T(8,128)S(1)} %get-tuple-element.51), channel_id=1, source_target_pairs={{0,8},{8,16},{16,24},{1,9},{9,17},{17,25},{2,10},{10,18},{18,26},{... | collective-permute-start | bytes 491528 | tf_op jit(solution)/shard_map/ppermute | solution.py:582
  36.7 6.3 %collective-permute-start.3 = (f32[2,10,8,256]{3,2,1,0:T(8,128)S(1)}, f32[2,10,8,256]{3,2,1,0:T(8,128)S(1)}, u32[]{:S(2)}, u32[]{:S(2)}) collective-permute-start(f32[2,10,8,256]{3,2,1,0:T(8,128)S(1)} %get-tuple-element.52), channel_id=1, source_target_pairs={{8,0},{16,8},{24,16},{9,1},{17,9},{25,17},{10,2},{18,10},{26,18},{... | collective-permute-start | bytes 491528 | tf_op jit(solution)/shard_map/ppermute | solution.py:582
  46.5 5.9 %collective-permute-start.6 = (f32[16,8,256]{2,1,0:T(8,128)S(1)}, f32[16,8,256]{2,1,0:T(8,128)S(1)}, u32[]{:S(2)}, u32[]{:S(2)}) collective-permute-start(f32[16,8,256]{2,1,0:T(8,128)S(1)} %get-tuple-element.69), channel_id=1, source_target_pairs={{0,1},{1,2},{2,3},{3,4},{4,5},{5,6},{6,7},{8,9},{9,10},{10,11},{11... | collective-permute-start | bytes 393224 | tf_op jit(solution)/shard_map/ppermute | solution.py:582
  49.0 8.0 %collective-permute-start.7 = (f32[16,8,256]{2,1,0:T(8,128)S(1)}, f32[16,8,256]{2,1,0:T(8,128)S(1)}, u32[]{:S(2)}, u32[]{:S(2)}) collective-permute-start(f32[16,8,256]{2,1,0:T(8,128)S(1)} %get-tuple-element.70), channel_id=1, source_target_pairs={{1,0},{2,1},{3,2},{4,3},{5,4},{6,5},{7,6},{9,8},{10,9},{11,10},{12... | collective-permute-start | bytes 393224 | tf_op jit(solution)/shard_map/ppermute | solution.py:582
  57.1 8.1 %collective-permute-start.8 = (f32[2,4,40,256]{3,2,1,0:T(8,128)S(1)}, f32[2,4,40,256]{3,2,1,0:T(8,128)S(1)}, u32[]{:S(2)}, u32[]{:S(2)}) collective-permute-start(f32[2,4,40,256]{3,2,1,0:T(8,128)S(1)} %get-tuple-element.71), channel_id=1, source_target_pairs={{0,8},{8,16},{16,24},{1,9},{9,17},{17,25},{2,10},{10,18},{18,26},{... | collective-permute-start | bytes 983048 | tf_op jit(solution)/shard_map/ppermute | solution.py:582
  59.1 6.0 %collective-permute-start.9 = (f32[2,4,40,256]{3,2,1,0:T(8,128)S(1)}, f32[2,4,40,256]{3,2,1,0:T(8,128)S(1)}, u32[]{:S(2)}, u32[]{:S(2)}) collective-permute-start(f32[2,4,40,256]{3,2,1,0:T(8,128)S(1)} %get-tuple-element.72), channel_id=1, source_target_pairs={{8,0},{16,8},{24,16},{9,1},{17,9},{25,17},{10,2},{18,10},{26,18},{... | collective-permute-start | bytes 983048 | tf_op jit(solution)/shard_map/ppermute | solution.py:582

commit v5 on v4

--- a/solution.py
+++ b/solution.py
@@ -77,7 +77,7 @@
             body(i)
             return carry
 
-        lax.fori_loop(lo, hi, step, 0, unroll=2)
+        lax.fori_loop(lo, hi, step, 0, unroll=4)
 
 
 def half_step(u_ref, p_ref, w_ref, ranges):
@@ -245,35 +245,17 @@
         c.wait()
 
 
-def rows_kernel(b_ref, cf_ref, ct_ref, mr_ref, d_ref, top_ref, bot_ref, *scratch):
-    blocks, coefs, sems = scratch
+def edges_kernel(
+    b_ref, cf_ref, ct_ref, mr_ref, d_ref, lo_ref, hi_ref, top_ref, bot_ref,
+    blocks, coefs, row_blocks, row_coefs, sems,
+):
     nx, ny, _ = cf_ref.shape
     pairs = []
     for side, at in enumerate((0, ny - 8)):
         rows = pl.ds(at, 8)
-        pairs.append((b_ref.at[:, :, rows], blocks.at[side]))
+        pairs.append((b_ref.at[:, :, rows], row_blocks.at[side]))
         for k, ref in enumerate((cf_ref, ct_ref, mr_ref, d_ref)):
-            pairs.append((ref.at[:, rows], coefs.at[side, k]))
-    fetch(pairs, sems)
-    for side, out_ref in enumerate((top_ref, bot_ref)):
-        get = own_values(blocks.at[side], *(coefs.at[side, k] for k in range(4)))
-        top = side == 0
-
-        def body(j, carry):
-            a, b = get(2 * j, pl.ds(0, 8)), get(2 * j + 1, pl.ds(0, 8))
-            out_ref[2 * j] = pack_pair(a[0], a[1], top)
-            out_ref[2 * j + 1] = pack_pair(b[0], b[1], top)
-            for f in range(3):
-                out_ref[nx + f * nx // 2 + j] = pack_pair(a[2 + f], b[2 + f], top)
-            return carry
-
-        lax.fori_loop(0, nx // 2, body, 0, unroll=2)
-
-
-def planes_kernel(b_ref, cf_ref, ct_ref, mr_ref, d_ref, lo_ref, hi_ref, *scratch):
-    blocks, coefs, sems = scratch
-    nx, ny, _ = cf_ref.shape
-    pairs = []
+            pairs.append((ref.at[:, rows], row_coefs.at[side, k]))
     for side, at in enumerate((0, nx - H)):
         span = pl.ds(at, H)
         pairs.append((b_ref.at[:, span], blocks.at[side]))
@@ -285,6 +267,19 @@
         for i in range(H):
             for f, value in enumerate(get(i, pl.ds(0, ny))):
                 out_ref[f, i] = value
+    for side, out_ref in enumerate((top_ref, bot_ref)):
+        get = own_values(row_blocks.at[side], *(row_coefs.at[side, k] for k in range(4)))
+        top = side == 0
+
+        def body(j, carry):
+            a, b = get(2 * j, pl.ds(0, 8)), get(2 * j + 1, pl.ds(0, 8))
+            out_ref[2 * j] = pack_pair(a[0], a[1], top)
+            out_ref[2 * j + 1] = pack_pair(b[0], b[1], top)
+            for f in range(3):
+                out_ref[nx + f * nx // 2 + j] = pack_pair(a[2 + f], b[2 + f], top)
+            return carry
+
+        lax.fori_loop(0, nx // 2, body, 0, unroll=2)
 
 
 def corners_kernel(after_ref, yl_ref, yr_ref, lo_ref, hi_ref):
@@ -332,11 +327,11 @@
 
     loop([(0, nx)], body)
     blank = jnp.zeros((ny + 8, nz), F32)
-    for ref in (u_ref, w_ref):
-        for part in range(2):
-            ref[part, H - 1] = blank
-            ref[part, nx + H] = blank
-    half_step(u_ref, p_ref, w_ref, [(H, nx + H)])
+    for part in range(2):
+        u_ref[part, H - 1] = blank
+        w_ref[part, H - 1] = blank
+        w_ref[part, nx // 2 + H] = blank
+    half_step(u_ref, p_ref, w_ref, [(H, nx // 2 + H)])
 
     def dots(i, acc):
         acc = list(acc)
@@ -350,7 +345,7 @@
             acc[2] = acc[2] + fold(br * br + bi * bi)
         return tuple(acc)
 
-    acc = lax.fori_loop(0, nx, dots, (jnp.zeros((8, 128), F32),) * 3, unroll=2)
+    acc = lax.fori_loop(0, nx // 2, dots, (jnp.zeros((8, 128), F32),) * 3, unroll=2)
     put(pack_lanes(acc), out_ref)
 
 
@@ -570,7 +565,7 @@
         out_shape=[jax.ShapeDtypeStruct(s, F32) for s in outs],
         in_specs=[pl.BlockSpec(memory_space=pl.ANY)] * len(args),
         out_specs=vmem(len(outs)),
-        scratch_shapes=[pltpu.VMEM(s, F32) for s in scratch] + [pltpu.SemaphoreType.DMA((10,))],
+        scratch_shapes=[pltpu.VMEM(s, F32) for s in scratch] + [pltpu.SemaphoreType.DMA((20,))],
         compiler_params=pltpu.CompilerParams(vmem_limit_bytes=LIMIT),
     )(*(pltpu.with_memory_space_constraint(x, pltpu.HBM) for x in args))
 
@@ -593,13 +588,11 @@
     corner = (2, H + 3 * H // 2, 8, nz)
     inputs = (b, cf, ct, mr, d)
 
-    top, bot = edge_call(
-        rows_kernel, [rim, rim], [(2, 2, nx, 8, nz), (2, 4, nx, 8, nz)], *inputs
+    lo, hi, top, bot = edge_call(
+        edges_kernel, [(5, H, ny, nz)] * 2 + [rim, rim],
+        [(2, 2, H, ny, nz), (2, 4, H, ny, nz), (2, 2, nx, 8, nz), (2, 4, nx, 8, nz)], *inputs
     )
     yl, yr = both_ways(top, bot, "gy")
-    lo, hi = edge_call(
-        planes_kernel, [(5, H, ny, nz)] * 2, [(2, 2, H, ny, nz), (2, 4, H, ny, nz)], *inputs
-    )
     xl, xr = both_ways(lo, hi, "gx")
     *state, th, b, cf, ct = edge_call(
         own_kernel, [ext] * 4 + [(peers, 1, 128), b.shape, cf.shape, ct.shape],

time: 86.9 us -> 82.3 us (0.947)
  Pallas kernels: 30.4 us -> 25.4 us
    pallas_call x8, Pallas kernels: 21.8 us -> 19.2 us  [call(): pl.pallas_call(kernel, out_shape=[jax.ShapeDtypeStruct(s, F32) for s in o...]
    pallas_call x3 -> x2, Pallas kernels: 8.62 us -> 6.19 us  [edge_call(): pl.pallas_call(kernel, out_shape=[jax.ShapeDtypeStruct(s, F32) for s in o...]
  transfers between devices with their start and end apart: 10 -> 10, of which waited for: 2 -> 2; matrix products, arithmetic and copies ran while one was open for 0% -> 0% of each run, Pallas kernels for 20% -> 16%
where the time goes in v5:
time: 82.3 us; the launch traced here: 81.9 us
  blocking collectives  30.5 us (37%)
  Pallas kernels  25.4 us (31%)
  starting transfers between devices  19.5 us (24%)
  waiting for transfers between devices  5.74 us (7%)
    pallas_call x8, Pallas kernels, call(): pl.pallas_call(kernel, out_shape=[jax.ShapeDtypeStruct(s, F32) for s in o...  19.2 us
    all_to_all x1, blocking collectives, local(): th = lax.all_to_all(th, AXES, 0, 0)  16.4 us
    all_to_all x1, blocking collectives, local(): gram = lax.all_to_all(gram, AXES, 0, 0)  14.1 us
    ppermute x5, starting transfers between devices, both_ways(): lax.ppermute(to_upper, axis, up)  13 us
    ppermute x5, starting transfers between devices, both_ways(): lax.ppermute(to_lower, axis, down)  6.46 us
    pallas_call x2, Pallas kernels, edge_call(): pl.pallas_call(kernel, out_shape=[jax.ShapeDtypeStruct(s, F32) for s in o...  6.19 us
    ppermute x5, waiting for transfers between devices, both_ways(): lax.ppermute(to_lower, axis, down)  4.73 us
  transfers between devices with their start and end apart: 10, of which 2 were waited for; matrix products, arithmetic and copies ran while one was open for 0% of the time, Pallas kernels for 16%

profile of v5, /device:TPU:0, one launch (start us, length us, event | category | flops | bytes accessed | tf_op | source)
XLA Modules:
  0.0 81.9 jit_solution(535116750841130874)
XLA Ops:
  0.6 2.3 %shard_map.69 = (f32[5,4,32,256]{3,2,1,0:T(8,128)S(1)}, f32[5,4,32,256]{3,2,1,0:T(8,128)S(1)}, f32[40,8,256]{2,1,0:T(8,128)S(1)}, f32[40,8,256]{2,1,0:T(8,128)S(1)}) custom-call(f32[2,16,32,256]{3,2,1,0:T(8,128)} %b_ref.1, f32[16,32,256]{2,1,0:T(8,128)} %cf_ref.1, f32[16,32,256]{2,1,0:T(8,128)} %ct_ref.1, f32[16,32,256]{2,1,0:T(8,128)} %mr_ref.1, ...), custom_call_target="tpu_custom_call" | custom-call | tf_op jit(solution)/shard_map/pallas_call | solution.py:563
  2.9 2.4 %collective-permute-start.4 = (f32[5,4,32,256]{3,2,1,0:T(8,128)S(1)}, f32[5,4,32,256]{3,2,1,0:T(8,128)S(1)}, u32[]{:S(2)}, u32[]{:S(2)}) collective-permute-start(f32[5,4,32,256]{3,2,1,0:T(8,128)S(1)} %get-tuple-element.53), channel_id=1, source_target_pairs={{0,8},{8,16},{16,24},{1,9},{9,17},{17,25},{2,10},{10,18},{18,26},{... | collective-permute-start | bytes 1966088 | tf_op jit(solution)/shard_map/ppermute | solution.py:577
  5.3 1.3 %collective-permute-start.5 = (f32[5,4,32,256]{3,2,1,0:T(8,128)S(1)}, f32[5,4,32,256]{3,2,1,0:T(8,128)S(1)}, u32[]{:S(2)}, u32[]{:S(2)}) collective-permute-start(f32[5,4,32,256]{3,2,1,0:T(8,128)S(1)} %get-tuple-element.54), channel_id=1, source_target_pairs={{8,0},{16,8},{24,16},{9,1},{17,9},{25,17},{10,2},{18,10},{26,18},{... | collective-permute-start | bytes 1966088 | tf_op jit(solution)/shard_map/ppermute | solution.py:577
  6.6 4.2 %collective-permute-start = (f32[40,8,256]{2,1,0:T(8,128)S(1)}, f32[40,8,256]{2,1,0:T(8,128)S(1)}, u32[]{:S(2)}, u32[]{:S(2)}) collective-permute-start(f32[40,8,256]{2,1,0:T(8,128)S(1)} %get-tuple-element.49), channel_id=1, source_target_pairs={{0,1},{1,2},{2,3},{3,4},{4,5},{5,6},{6,7},{8,9},{9,10},{10,11},{11... | collective-permute-start | bytes 983048 | tf_op jit(solution)/shard_map/ppermute | solution.py:577
  10.9 1.3 %collective-permute-start.1 = (f32[40,8,256]{2,1,0:T(8,128)S(1)}, f32[40,8,256]{2,1,0:T(8,128)S(1)}, u32[]{:S(2)}, u32[]{:S(2)}) collective-permute-start(f32[40,8,256]{2,1,0:T(8,128)S(1)} %get-tuple-element.50), channel_id=1, source_target_pairs={{1,0},{2,1},{3,2},{4,3},{5,4},{6,5},{7,6},{9,8},{10,9},{11,10},{12... | collective-permute-start | bytes 983048 | tf_op jit(solution)/shard_map/ppermute | solution.py:577
  12.2 3.9 %shard_map.68 = (f32[2,24,40,256]{3,2,1,0:T(8,128)S(1)}, f32[2,24,40,256]{3,2,1,0:T(8,128)S(1)}, f32[2,24,40,256]{3,2,1,0:T(8,128)S(1)}, f32[2,24,40,256]{3,2,1,...) custom-call(f32[2,16,32,256]{3,2,1,0:T(8,128)} %b_ref.1, ...), custom_call_target="tpu_custom_call" | custom-call | tf_op jit(solution)/shard_map/pallas_call | solution.py:563
  16.1 16.4 %all_to_all.10.after_ref.th_ref = f32[32,1,128]{2,1,0:T(1,128)S(1)} all-to-all(f32[32,1,128]{2,1,0:T(1,128)S(1)} %get-tuple-element.46), channel_id=1, replica_groups=mesh['gx'=4,'gy'=8] {'gx','gy'}, dimensions={0} | all-to-all | bytes 32768 | tf_op jit(solution)/shard_map/all_to_all | solution.py:601
  32.5 1.8 %collective-permute-start.2 = (f32[2,10,8,256]{3,2,1,0:T(8,128)S(1)}, f32[2,10,8,256]{3,2,1,0:T(8,128)S(1)}, u32[]{:S(2)}, u32[]{:S(2)}) collective-permute-start(f32[2,10,8,256]{3,2,1,0:T(8,128)S(1)} %get-tuple-element.51), channel_id=1, source_target_pairs={{0,8},{8,16},{16,24},{1,9},{9,17},{17,25},{2,10},{10,18},{18,26},{... | collective-permute-start | bytes 491528 | tf_op jit(solution)/shard_map/ppermute | solution.py:577
  34.3 1.3 %collective-permute-start.3 = (f32[2,10,8,256]{3,2,1,0:T(8,128)S(1)}, f32[2,10,8,256]{3,2,1,0:T(8,128)S(1)}, u32[]{:S(2)}, u32[]{:S(2)}) collective-permute-start(f32[2,10,8,256]{3,2,1,0:T(8,128)S(1)} %get-tuple-element.52), channel_id=1, source_target_pairs={{8,0},{16,8},{24,16},{9,1},{17,9},{25,17},{10,2},{18,10},{26,18},{... | collective-permute-start | bytes 491528 | tf_op jit(solution)/shard_map/ppermute | solution.py:577
  35.6 0.0 collective-permute-done.4.xl_ref
  35.6 4.4 %shard_map.71 = (f32[2,24,40,256]{3,2,1,0:T(8,128)S(1)}, f32[2,24,40,256]{3,2,1,0:T(8,128)S(1)}, f32[2,24,40,256]{3,2,1,0:T(8,128)S(1)}, f32[2,24,40,256]{3,2,1,...) custom-call(f32[32,1,128]{2,1,0:T(1,128)S(1)} %all_to_all.10.after_r, ...), custom_call_target="tpu_custom_call", output_to_operand_aliasing={{0}: (5, {}), {1}: (6, {}), {2}: (7, {}), {3}: (8, {})} | custom-call | tf_op jit(solution)/shard_map/pallas_call | solution.py:551
  40.1 2.6 %shard_map.72 = (f32[2,24,40,256]{3,2,1,0:T(8,128)S(1)}, f32[2,24,40,256]{3,2,1,0:T(8,128)S(1)}, f32[2,24,40,256]{3,2,1,0:T(8,128)S(1)}, f32[2,24,40,256]{3,2,1,...) custom-call(f32[32,1,128]{2,1,0:T(1,128)S(1)} %all_to_all.10.after_r, ...), custom_call_target="tpu_custom_call", output_to_operand_aliasing={{0}: (3, {}), {1}: (4, {}), {2}: (5, {}), {3}: (6, {}), {4}... | custom-call | tf_op jit(solution)/shard_map/pallas_call | solution.py:551
  42.7 2.5 %collective-permute-start.6 = (f32[16,8,256]{2,1,0:T(8,128)S(1)}, f32[16,8,256]{2,1,0:T(8,128)S(1)}, u32[]{:S(2)}, u32[]{:S(2)}) collective-permute-start(f32[16,8,256]{2,1,0:T(8,128)S(1)} %get-tuple-element.69), channel_id=1, source_target_pairs={{0,1},{1,2},{2,3},{3,4},{4,5},{5,6},{6,7},{8,9},{9,10},{10,11},{11... | collective-permute-start | bytes 393224 | tf_op jit(solution)/shard_map/ppermute | solution.py:577
  45.2 1.3 %collective-permute-start.7 = (f32[16,8,256]{2,1,0:T(8,128)S(1)}, f32[16,8,256]{2,1,0:T(8,128)S(1)}, u32[]{:S(2)}, u32[]{:S(2)}) collective-permute-start(f32[16,8,256]{2,1,0:T(8,128)S(1)} %get-tuple-element.70), channel_id=1, source_target_pairs={{1,0},{2,1},{3,2},{4,3},{5,4},{6,5},{7,6},{9,8},{10,9},{11,10},{12... | collective-permute-start | bytes 393224 | tf_op jit(solution)/shard_map/ppermute | solution.py:577
  46.5 0.9 %shard_map.73.e_ref = f32[1,1,128]{2,1,0:T(1,128)S(1)} custom-call(f32[2,16,32,256]{3,2,1,0:T(8,128)S(1)} %get-tuple-element.47.b_ref, f32[16,32,256]{2,1,0:T(8,128)S(1)} %get-tuple-element.48.ct_ref, f32[2,24,40,256]{3,2,1,0:T(8,128)S(1)} %get-tuple-element.67.v1_ref, f32[2,24,40,256]{3,2,1,0:T(8,128)S(1)} %get-tuple-element.68.v2_ref._), custom_call_target="tpu_custom_call" | custom-call | tf_op jit(solution)/shard_map/pallas_call | solution.py:551
  47.4 1.0 %collective-permute-done.6.yl_ref = f32[16,8,256]{2,1,0:T(8,128)S(1)} collective-permute-done((f32[16,8,256]{2,1,0:T(8,128)S(1)}, f32[16,8,256]{2,1,0:T(8,128)S(1)}, u32[]{:S(2)}, u32[]{:S(2)}) %collective-permute-start.6) | collective-permute-done | bytes 131104 | tf_op jit(solution)/shard_map/ppermute | solution.py:577
  48.4 4.7 %collective-permute-done.7.yr_ref = f32[16,8,256]{2,1,0:T(8,128)S(1)} collective-permute-done((f32[16,8,256]{2,1,0:T(8,128)S(1)}, f32[16,8,256]{2,1,0:T(8,128)S(1)}, u32[]{:S(2)}, u32[]{:S(2)}) %collective-permute-start.7) | collective-permute-done | bytes 131104 | tf_op jit(solution)/shard_map/ppermute | solution.py:577
  53.1 0.1 shard_map.74
  53.2 2.1 %collective-permute-start.8 = (f32[2,4,40,256]{3,2,1,0:T(8,128)S(1)}, f32[2,4,40,256]{3,2,1,0:T(8,128)S(1)}, u32[]{:S(2)}, u32[]{:S(2)}) collective-permute-start(f32[2,4,40,256]{3,2,1,0:T(8,128)S(1)} %get-tuple-element.71), channel_id=1, source_target_pairs={{0,8},{8,16},{16,24},{1,9},{9,17},{17,25},{2,10},{10,18},{18,26},{... | collective-permute-start | bytes 983048 | tf_op jit(solution)/shard_map/ppermute | solution.py:577
  55.3 1.3 %collective-permute-start.9 = (f32[2,4,40,256]{3,2,1,0:T(8,128)S(1)}, f32[2,4,40,256]{3,2,1,0:T(8,128)S(1)}, u32[]{:S(2)}, u32[]{:S(2)}) collective-permute-start(f32[2,4,40,256]{3,2,1,0:T(8,128)S(1)} %get-tuple-element.72), channel_id=1, source_target_pairs={{8,0},{16,8},{24,16},{9,1},{17,9},{25,17},{10,2},{18,10},{26,18},{... | collective-permute-start | bytes 983048 | tf_op jit(solution)/shard_map/ppermute | solution.py:577
  56.6 4.2 %shard_map.75 = (f32[2,24,40,256]{3,2,1,0:T(8,128)S(1)}, f32[2,24,40,256]{3,2,1,0:T(8,128)S(1)}, f32[2,24,40,256]{3,2,1,0:T(8,128)S(1)}, f32[2,24,40,256]{3,2,1,0:T(8,128)S(1)}, f32[2,24,40,256]{3,2,1,0:T(8,128)S(1)}) custom-call(f32[32,1,128]{2,1,0:T(1,128)S(1)} %all_to_all.10.after_ref.th_ref, f32[2,24,40,256]{3,2,1,0:T(8,128)S(1)} %get-tuple-element.73.p_ref, ...), custom_call_target="tpu_custom_call" | custom-call | tf_op jit(solution)/shard_map/pallas_call | solution.py:551
  60.8 4.1 %shard_map.76 = (f32[2,24,40,256]{3,2,1,0:T(8,128)S(1)}, f32[2,24,40,256]{3,2,1,0:T(8,128)S(1)}, f32[2,24,40,256]{3,2,1,0:T(8,128)S(1)}, f32[2,24,40,256]{3,2,1,...) custom-call(f32[32,1,128]{2,1,0:T(1,128)S(1)} %all_to_all.10.after_r, ...), custom_call_target="tpu_custom_call", output_to_operand_aliasing={{0}: (9, {}), {1}: (10, {}), {2}: (11, {}), {3}: (12, {}), ... | custom-call | tf_op jit(solution)/shard_map/pallas_call | solution.py:551
  64.9 14.1 %all_to_all.11.g_ref = f32[32,1,128]{2,1,0:T(1,128)S(1)} all-to-all(f32[32,1,128]{2,1,0:T(1,128)S(1)} %get-tuple-element.81), channel_id=1, replica_groups=mesh['gx'=4,'gy'=8] {'gx','gy'}, dimensions={0} | all-to-all | bytes 32768 | tf_op jit(solution)/shard_map/all_to_all | solution.py:622
  79.0 2.9 %shard_map.77 = (f32[2,16,32,256]{3,2,1,0:T(8,128)}, f32[2,16,32,256]{3,2,1,0:T(8,128)}) custom-call(f32[32,1,128]{2,1,0:T(1,128)S(1)} %all_to_all.10.after_ref.th_ref, f32[32,1,128]{2,1,0:T(1,128)S(1)} %all_to_all.11.g_ref, f32[2,16,32,256]{3,2,1,0:T(8,128)S(1)} %get-tuple-element.47.b_ref, f32[16,32,256]{2,1,0:T(8,128)S(1)} %get-tuple-element.82.cf_ref, ...), custom_call_target="tpu_custom_call" | custom-call | tf_op jit(solution)/shard_map/pallas_call | solution.py:551
  (8 shorter events, 0.0 us)
Async XLA Ops:
  2.9 32.7 %collective-permute-start.4 = (f32[5,4,32,256]{3,2,1,0:T(8,128)S(1)}, f32[5,4,32,256]{3,2,1,0:T(8,128)S(1)}, u32[]{:S(2)}, u32[]{:S(2)}) collective-permute-start(f32[5,4,32,256]{3,2,1,0:T(8,128)S(1)} %get-tuple-element.53), channel_id=1, source_target_pairs={{0,8},{8,16},{16,24},{1,9},{9,17},{17,25},{2,10},{10,18},{18,26},{... | collective-permute-start | bytes 1966088 | tf_op jit(solution)/shard_map/ppermute | solution.py:577
  5.3 30.3 %collective-permute-start.5 = (f32[5,4,32,256]{3,2,1,0:T(8,128)S(1)}, f32[5,4,32,256]{3,2,1,0:T(8,128)S(1)}, u32[]{:S(2)}, u32[]{:S(2)}) collective-permute-start(f32[5,4,32,256]{3,2,1,0:T(8,128)S(1)} %get-tuple-element.54), channel_id=1, source_target_pairs={{8,0},{16,8},{24,16},{9,1},{17,9},{25,17},{10,2},{18,10},{26,18},{... | collective-permute-start | bytes 1966088 | tf_op jit(solution)/shard_map/ppermute | solution.py:577
  6.6 25.9 %collective-permute-start = (f32[40,8,256]{2,1,0:T(8,128)S(1)}, f32[40,8,256]{2,1,0:T(8,128)S(1)}, u32[]{:S(2)}, u32[]{:S(2)}) collective-permute-start(f32[40,8,256]{2,1,0:T(8,128)S(1)} %get-tuple-element.49), channel_id=1, source_target_pairs={{0,1},{1,2},{2,3},{3,4},{4,5},{5,6},{6,7},{8,9},{9,10},{10,11},{11... | collective-permute-start | bytes 983048 | tf_op jit(solution)/shard_map/ppermute | solution.py:577
  10.9 21.6 %collective-permute-start.1 = (f32[40,8,256]{2,1,0:T(8,128)S(1)}, f32[40,8,256]{2,1,0:T(8,128)S(1)}, u32[]{:S(2)}, u32[]{:S(2)}) collective-permute-start(f32[40,8,256]{2,1,0:T(8,128)S(1)} %get-tuple-element.50), channel_id=1, source_target_pairs={{1,0},{2,1},{3,2},{4,3},{5,4},{6,5},{7,6},{9,8},{10,9},{11,10},{12... | collective-permute-start | bytes 983048 | tf_op jit(solution)/shard_map/ppermute | solution.py:577
  32.5 7.5 %collective-permute-start.2 = (f32[2,10,8,256]{3,2,1,0:T(8,128)S(1)}, f32[2,10,8,256]{3,2,1,0:T(8,128)S(1)}, u32[]{:S(2)}, u32[]{:S(2)}) collective-permute-start(f32[2,10,8,256]{3,2,1,0:T(8,128)S(1)} %get-tuple-element.51), channel_id=1, source_target_pairs={{0,8},{8,16},{16,24},{1,9},{9,17},{17,25},{2,10},{10,18},{18,26},{... | collective-permute-start | bytes 491528 | tf_op jit(solution)/shard_map/ppermute | solution.py:577
  34.3 5.8 %collective-permute-start.3 = (f32[2,10,8,256]{3,2,1,0:T(8,128)S(1)}, f32[2,10,8,256]{3,2,1,0:T(8,128)S(1)}, u32[]{:S(2)}, u32[]{:S(2)}) collective-permute-start(f32[2,10,8,256]{3,2,1,0:T(8,128)S(1)} %get-tuple-element.52), channel_id=1, source_target_pairs={{8,0},{16,8},{24,16},{9,1},{17,9},{25,17},{10,2},{18,10},{26,18},{... | collective-permute-start | bytes 491528 | tf_op jit(solution)/shard_map/ppermute | solution.py:577
  42.7 5.7 %collective-permute-start.6 = (f32[16,8,256]{2,1,0:T(8,128)S(1)}, f32[16,8,256]{2,1,0:T(8,128)S(1)}, u32[]{:S(2)}, u32[]{:S(2)}) collective-permute-start(f32[16,8,256]{2,1,0:T(8,128)S(1)} %get-tuple-element.69), channel_id=1, source_target_pairs={{0,1},{1,2},{2,3},{3,4},{4,5},{5,6},{6,7},{8,9},{9,10},{10,11},{11... | collective-permute-start | bytes 393224 | tf_op jit(solution)/shard_map/ppermute | solution.py:577
  45.2 7.9 %collective-permute-start.7 = (f32[16,8,256]{2,1,0:T(8,128)S(1)}, f32[16,8,256]{2,1,0:T(8,128)S(1)}, u32[]{:S(2)}, u32[]{:S(2)}) collective-permute-start(f32[16,8,256]{2,1,0:T(8,128)S(1)} %get-tuple-element.70), channel_id=1, source_target_pairs={{1,0},{2,1},{3,2},{4,3},{5,4},{6,5},{7,6},{9,8},{10,9},{11,10},{12... | collective-permute-start | bytes 393224 | tf_op jit(solution)/shard_map/ppermute | solution.py:577
  53.2 7.6 %collective-permute-start.8 = (f32[2,4,40,256]{3,2,1,0:T(8,128)S(1)}, f32[2,4,40,256]{3,2,1,0:T(8,128)S(1)}, u32[]{:S(2)}, u32[]{:S(2)}) collective-permute-start(f32[2,4,40,256]{3,2,1,0:T(8,128)S(1)} %get-tuple-element.71), channel_id=1, source_target_pairs={{0,8},{8,16},{16,24},{1,9},{9,17},{17,25},{2,10},{10,18},{18,26},{... | collective-permute-start | bytes 983048 | tf_op jit(solution)/shard_map/ppermute | solution.py:577
  55.3 5.5 %collective-permute-start.9 = (f32[2,4,40,256]{3,2,1,0:T(8,128)S(1)}, f32[2,4,40,256]{3,2,1,0:T(8,128)S(1)}, u32[]{:S(2)}, u32[]{:S(2)}) collective-permute-start(f32[2,4,40,256]{3,2,1,0:T(8,128)S(1)} %get-tuple-element.72), channel_id=1, source_target_pairs={{8,0},{16,8},{24,16},{9,1},{17,9},{25,17},{10,2},{18,10},{26,18},{... | collective-permute-start | bytes 983048 | tf_op jit(solution)/shard_map/ppermute | solution.py:577

commit v6 on v5

--- a/solution.py
+++ b/solution.py
@@ -11,6 +11,8 @@
 AXES = ("gx", "gy")
 F32 = jnp.float32
 LIMIT = 24 * 1024 * 1024
+SCALE = 160.0
+CHUNKS = 4
 FALLBACK = (0.72, -0.28)
 
 
@@ -44,19 +46,25 @@
 
 def smooth_yz(plane):
     rows, lanes = plane.shape
-    y = plane + plane + pltpu.roll(plane, 1, 0) + pltpu.roll(plane, rows - 1, 0)
-    lane = lax.broadcasted_iota(jnp.int32, plane.shape, 1)
-    up = jnp.where(lane == 0, 0.0, pltpu.roll(y, 1, 1))
-    down = jnp.where(lane == lanes - 1, 0.0, pltpu.roll(y, lanes - 1, 1))
-    return y + y + up + down
-
-
-def weighted(ref, i):
+    lane = lax.broadcasted_iota(jnp.int32, (rows, 128), 1)
+    parts = [plane[:, k : k + 128] for k in range(0, lanes, 128)]
+    parts = [x + pltpu.roll(x, rows - 1, 0) for x in parts]
+    parts = [x + pltpu.roll(x, 1, 0) for x in parts]
+    ups = [pltpu.roll(x, 1, 1) for x in parts]
+    downs = [pltpu.roll(x, 127, 1) for x in parts]
+    out = []
+    for k, x in enumerate(parts):
+        up = jnp.where(lane == 0, ups[k - 1] if k else 0.0, ups[k])
+        down = jnp.where(lane == 127, downs[k + 1] if k + 1 < len(parts) else 0.0, downs[k])
+        out.append(x + x + up + down)
+    return jnp.concatenate(out, axis=1)
+
+
+def sums(ref, i):
     out = []
     for part in range(2):
         mid = ref[part, i]
-        total = smooth_yz(ref[part, i - 1] + mid + mid + ref[part, i + 1])
-        out.append((total - 8.0 * mid) * (1.0 / 160.0))
+        out.append(smooth_yz((ref[part, i - 1] + mid) + (mid + ref[part, i + 1])))
     return tuple(out)
 
 
@@ -65,9 +73,9 @@
     mod = mr * mr + shift * shift
     den = mod * c
     inv = 1.0 / jnp.where(den == 0.0, 1.0, den)
-    k = OMEGA * c * c * inv
-    rc = mod * inv
-    return (k * mr, -(k * shift)), (rc * mr, rc * d)
+    k = (OMEGA / SCALE) * c * c * inv
+    rc = SCALE * mod * inv
+    return (k * mr, -(k * shift)), (rc * mr + 8.0, rc * d)
 
 
 def loop(ranges, body):
@@ -82,16 +90,18 @@
 
 def half_step(u_ref, p_ref, w_ref, ranges):
     def body(i):
-        pw = cmul((p_ref[0, i], p_ref[1, i]), weighted(u_ref, i))
-        w_ref[0, i] = 1.2 * u_ref[0, i] + pw[0]
-        w_ref[1, i] = 1.2 * u_ref[1, i] + pw[1]
+        u = (u_ref[0, i], u_ref[1, i])
+        s = sums(u_ref, i)
+        pw = cmul((p_ref[0, i], p_ref[1, i]), (s[0] - 8.0 * u[0], s[1] - 8.0 * u[1]))
+        w_ref[0, i] = 1.2 * u[0] + pw[0]
+        w_ref[1, i] = 1.2 * u[1] + pw[1]
 
     loop(ranges, body)
 
 
 def image(w_ref, n_ref, i):
     nw = cmul((n_ref[0, i], n_ref[1, i]), (w_ref[0, i], w_ref[1, i]))
-    return csub(nw, weighted(w_ref, i))
+    return csub(nw, sums(w_ref, i))
 
 
 def advance(w_ref, n_ref, v_ref, th, next_ref, ranges, p_ref=None, u_ref=None):
@@ -241,6 +251,10 @@
     copies = [pltpu.make_async_copy(a, b, sems.at[k]) for k, (a, b) in enumerate(pairs)]
     for c in copies:
         c.start()
+    return copies
+
+
+def wait_for(copies):
     for c in copies:
         c.wait()
 
@@ -251,22 +265,24 @@
 ):
     nx, ny, _ = cf_ref.shape
     pairs = []
+    for side, at in enumerate((0, nx - H)):
+        span = pl.ds(at, H)
+        pairs.append((b_ref.at[:, span], blocks.at[side]))
+        for k, ref in enumerate((cf_ref, ct_ref, mr_ref, d_ref)):
+            pairs.append((ref.at[span], coefs.at[side, k]))
     for side, at in enumerate((0, ny - 8)):
         rows = pl.ds(at, 8)
         pairs.append((b_ref.at[:, :, rows], row_blocks.at[side]))
         for k, ref in enumerate((cf_ref, ct_ref, mr_ref, d_ref)):
             pairs.append((ref.at[:, rows], row_coefs.at[side, k]))
-    for side, at in enumerate((0, nx - H)):
-        span = pl.ds(at, H)
-        pairs.append((b_ref.at[:, span], blocks.at[side]))
-        for k, ref in enumerate((cf_ref, ct_ref, mr_ref, d_ref)):
-            pairs.append((ref.at[span], coefs.at[side, k]))
-    fetch(pairs, sems)
+    copies = fetch(pairs, sems)
+    wait_for(copies[:10])
     for side, out_ref in enumerate((lo_ref, hi_ref)):
         get = own_values(blocks.at[side], *(coefs.at[side, k] for k in range(4)))
         for i in range(H):
             for f, value in enumerate(get(i, pl.ds(0, ny))):
                 out_ref[f, i] = value
+    wait_for(copies[10:])
     for side, out_ref in enumerate((top_ref, bot_ref)):
         get = own_values(row_blocks.at[side], *(row_coefs.at[side, k] for k in range(4)))
         top = side == 0
@@ -313,7 +329,7 @@
 ):
     nx, ny, nz = cf_ref.shape
     sources = (b_any, cf_any, ct_any, mr_any, d_any)
-    fetch(list(zip(sources, (b_ref, cf_ref, ct_ref, mr_ref, d_ref))), sems)
+    wait_for(fetch(list(zip(sources, (b_ref, cf_ref, ct_ref, mr_ref, d_ref))), sems))
     get = own_values(b_ref, cf_ref, ct_ref, mr_ref, d_ref)
     rows, rest = pl.ds(0, ny), pl.ds(ny, 8)
     zero = jnp.zeros((8, nz), F32)
@@ -512,7 +528,8 @@
 def final_kernel(
     th_ref, g_ref, b_ref, cf_ref, ct_ref,
     w0_ref, w1_ref, w2_ref, w3_ref, v1_ref, v2_ref, v3_ref, v4_ref,
-    sol_ref, res_ref,
+    sol_any, res_any,
+    sol_ref, res_ref, sems,
 ):
     nx, ny, nz = cf_ref.shape
     th = shift_from(th_ref)
@@ -531,7 +548,7 @@
             for c, ref in zip(answer, (w0_ref, w1_ref, w2_ref, w3_ref)):
                 t = cmul(c, (ref[0, i + H, rows], ref[1, i + H, rows]))
                 acc = t if acc is None else cadd(acc, t)
-            inv = 1.0 / cf_ref[i, rows]
+            inv = SCALE / cf_ref[i, rows]
             sol_ref[0, i, rows] = acc[0] * inv
             sol_ref[1, i, rows] = acc[1] * inv
             acc = None
@@ -544,7 +561,18 @@
             res_ref[1, i, rows] = acc[1] * ct + t[1]
         return carry
 
-    lax.fori_loop(0, nx, body, 0)
+    copies = []
+    for k in range(CHUNKS):
+        lo, hi = k * nx // CHUNKS, (k + 1) * nx // CHUNKS
+        lax.fori_loop(lo, hi, body, 0)
+        span = pl.ds(lo, hi - lo)
+        for a, b in ((sol_ref, sol_any), (res_ref, res_any)):
+            copies.append(
+                pltpu.make_async_copy(a.at[:, span], b.at[:, span], sems.at[len(copies)])
+            )
+            copies[-1].start()
+    for copy in copies:
+        copy.wait()
 
 
 def call(kernel, outs, scratch, *args, alias=None):
@@ -620,8 +648,16 @@
         alias={9 + k: k for k in range(6)},
     )
     gram = lax.all_to_all(gram, AXES, 0, 0)
+    args = (th, gram, b, cf, ct, w0, w1, w2, w3, v1, v2, v3, v4)
     return tuple(
-        call(final_kernel, [own, own], [], th, gram, b, cf, ct, w0, w1, w2, w3, v1, v2, v3, v4)
+        pl.pallas_call(
+            final_kernel,
+            out_shape=[jax.ShapeDtypeStruct(own, F32)] * 2,
+            in_specs=vmem(len(args)),
+            out_specs=[pl.BlockSpec(memory_space=pl.ANY)] * 2,
+            scratch_shapes=[pltpu.VMEM(own, F32)] * 2 + [pltpu.SemaphoreType.DMA((2 * CHUNKS,))],
+            compiler_params=pltpu.CompilerParams(vmem_limit_bytes=LIMIT),
+        )(*args)
     )
 
 

time: 82.3 us -> 81.1 us (0.985)
  Pallas kernels: 25.4 us -> 23.9 us
    pallas_call x8 -> x7, Pallas kernels: 19.2 us -> 15.4 us  [call(): pl.pallas_call(kernel, out_shape=[jax.ShapeDtypeStruct(s, F32) for s in o...]
    pallas_call x0 -> x1, Pallas kernels: none -> 2.49 us  [local(): pl.pallas_call(final_kernel, out_shape=[jax.ShapeDtypeStruct(own, F32)] *...]
where the time goes in v6:
time: 81.1 us; the launch traced here: 80.7 us
  blocking collectives  30.7 us (38%)
  Pallas kernels  23.9 us (29%)
  starting transfers between devices  19.7 us (24%)
  waiting for transfers between devices  5.54 us (7%)
    all_to_all x1, blocking collectives, local(): th = lax.all_to_all(th, AXES, 0, 0)  16.4 us
    pallas_call x7, Pallas kernels, call(): pl.pallas_call(kernel, out_shape=[jax.ShapeDtypeStruct(s, F32) for s in o...  15.4 us
    all_to_all x1, blocking collectives, local(): gram = lax.all_to_all(gram, AXES, 0, 0)  14.3 us
    ppermute x5, starting transfers between devices, both_ways(): lax.ppermute(to_upper, axis, up)  13.2 us
    ppermute x5, starting transfers between devices, both_ways(): lax.ppermute(to_lower, axis, down)  6.46 us
    pallas_call x2, Pallas kernels, edge_call(): pl.pallas_call(kernel, out_shape=[jax.ShapeDtypeStruct(s, F32) for s in o...  6.05 us
    ppermute x5, waiting for transfers between devices, both_ways(): lax.ppermute(to_lower, axis, down)  4.73 us
    pallas_call x1, Pallas kernels, local(): pl.pallas_call(final_kernel, out_shape=[jax.ShapeDtypeStruct(own, F32)] *...  2.49 us
  transfers between devices with their start and end apart: 10, of which 2 were waited for; matrix products, arithmetic and copies ran while one was open for 0% of the time, Pallas kernels for 16%

profile of v6, /device:TPU:0, one launch (start us, length us, event | category | flops | bytes accessed | tf_op | source)
XLA Modules:
  0.0 80.7 jit_solution(9891885248755817322)
XLA Ops:
  0.6 2.2 %shard_map.69 = (f32[5,4,32,256]{3,2,1,0:T(8,128)S(1)}, f32[5,4,32,256]{3,2,1,0:T(8,128)S(1)}, f32[40,8,256]{2,1,0:T(8,128)S(1)}, f32[40,8,256]{2,1,0:T(8,128)S(1)}) custom-call(f32[2,16,32,256]{3,2,1,0:T(8,128)} %b_ref.1, f32[16,32,256]{2,1,0:T(8,128)} %cf_ref.1, f32[16,32,256]{2,1,0:T(8,128)} %ct_ref.1, f32[16,32,256]{2,1,0:T(8,128)} %mr_ref.1, ...), custom_call_target="tpu_custom_call" | custom-call | tf_op jit(solution)/shard_map/pallas_call | solution.py:591
  2.8 2.4 %collective-permute-start.4 = (f32[5,4,32,256]{3,2,1,0:T(8,128)S(1)}, f32[5,4,32,256]{3,2,1,0:T(8,128)S(1)}, u32[]{:S(2)}, u32[]{:S(2)}) collective-permute-start(f32[5,4,32,256]{3,2,1,0:T(8,128)S(1)} %get-tuple-element.53), channel_id=1, source_target_pairs={{0,8},{8,16},{16,24},{1,9},{9,17},{17,25},{2,10},{10,18},{18,26},{... | collective-permute-start | bytes 1966088 | tf_op jit(solution)/shard_map/ppermute | solution.py:605
  5.2 1.3 %collective-permute-start.5 = (f32[5,4,32,256]{3,2,1,0:T(8,128)S(1)}, f32[5,4,32,256]{3,2,1,0:T(8,128)S(1)}, u32[]{:S(2)}, u32[]{:S(2)}) collective-permute-start(f32[5,4,32,256]{3,2,1,0:T(8,128)S(1)} %get-tuple-element.54), channel_id=1, source_target_pairs={{8,0},{16,8},{24,16},{9,1},{17,9},{25,17},{10,2},{18,10},{26,18},{... | collective-permute-start | bytes 1966088 | tf_op jit(solution)/shard_map/ppermute | solution.py:605
  6.5 4.2 %collective-permute-start = (f32[40,8,256]{2,1,0:T(8,128)S(1)}, f32[40,8,256]{2,1,0:T(8,128)S(1)}, u32[]{:S(2)}, u32[]{:S(2)}) collective-permute-start(f32[40,8,256]{2,1,0:T(8,128)S(1)} %get-tuple-element.49), channel_id=1, source_target_pairs={{0,1},{1,2},{2,3},{3,4},{4,5},{5,6},{6,7},{8,9},{9,10},{10,11},{11... | collective-permute-start | bytes 983048 | tf_op jit(solution)/shard_map/ppermute | solution.py:605
  10.8 1.3 %collective-permute-start.1 = (f32[40,8,256]{2,1,0:T(8,128)S(1)}, f32[40,8,256]{2,1,0:T(8,128)S(1)}, u32[]{:S(2)}, u32[]{:S(2)}) collective-permute-start(f32[40,8,256]{2,1,0:T(8,128)S(1)} %get-tuple-element.50), channel_id=1, source_target_pairs={{1,0},{2,1},{3,2},{4,3},{5,4},{6,5},{7,6},{9,8},{10,9},{11,10},{12... | collective-permute-start | bytes 983048 | tf_op jit(solution)/shard_map/ppermute | solution.py:605
  12.1 3.9 %shard_map.68 = (f32[2,24,40,256]{3,2,1,0:T(8,128)S(1)}, f32[2,24,40,256]{3,2,1,0:T(8,128)S(1)}, f32[2,24,40,256]{3,2,1,0:T(8,128)S(1)}, f32[2,24,40,256]{3,2,1,...) custom-call(f32[2,16,32,256]{3,2,1,0:T(8,128)} %b_ref.1, ...), custom_call_target="tpu_custom_call" | custom-call | tf_op jit(solution)/shard_map/pallas_call | solution.py:591
  16.0 16.4 %all_to_all.10.after_ref.th_ref = f32[32,1,128]{2,1,0:T(1,128)S(1)} all-to-all(f32[32,1,128]{2,1,0:T(1,128)S(1)} %get-tuple-element.46), channel_id=1, replica_groups=mesh['gx'=4,'gy'=8] {'gx','gy'}, dimensions={0} | all-to-all | bytes 32768 | tf_op jit(solution)/shard_map/all_to_all | solution.py:629
  32.4 0.0 collective-permute-done.yl_ref
  32.4 1.8 %collective-permute-start.2 = (f32[2,10,8,256]{3,2,1,0:T(8,128)S(1)}, f32[2,10,8,256]{3,2,1,0:T(8,128)S(1)}, u32[]{:S(2)}, u32[]{:S(2)}) collective-permute-start(f32[2,10,8,256]{3,2,1,0:T(8,128)S(1)} %get-tuple-element.51), channel_id=1, source_target_pairs={{0,8},{8,16},{16,24},{1,9},{9,17},{17,25},{2,10},{10,18},{18,26},{... | collective-permute-start | bytes 491528 | tf_op jit(solution)/shard_map/ppermute | solution.py:605
  34.2 1.3 %collective-permute-start.3 = (f32[2,10,8,256]{3,2,1,0:T(8,128)S(1)}, f32[2,10,8,256]{3,2,1,0:T(8,128)S(1)}, u32[]{:S(2)}, u32[]{:S(2)}) collective-permute-start(f32[2,10,8,256]{3,2,1,0:T(8,128)S(1)} %get-tuple-element.52), channel_id=1, source_target_pairs={{8,0},{16,8},{24,16},{9,1},{17,9},{25,17},{10,2},{18,10},{26,18},{... | collective-permute-start | bytes 491528 | tf_op jit(solution)/shard_map/ppermute | solution.py:605
  35.5 4.3 %shard_map.71 = (f32[2,24,40,256]{3,2,1,0:T(8,128)S(1)}, f32[2,24,40,256]{3,2,1,0:T(8,128)S(1)}, f32[2,24,40,256]{3,2,1,0:T(8,128)S(1)}, f32[2,24,40,256]{3,2,1,...) custom-call(f32[32,1,128]{2,1,0:T(1,128)S(1)} %all_to_all.10.after_r, ...), custom_call_target="tpu_custom_call", output_to_operand_aliasing={{0}: (5, {}), {1}: (6, {}), {2}: (7, {}), {3}: (8, {})} | custom-call | tf_op jit(solution)/shard_map/pallas_call | solution.py:579
  39.8 2.4 %shard_map.72 = (f32[2,24,40,256]{3,2,1,0:T(8,128)S(1)}, f32[2,24,40,256]{3,2,1,0:T(8,128)S(1)}, f32[2,24,40,256]{3,2,1,0:T(8,128)S(1)}, f32[2,24,40,256]{3,2,1,...) custom-call(f32[32,1,128]{2,1,0:T(1,128)S(1)} %all_to_all.10.after_r, ...), custom_call_target="tpu_custom_call", output_to_operand_aliasing={{0}: (3, {}), {1}: (4, {}), {2}: (5, {}), {3}: (6, {}), {4}... | custom-call | tf_op jit(solution)/shard_map/pallas_call | solution.py:579
  42.1 2.5 %collective-permute-start.6 = (f32[16,8,256]{2,1,0:T(8,128)S(1)}, f32[16,8,256]{2,1,0:T(8,128)S(1)}, u32[]{:S(2)}, u32[]{:S(2)}) collective-permute-start(f32[16,8,256]{2,1,0:T(8,128)S(1)} %get-tuple-element.69), channel_id=1, source_target_pairs={{0,1},{1,2},{2,3},{3,4},{4,5},{5,6},{6,7},{8,9},{9,10},{10,11},{11... | collective-permute-start | bytes 393224 | tf_op jit(solution)/shard_map/ppermute | solution.py:605
  44.7 1.3 %collective-permute-start.7 = (f32[16,8,256]{2,1,0:T(8,128)S(1)}, f32[16,8,256]{2,1,0:T(8,128)S(1)}, u32[]{:S(2)}, u32[]{:S(2)}) collective-permute-start(f32[16,8,256]{2,1,0:T(8,128)S(1)} %get-tuple-element.70), channel_id=1, source_target_pairs={{1,0},{2,1},{3,2},{4,3},{5,4},{6,5},{7,6},{9,8},{10,9},{11,10},{12... | collective-permute-start | bytes 393224 | tf_op jit(solution)/shard_map/ppermute | solution.py:605
  46.0 0.9 %shard_map.73.e_ref = f32[1,1,128]{2,1,0:T(1,128)S(1)} custom-call(f32[2,16,32,256]{3,2,1,0:T(8,128)S(1)} %get-tuple-element.47.b_ref, f32[16,32,256]{2,1,0:T(8,128)S(1)} %get-tuple-element.48.ct_ref, f32[2,24,40,256]{3,2,1,0:T(8,128)S(1)} %get-tuple-element.67.v1_ref, f32[2,24,40,256]{3,2,1,0:T(8,128)S(1)} %get-tuple-element.68.v2_ref._), custom_call_target="tpu_custom_call" | custom-call | tf_op jit(solution)/shard_map/pallas_call | solution.py:579
  46.8 0.8 collective-permute-done.6.yl_ref
  47.6 4.7 %collective-permute-done.7.yr_ref = f32[16,8,256]{2,1,0:T(8,128)S(1)} collective-permute-done((f32[16,8,256]{2,1,0:T(8,128)S(1)}, f32[16,8,256]{2,1,0:T(8,128)S(1)}, u32[]{:S(2)}, u32[]{:S(2)}) %collective-permute-start.7) | collective-permute-done | bytes 131104 | tf_op jit(solution)/shard_map/ppermute | solution.py:605
  52.4 0.1 shard_map.74
  52.4 2.3 %collective-permute-start.8 = (f32[2,4,40,256]{3,2,1,0:T(8,128)S(1)}, f32[2,4,40,256]{3,2,1,0:T(8,128)S(1)}, u32[]{:S(2)}, u32[]{:S(2)}) collective-permute-start(f32[2,4,40,256]{3,2,1,0:T(8,128)S(1)} %get-tuple-element.71), channel_id=1, source_target_pairs={{0,8},{8,16},{16,24},{1,9},{9,17},{17,25},{2,10},{10,18},{18,26},{... | collective-permute-start | bytes 983048 | tf_op jit(solution)/shard_map/ppermute | solution.py:605
  54.8 1.3 %collective-permute-start.9 = (f32[2,4,40,256]{3,2,1,0:T(8,128)S(1)}, f32[2,4,40,256]{3,2,1,0:T(8,128)S(1)}, u32[]{:S(2)}, u32[]{:S(2)}) collective-permute-start(f32[2,4,40,256]{3,2,1,0:T(8,128)S(1)} %get-tuple-element.72), channel_id=1, source_target_pairs={{8,0},{16,8},{24,16},{9,1},{17,9},{25,17},{10,2},{18,10},{26,18},{... | collective-permute-start | bytes 983048 | tf_op jit(solution)/shard_map/ppermute | solution.py:605
  56.1 4.0 %shard_map.75 = (f32[2,24,40,256]{3,2,1,0:T(8,128)S(1)}, f32[2,24,40,256]{3,2,1,0:T(8,128)S(1)}, f32[2,24,40,256]{3,2,1,0:T(8,128)S(1)}, f32[2,24,40,256]{3,2,1,0:T(8,128)S(1)}, f32[2,24,40,256]{3,2,1,0:T(8,128)S(1)}) custom-call(f32[32,1,128]{2,1,0:T(1,128)S(1)} %all_to_all.10.after_ref.th_ref, f32[2,24,40,256]{3,2,1,0:T(8,128)S(1)} %get-tuple-element.73.p_ref, ...), custom_call_target="tpu_custom_call" | custom-call | tf_op jit(solution)/shard_map/pallas_call | solution.py:579
  60.1 3.8 %shard_map.76 = (f32[2,24,40,256]{3,2,1,0:T(8,128)S(1)}, f32[2,24,40,256]{3,2,1,0:T(8,128)S(1)}, f32[2,24,40,256]{3,2,1,0:T(8,128)S(1)}, f32[2,24,40,256]{3,2,1,...) custom-call(f32[32,1,128]{2,1,0:T(1,128)S(1)} %all_to_all.10.after_r, ...), custom_call_target="tpu_custom_call", output_to_operand_aliasing={{0}: (9, {}), {1}: (10, {}), {2}: (11, {}), {3}: (12, {}), ... | custom-call | tf_op jit(solution)/shard_map/pallas_call | solution.py:579
  63.9 14.3 %all_to_all.11.g_ref = f32[32,1,128]{2,1,0:T(1,128)S(1)} all-to-all(f32[32,1,128]{2,1,0:T(1,128)S(1)} %get-tuple-element.81), channel_id=1, replica_groups=mesh['gx'=4,'gy'=8] {'gx','gy'}, dimensions={0} | all-to-all | bytes 32768 | tf_op jit(solution)/shard_map/all_to_all | solution.py:650
  78.2 2.5 %shard_map.77 = (f32[2,16,32,256]{3,2,1,0:T(8,128)}, f32[2,16,32,256]{3,2,1,0:T(8,128)}) custom-call(f32[32,1,128]{2,1,0:T(1,128)S(1)} %all_to_all.10.after_ref.th_ref, f32[32,1,128]{2,1,0:T(1,128)S(1)} %all_to_all.11.g_ref, f32[2,16,32,256]{3,2,1,0:T(8,128)S(1)} %get-tuple-element.47.b_ref, f32[16,32,256]{2,1,0:T(8,128)S(1)} %get-tuple-element.82.cf_ref, ...), custom_call_target="tpu_custom_call" | custom-call | tf_op jit(solution)/shard_map/pallas_call | solution.py:653
  (8 shorter events, 0.0 us)
Async XLA Ops:
  2.8 32.6 %collective-permute-start.4 = (f32[5,4,32,256]{3,2,1,0:T(8,128)S(1)}, f32[5,4,32,256]{3,2,1,0:T(8,128)S(1)}, u32[]{:S(2)}, u32[]{:S(2)}) collective-permute-start(f32[5,4,32,256]{3,2,1,0:T(8,128)S(1)} %get-tuple-element.53), channel_id=1, source_target_pairs={{0,8},{8,16},{16,24},{1,9},{9,17},{17,25},{2,10},{10,18},{18,26},{... | collective-permute-start | bytes 1966088 | tf_op jit(solution)/shard_map/ppermute | solution.py:605
  5.2 30.3 %collective-permute-start.5 = (f32[5,4,32,256]{3,2,1,0:T(8,128)S(1)}, f32[5,4,32,256]{3,2,1,0:T(8,128)S(1)}, u32[]{:S(2)}, u32[]{:S(2)}) collective-permute-start(f32[5,4,32,256]{3,2,1,0:T(8,128)S(1)} %get-tuple-element.54), channel_id=1, source_target_pairs={{8,0},{16,8},{24,16},{9,1},{17,9},{25,17},{10,2},{18,10},{26,18},{... | collective-permute-start | bytes 1966088 | tf_op jit(solution)/shard_map/ppermute | solution.py:605
  6.5 25.9 %collective-permute-start = (f32[40,8,256]{2,1,0:T(8,128)S(1)}, f32[40,8,256]{2,1,0:T(8,128)S(1)}, u32[]{:S(2)}, u32[]{:S(2)}) collective-permute-start(f32[40,8,256]{2,1,0:T(8,128)S(1)} %get-tuple-element.49), channel_id=1, source_target_pairs={{0,1},{1,2},{2,3},{3,4},{4,5},{5,6},{6,7},{8,9},{9,10},{10,11},{11... | collective-permute-start | bytes 983048 | tf_op jit(solution)/shard_map/ppermute | solution.py:605
  10.8 21.6 %collective-permute-start.1 = (f32[40,8,256]{2,1,0:T(8,128)S(1)}, f32[40,8,256]{2,1,0:T(8,128)S(1)}, u32[]{:S(2)}, u32[]{:S(2)}) collective-permute-start(f32[40,8,256]{2,1,0:T(8,128)S(1)} %get-tuple-element.50), channel_id=1, source_target_pairs={{1,0},{2,1},{3,2},{4,3},{5,4},{6,5},{7,6},{9,8},{10,9},{11,10},{12... | collective-permute-start | bytes 983048 | tf_op jit(solution)/shard_map/ppermute | solution.py:605
  32.4 7.4 %collective-permute-start.2 = (f32[2,10,8,256]{3,2,1,0:T(8,128)S(1)}, f32[2,10,8,256]{3,2,1,0:T(8,128)S(1)}, u32[]{:S(2)}, u32[]{:S(2)}) collective-permute-start(f32[2,10,8,256]{3,2,1,0:T(8,128)S(1)} %get-tuple-element.51), channel_id=1, source_target_pairs={{0,8},{8,16},{16,24},{1,9},{9,17},{17,25},{2,10},{10,18},{18,26},{... | collective-permute-start | bytes 491528 | tf_op jit(solution)/shard_map/ppermute | solution.py:605
  34.2 5.6 %collective-permute-start.3 = (f32[2,10,8,256]{3,2,1,0:T(8,128)S(1)}, f32[2,10,8,256]{3,2,1,0:T(8,128)S(1)}, u32[]{:S(2)}, u32[]{:S(2)}) collective-permute-start(f32[2,10,8,256]{3,2,1,0:T(8,128)S(1)} %get-tuple-element.52), channel_id=1, source_target_pairs={{8,0},{16,8},{24,16},{9,1},{17,9},{25,17},{10,2},{18,10},{26,18},{... | collective-permute-start | bytes 491528 | tf_op jit(solution)/shard_map/ppermute | solution.py:605
  42.1 5.5 %collective-permute-start.6 = (f32[16,8,256]{2,1,0:T(8,128)S(1)}, f32[16,8,256]{2,1,0:T(8,128)S(1)}, u32[]{:S(2)}, u32[]{:S(2)}) collective-permute-start(f32[16,8,256]{2,1,0:T(8,128)S(1)} %get-tuple-element.69), channel_id=1, source_target_pairs={{0,1},{1,2},{2,3},{3,4},{4,5},{5,6},{6,7},{8,9},{9,10},{10,11},{11... | collective-permute-start | bytes 393224 | tf_op jit(solution)/shard_map/ppermute | solution.py:605
  44.7 7.7 %collective-permute-start.7 = (f32[16,8,256]{2,1,0:T(8,128)S(1)}, f32[16,8,256]{2,1,0:T(8,128)S(1)}, u32[]{:S(2)}, u32[]{:S(2)}) collective-permute-start(f32[16,8,256]{2,1,0:T(8,128)S(1)} %get-tuple-element.70), channel_id=1, source_target_pairs={{1,0},{2,1},{3,2},{4,3},{5,4},{6,5},{7,6},{9,8},{10,9},{11,10},{12... | collective-permute-start | bytes 393224 | tf_op jit(solution)/shard_map/ppermute | solution.py:605
  52.4 7.6 %collective-permute-start.8 = (f32[2,4,40,256]{3,2,1,0:T(8,128)S(1)}, f32[2,4,40,256]{3,2,1,0:T(8,128)S(1)}, u32[]{:S(2)}, u32[]{:S(2)}) collective-permute-start(f32[2,4,40,256]{3,2,1,0:T(8,128)S(1)} %get-tuple-element.71), channel_id=1, source_target_pairs={{0,8},{8,16},{16,24},{1,9},{9,17},{17,25},{2,10},{10,18},{18,26},{... | collective-permute-start | bytes 983048 | tf_op jit(solution)/shard_map/ppermute | solution.py:605
  54.8 5.3 %collective-permute-start.9 = (f32[2,4,40,256]{3,2,1,0:T(8,128)S(1)}, f32[2,4,40,256]{3,2,1,0:T(8,128)S(1)}, u32[]{:S(2)}, u32[]{:S(2)}) collective-permute-start(f32[2,4,40,256]{3,2,1,0:T(8,128)S(1)} %get-tuple-element.72), channel_id=1, source_target_pairs={{8,0},{16,8},{24,16},{9,1},{17,9},{25,17},{10,2},{18,10},{26,18},{... | collective-permute-start | bytes 983048 | tf_op jit(solution)/shard_map/ppermute | solution.py:605

commit v7 on v6

--- a/solution.py
+++ b/solution.py
@@ -159,8 +159,8 @@
     return [(left, right) for right in rights for left in range(right + 1)]
 
 
-def gram_rows(fields, ct_ref, pairs, first=0):
-    nx, ny, _ = ct_ref.shape
+def gram_rows(fields, ct_ref, pairs, spans, first=0):
+    ny = ct_ref.shape[1]
     used = sorted({k for pair in pairs for k in pair})
     count = sum(1 if left == right else 2 for left, right in pairs)
 
@@ -184,7 +184,9 @@
                     k += 1
         return tuple(acc)
 
-    acc = lax.fori_loop(0, nx, body, (jnp.zeros((8, 128), F32),) * count)
+    acc = (jnp.zeros((8, 128), F32),) * count
+    for lo, hi in spans:
+        acc = lax.fori_loop(lo, hi, body, acc)
     return pack_lanes(acc, first)
 
 
@@ -423,7 +425,7 @@
 
 def early_kernel(b_ref, ct_ref, v1_ref, v2_ref, out_ref):
     fields = ((b_ref, 0, False), (v1_ref, H, True), (v2_ref, H, True))
-    put(gram_rows(fields, ct_ref, EARLY), out_ref)
+    put(gram_rows(fields, ct_ref, EARLY, [(0, ct_ref.shape[0])]), out_ref)
 
 
 def rows_back_kernel(yl_ref, yr_ref, _, v_ref, lo_ref, hi_ref):
@@ -441,7 +443,14 @@
             hi_ref[part, i] = v_ref[part, nx + i]
 
 
-def inner_kernel(th_ref, p_ref, n_ref, v_ref, u_ref, w2_ref, w3_ref, v3_ref, v4_ref):
+def late_fields(b_ref, *refs):
+    return ((b_ref, 0, False),) + tuple((ref, H, True) for ref in refs)
+
+
+def inner_kernel(
+    th_ref, e_ref, p_ref, n_ref, b_ref, ct_ref, v1_ref, v_ref,
+    u_ref, w2_ref, w3_ref, v3_ref, v4_ref, out_ref,
+):
     planes = p_ref.shape[1]
     th = shift_from(th_ref)
 
@@ -454,6 +463,8 @@
     two_applications(
         inside, planes, th, p_ref, n_ref, u_ref, v_ref, (w2_ref, w3_ref), (v3_ref, v4_ref)
     )
+    fields = late_fields(b_ref, v1_ref, v_ref, v3_ref, v4_ref)
+    put(e_ref[0] + gram_rows(fields, ct_ref, LATE, [(H, planes - 3 * H)], 9), out_ref)
 
 
 def second_kernel(th_ref, e_ref, xl_ref, xr_ref, p_ref, n_ref, b_ref, ct_ref, v1_ref, *refs):
@@ -470,11 +481,9 @@
     two_applications(
         outside, planes, th, p_ref, n_ref, u_ref, v2_ref, (w2_ref, w3_ref), (v3_ref, v4_ref)
     )
-    fields = (
-        (b_ref, 0, False), (v1_ref, H, True), (v2_ref, H, True), (v3_ref, H, True),
-        (v4_ref, H, True),
-    )
-    put(e_ref[0] + gram_rows(fields, ct_ref, LATE, 9), out_ref)
+    fields = late_fields(b_ref, v1_ref, v2_ref, v3_ref, v4_ref)
+    nx = planes - 2 * H
+    put(e_ref[0] + gram_rows(fields, ct_ref, LATE, [(0, H), (nx - H, nx)], 9), out_ref)
 
 
 def recurrences(th, gram):
@@ -641,7 +650,9 @@
     early = call(early_kernel, [(1, 1, 128)], [], b, ct, v1, v2)[0]
     v2, lo, hi = call(rows_back_kernel, [ext, face, face], [], yl, yr, v2, alias={2: 0})
     xl, xr = both_ways(lo, hi, "gx")
-    state = call(inner_kernel, [ext] * 5, [], th, p, n, v2)
+    *state, early = call(
+        inner_kernel, [ext] * 5 + [(1, 1, 128)], [], th, early, p, n, b, ct, v1, v2
+    )
     v2, _, w2, w3, v3, v4, gram = call(
         second_kernel, [ext] * 6 + [(peers, 1, 128)], [],
         th, early, xl, xr, p, n, b, ct, v1, v2, *state,

time: 81.1 us -> 80.4 us (level)
  transfers between devices with their start and end apart: 10 -> 10, of which waited for: 2 -> 2; matrix products, arithmetic and copies ran while one was open for 0% -> 0% of each run, Pallas kernels for 16% -> 17%
where the time goes in v7:
time: 80.4 us; the launch traced here: 80 us
  blocking collectives  29.9 us (37%)
  Pallas kernels  24 us (30%)
  starting transfers between devices  19.7 us (25%)
  waiting for transfers between devices  5.54 us (7%)
  between operations  0.81 us (1%)
    all_to_all x1, blocking collectives, local(): th = lax.all_to_all(th, AXES, 0, 0)  16.4 us
    pallas_call x7, Pallas kernels, call(): pl.pallas_call(kernel, out_shape=[jax.ShapeDtypeStruct(s, F32) for s in o...  15.5 us
    all_to_all x1, blocking collectives, local(): gram = lax.all_to_all(gram, AXES, 0, 0)  13.5 us
    ppermute x5, starting transfers between devices, both_ways(): lax.ppermute(to_upper, axis, up)  13.2 us
    ppermute x5, starting transfers between devices, both_ways(): lax.ppermute(to_lower, axis, down)  6.46 us
    pallas_call x2, Pallas kernels, edge_call(): pl.pallas_call(kernel, out_shape=[jax.ShapeDtypeStruct(s, F32) for s in o...  6.05 us
    ppermute x5, waiting for transfers between devices, both_ways(): lax.ppermute(to_lower, axis, down)  4.73 us
    pallas_call x1, Pallas kernels, local(): pl.pallas_call(final_kernel, out_shape=[jax.ShapeDtypeStruct(own, F32)] *...  2.49 us
  transfers between devices with their start and end apart: 10, of which 2 were waited for; matrix products, arithmetic and copies ran while one was open for 0% of the time, Pallas kernels for 17%

profile of v7, /device:TPU:0, one launch (start us, length us, event | category | flops | bytes accessed | tf_op | source)
XLA Modules:
  0.0 80.0 jit_solution(9030550945997148478)
XLA Ops:
  0.6 2.2 %shard_map.69 = (f32[5,4,32,256]{3,2,1,0:T(8,128)S(1)}, f32[5,4,32,256]{3,2,1,0:T(8,128)S(1)}, f32[40,8,256]{2,1,0:T(8,128)S(1)}, f32[40,8,256]{2,1,0:T(8,128)S(1)}) custom-call(f32[2,16,32,256]{3,2,1,0:T(8,128)} %b_ref.1, f32[16,32,256]{2,1,0:T(8,128)} %cf_ref.1, f32[16,32,256]{2,1,0:T(8,128)} %ct_ref.1, f32[16,32,256]{2,1,0:T(8,128)} %mr_ref.1, ...), custom_call_target="tpu_custom_call" | custom-call | tf_op jit(solution)/shard_map/pallas_call | solution.py:600
  2.8 2.4 %collective-permute-start.4 = (f32[5,4,32,256]{3,2,1,0:T(8,128)S(1)}, f32[5,4,32,256]{3,2,1,0:T(8,128)S(1)}, u32[]{:S(2)}, u32[]{:S(2)}) collective-permute-start(f32[5,4,32,256]{3,2,1,0:T(8,128)S(1)} %get-tuple-element.54), channel_id=1, source_target_pairs={{0,8},{8,16},{16,24},{1,9},{9,17},{17,25},{2,10},{10,18},{18,26},{... | collective-permute-start | bytes 1966088 | tf_op jit(solution)/shard_map/ppermute | solution.py:614
  5.2 1.3 %collective-permute-start.5 = (f32[5,4,32,256]{3,2,1,0:T(8,128)S(1)}, f32[5,4,32,256]{3,2,1,0:T(8,128)S(1)}, u32[]{:S(2)}, u32[]{:S(2)}) collective-permute-start(f32[5,4,32,256]{3,2,1,0:T(8,128)S(1)} %get-tuple-element.55), channel_id=1, source_target_pairs={{8,0},{16,8},{24,16},{9,1},{17,9},{25,17},{10,2},{18,10},{26,18},{... | collective-permute-start | bytes 1966088 | tf_op jit(solution)/shard_map/ppermute | solution.py:614
  6.5 4.2 %collective-permute-start = (f32[40,8,256]{2,1,0:T(8,128)S(1)}, f32[40,8,256]{2,1,0:T(8,128)S(1)}, u32[]{:S(2)}, u32[]{:S(2)}) collective-permute-start(f32[40,8,256]{2,1,0:T(8,128)S(1)} %get-tuple-element.50), channel_id=1, source_target_pairs={{0,1},{1,2},{2,3},{3,4},{4,5},{5,6},{6,7},{8,9},{9,10},{10,11},{11... | collective-permute-start | bytes 983048 | tf_op jit(solution)/shard_map/ppermute | solution.py:614
  10.8 1.3 %collective-permute-start.1 = (f32[40,8,256]{2,1,0:T(8,128)S(1)}, f32[40,8,256]{2,1,0:T(8,128)S(1)}, u32[]{:S(2)}, u32[]{:S(2)}) collective-permute-start(f32[40,8,256]{2,1,0:T(8,128)S(1)} %get-tuple-element.51), channel_id=1, source_target_pairs={{1,0},{2,1},{3,2},{4,3},{5,4},{6,5},{7,6},{9,8},{10,9},{11,10},{12... | collective-permute-start | bytes 983048 | tf_op jit(solution)/shard_map/ppermute | solution.py:614
  12.1 3.9 %shard_map.68 = (f32[2,24,40,256]{3,2,1,0:T(8,128)S(1)}, f32[2,24,40,256]{3,2,1,0:T(8,128)S(1)}, f32[2,24,40,256]{3,2,1,0:T(8,128)S(1)}, f32[2,24,40,256]{3,2,1,...) custom-call(f32[2,16,32,256]{3,2,1,0:T(8,128)} %b_ref.1, ...), custom_call_target="tpu_custom_call" | custom-call | tf_op jit(solution)/shard_map/pallas_call | solution.py:600
  16.0 16.4 %all_to_all.10.after_ref.th_ref = f32[32,1,128]{2,1,0:T(1,128)S(1)} all-to-all(f32[32,1,128]{2,1,0:T(1,128)S(1)} %get-tuple-element.47), channel_id=1, replica_groups=mesh['gx'=4,'gy'=8] {'gx','gy'}, dimensions={0} | all-to-all | bytes 32768 | tf_op jit(solution)/shard_map/all_to_all | solution.py:638
  32.4 0.0 collective-permute-done.1.yr_ref
  32.4 1.8 %collective-permute-start.2 = (f32[2,10,8,256]{3,2,1,0:T(8,128)S(1)}, f32[2,10,8,256]{3,2,1,0:T(8,128)S(1)}, u32[]{:S(2)}, u32[]{:S(2)}) collective-permute-start(f32[2,10,8,256]{3,2,1,0:T(8,128)S(1)} %get-tuple-element.52), channel_id=1, source_target_pairs={{0,8},{8,16},{16,24},{1,9},{9,17},{17,25},{2,10},{10,18},{18,26},{... | collective-permute-start | bytes 491528 | tf_op jit(solution)/shard_map/ppermute | solution.py:614
  34.2 1.3 %collective-permute-start.3 = (f32[2,10,8,256]{3,2,1,0:T(8,128)S(1)}, f32[2,10,8,256]{3,2,1,0:T(8,128)S(1)}, u32[]{:S(2)}, u32[]{:S(2)}) collective-permute-start(f32[2,10,8,256]{3,2,1,0:T(8,128)S(1)} %get-tuple-element.53), channel_id=1, source_target_pairs={{8,0},{16,8},{24,16},{9,1},{17,9},{25,17},{10,2},{18,10},{26,18},{... | collective-permute-start | bytes 491528 | tf_op jit(solution)/shard_map/ppermute | solution.py:614
  35.5 4.3 %shard_map.71 = (f32[2,24,40,256]{3,2,1,0:T(8,128)S(1)}, f32[2,24,40,256]{3,2,1,0:T(8,128)S(1)}, f32[2,24,40,256]{3,2,1,0:T(8,128)S(1)}, f32[2,24,40,256]{3,2,1,...) custom-call(f32[32,1,128]{2,1,0:T(1,128)S(1)} %all_to_all.10.after_r, ...), custom_call_target="tpu_custom_call", output_to_operand_aliasing={{0}: (5, {}), {1}: (6, {}), {2}: (7, {}), {3}: (8, {})} | custom-call | tf_op jit(solution)/shard_map/pallas_call | solution.py:588
  39.8 2.4 %shard_map.72 = (f32[2,24,40,256]{3,2,1,0:T(8,128)S(1)}, f32[2,24,40,256]{3,2,1,0:T(8,128)S(1)}, f32[2,24,40,256]{3,2,1,0:T(8,128)S(1)}, f32[2,24,40,256]{3,2,1,...) custom-call(f32[32,1,128]{2,1,0:T(1,128)S(1)} %all_to_all.10.after_r, ...), custom_call_target="tpu_custom_call", output_to_operand_aliasing={{0}: (3, {}), {1}: (4, {}), {2}: (5, {}), {3}: (6, {}), {4}... | custom-call | tf_op jit(solution)/shard_map/pallas_call | solution.py:588
  42.1 2.5 %collective-permute-start.6 = (f32[16,8,256]{2,1,0:T(8,128)S(1)}, f32[16,8,256]{2,1,0:T(8,128)S(1)}, u32[]{:S(2)}, u32[]{:S(2)}) collective-permute-start(f32[16,8,256]{2,1,0:T(8,128)S(1)} %get-tuple-element.72), channel_id=1, source_target_pairs={{0,1},{1,2},{2,3},{3,4},{4,5},{5,6},{6,7},{8,9},{9,10},{10,11},{11... | collective-permute-start | bytes 393224 | tf_op jit(solution)/shard_map/ppermute | solution.py:614
  44.7 1.3 %collective-permute-start.7 = (f32[16,8,256]{2,1,0:T(8,128)S(1)}, f32[16,8,256]{2,1,0:T(8,128)S(1)}, u32[]{:S(2)}, u32[]{:S(2)}) collective-permute-start(f32[16,8,256]{2,1,0:T(8,128)S(1)} %get-tuple-element.73), channel_id=1, source_target_pairs={{1,0},{2,1},{3,2},{4,3},{5,4},{6,5},{7,6},{9,8},{10,9},{11,10},{12... | collective-permute-start | bytes 393224 | tf_op jit(solution)/shard_map/ppermute | solution.py:614
  46.0 0.9 %shard_map.73.e_ref = f32[1,1,128]{2,1,0:T(1,128)S(1)} custom-call(f32[2,16,32,256]{3,2,1,0:T(8,128)S(1)} %get-tuple-element.48.b_ref, f32[16,32,256]{2,1,0:T(8,128)S(1)} %get-tuple-element.49.ct_ref, f32[2,24,40,256]{3,2,1,0:T(8,128)S(1)} %get-tuple-element.68.v1_ref, f32[2,24,40,256]{3,2,1,0:T(8,128)S(1)} %get-tuple-element.69.v2_ref._), custom_call_target="tpu_custom_call" | custom-call | tf_op jit(solution)/shard_map/pallas_call | solution.py:588
  46.8 0.8 %collective-permute-done.6.yl_ref = f32[16,8,256]{2,1,0:T(8,128)S(1)} collective-permute-done((f32[16,8,256]{2,1,0:T(8,128)S(1)}, f32[16,8,256]{2,1,0:T(8,128)S(1)}, u32[]{:S(2)}, u32[]{:S(2)}) %collective-permute-start.6) | collective-permute-done | bytes 131104 | tf_op jit(solution)/shard_map/ppermute | solution.py:614
  47.6 4.7 %collective-permute-done.7.yr_ref = f32[16,8,256]{2,1,0:T(8,128)S(1)} collective-permute-done((f32[16,8,256]{2,1,0:T(8,128)S(1)}, f32[16,8,256]{2,1,0:T(8,128)S(1)}, u32[]{:S(2)}, u32[]{:S(2)}) %collective-permute-start.7) | collective-permute-done | bytes 131104 | tf_op jit(solution)/shard_map/ppermute | solution.py:614
  52.4 0.1 shard_map.74
  52.4 2.3 %collective-permute-start.8 = (f32[2,4,40,256]{3,2,1,0:T(8,128)S(1)}, f32[2,4,40,256]{3,2,1,0:T(8,128)S(1)}, u32[]{:S(2)}, u32[]{:S(2)}) collective-permute-start(f32[2,4,40,256]{3,2,1,0:T(8,128)S(1)} %get-tuple-element.76), channel_id=1, source_target_pairs={{0,8},{8,16},{16,24},{1,9},{9,17},{17,25},{2,10},{10,18},{18,26},{... | collective-permute-start | bytes 983048 | tf_op jit(solution)/shard_map/ppermute | solution.py:614
  54.8 1.3 %collective-permute-start.9 = (f32[2,4,40,256]{3,2,1,0:T(8,128)S(1)}, f32[2,4,40,256]{3,2,1,0:T(8,128)S(1)}, u32[]{:S(2)}, u32[]{:S(2)}) collective-permute-start(f32[2,4,40,256]{3,2,1,0:T(8,128)S(1)} %get-tuple-element.77), channel_id=1, source_target_pairs={{8,0},{16,8},{24,16},{9,1},{17,9},{25,17},{10,2},{18,10},{26,18},{... | collective-permute-start | bytes 983048 | tf_op jit(solution)/shard_map/ppermute | solution.py:614
  56.1 4.7 %shard_map.75 = (f32[2,24,40,256]{3,2,1,0:T(8,128)S(1)}, f32[2,24,40,256]{3,2,1,0:T(8,128)S(1)}, f32[2,24,40,256]{3,2,1,0:T(8,128)S(1)}, f32[2,24,40,256]{3,2,1,...) custom-call(f32[32,1,128]{2,1,0:T(1,128)S(1)} %all_to_all.10.after_ref.th_ref, ...), custom_call_target="tpu_custom_call" | custom-call | tf_op jit(solution)/shard_map/pallas_call | solution.py:588
  60.9 3.1 %shard_map.76 = (f32[2,24,40,256]{3,2,1,0:T(8,128)S(1)}, f32[2,24,40,256]{3,2,1,0:T(8,128)S(1)}, f32[2,24,40,256]{3,2,1,0:T(8,128)S(1)}, f32[2,24,40,256]{3,2,1,...) custom-call(f32[32,1,128]{2,1,0:T(1,128)S(1)} %all_to_all.10.after_r, ...), custom_call_target="tpu_custom_call", output_to_operand_aliasing={{0}: (9, {}), {1}: (10, {}), {2}: (11, {}), {3}: (12, {}), ... | custom-call | tf_op jit(solution)/shard_map/pallas_call | solution.py:588
  64.0 13.5 %all_to_all.11.g_ref = f32[32,1,128]{2,1,0:T(1,128)S(1)} all-to-all(f32[32,1,128]{2,1,0:T(1,128)S(1)} %get-tuple-element.83), channel_id=1, replica_groups=mesh['gx'=4,'gy'=8] {'gx','gy'}, dimensions={0} | all-to-all | bytes 32768 | tf_op jit(solution)/shard_map/all_to_all | solution.py:661
  77.5 2.5 %shard_map.77 = (f32[2,16,32,256]{3,2,1,0:T(8,128)}, f32[2,16,32,256]{3,2,1,0:T(8,128)}) custom-call(f32[32,1,128]{2,1,0:T(1,128)S(1)} %all_to_all.10.after_ref.th_ref, f32[32,1,128]{2,1,0:T(1,128)S(1)} %all_to_all.11.g_ref, f32[2,16,32,256]{3,2,1,0:T(8,128)S(1)} %get-tuple-element.48.b_ref, f32[16,32,256]{2,1,0:T(8,128)S(1)} %get-tuple-element.84.cf_ref, ...), custom_call_target="tpu_custom_call" | custom-call | tf_op jit(solution)/shard_map/pallas_call | solution.py:664
  (8 shorter events, 0.0 us)
Async XLA Ops:
  2.8 32.7 %collective-permute-start.4 = (f32[5,4,32,256]{3,2,1,0:T(8,128)S(1)}, f32[5,4,32,256]{3,2,1,0:T(8,128)S(1)}, u32[]{:S(2)}, u32[]{:S(2)}) collective-permute-start(f32[5,4,32,256]{3,2,1,0:T(8,128)S(1)} %get-tuple-element.54), channel_id=1, source_target_pairs={{0,8},{8,16},{16,24},{1,9},{9,17},{17,25},{2,10},{10,18},{18,26},{... | collective-permute-start | bytes 1966088 | tf_op jit(solution)/shard_map/ppermute | solution.py:614
  5.2 30.3 %collective-permute-start.5 = (f32[5,4,32,256]{3,2,1,0:T(8,128)S(1)}, f32[5,4,32,256]{3,2,1,0:T(8,128)S(1)}, u32[]{:S(2)}, u32[]{:S(2)}) collective-permute-start(f32[5,4,32,256]{3,2,1,0:T(8,128)S(1)} %get-tuple-element.55), channel_id=1, source_target_pairs={{8,0},{16,8},{24,16},{9,1},{17,9},{25,17},{10,2},{18,10},{26,18},{... | collective-permute-start | bytes 1966088 | tf_op jit(solution)/shard_map/ppermute | solution.py:614
  6.5 25.9 %collective-permute-start = (f32[40,8,256]{2,1,0:T(8,128)S(1)}, f32[40,8,256]{2,1,0:T(8,128)S(1)}, u32[]{:S(2)}, u32[]{:S(2)}) collective-permute-start(f32[40,8,256]{2,1,0:T(8,128)S(1)} %get-tuple-element.50), channel_id=1, source_target_pairs={{0,1},{1,2},{2,3},{3,4},{4,5},{5,6},{6,7},{8,9},{9,10},{10,11},{11... | collective-permute-start | bytes 983048 | tf_op jit(solution)/shard_map/ppermute | solution.py:614
  10.8 21.6 %collective-permute-start.1 = (f32[40,8,256]{2,1,0:T(8,128)S(1)}, f32[40,8,256]{2,1,0:T(8,128)S(1)}, u32[]{:S(2)}, u32[]{:S(2)}) collective-permute-start(f32[40,8,256]{2,1,0:T(8,128)S(1)} %get-tuple-element.51), channel_id=1, source_target_pairs={{1,0},{2,1},{3,2},{4,3},{5,4},{6,5},{7,6},{9,8},{10,9},{11,10},{12... | collective-permute-start | bytes 983048 | tf_op jit(solution)/shard_map/ppermute | solution.py:614
  32.4 7.4 %collective-permute-start.2 = (f32[2,10,8,256]{3,2,1,0:T(8,128)S(1)}, f32[2,10,8,256]{3,2,1,0:T(8,128)S(1)}, u32[]{:S(2)}, u32[]{:S(2)}) collective-permute-start(f32[2,10,8,256]{3,2,1,0:T(8,128)S(1)} %get-tuple-element.52), channel_id=1, source_target_pairs={{0,8},{8,16},{16,24},{1,9},{9,17},{17,25},{2,10},{10,18},{18,26},{... | collective-permute-start | bytes 491528 | tf_op jit(solution)/shard_map/ppermute | solution.py:614
  34.2 5.6 %collective-permute-start.3 = (f32[2,10,8,256]{3,2,1,0:T(8,128)S(1)}, f32[2,10,8,256]{3,2,1,0:T(8,128)S(1)}, u32[]{:S(2)}, u32[]{:S(2)}) collective-permute-start(f32[2,10,8,256]{3,2,1,0:T(8,128)S(1)} %get-tuple-element.53), channel_id=1, source_target_pairs={{8,0},{16,8},{24,16},{9,1},{17,9},{25,17},{10,2},{18,10},{26,18},{... | collective-permute-start | bytes 491528 | tf_op jit(solution)/shard_map/ppermute | solution.py:614
  42.1 5.5 %collective-permute-start.6 = (f32[16,8,256]{2,1,0:T(8,128)S(1)}, f32[16,8,256]{2,1,0:T(8,128)S(1)}, u32[]{:S(2)}, u32[]{:S(2)}) collective-permute-start(f32[16,8,256]{2,1,0:T(8,128)S(1)} %get-tuple-element.72), channel_id=1, source_target_pairs={{0,1},{1,2},{2,3},{3,4},{4,5},{5,6},{6,7},{8,9},{9,10},{10,11},{11... | collective-permute-start | bytes 393224 | tf_op jit(solution)/shard_map/ppermute | solution.py:614
  44.7 7.7 %collective-permute-start.7 = (f32[16,8,256]{2,1,0:T(8,128)S(1)}, f32[16,8,256]{2,1,0:T(8,128)S(1)}, u32[]{:S(2)}, u32[]{:S(2)}) collective-permute-start(f32[16,8,256]{2,1,0:T(8,128)S(1)} %get-tuple-element.73), channel_id=1, source_target_pairs={{1,0},{2,1},{3,2},{4,3},{5,4},{6,5},{7,6},{9,8},{10,9},{11,10},{12... | collective-permute-start | bytes 393224 | tf_op jit(solution)/shard_map/ppermute | solution.py:614
  52.4 8.4 %collective-permute-start.8 = (f32[2,4,40,256]{3,2,1,0:T(8,128)S(1)}, f32[2,4,40,256]{3,2,1,0:T(8,128)S(1)}, u32[]{:S(2)}, u32[]{:S(2)}) collective-permute-start(f32[2,4,40,256]{3,2,1,0:T(8,128)S(1)} %get-tuple-element.76), channel_id=1, source_target_pairs={{0,8},{8,16},{16,24},{1,9},{9,17},{17,25},{2,10},{10,18},{18,26},{... | collective-permute-start | bytes 983048 | tf_op jit(solution)/shard_map/ppermute | solution.py:614
  54.8 6.1 %collective-permute-start.9 = (f32[2,4,40,256]{3,2,1,0:T(8,128)S(1)}, f32[2,4,40,256]{3,2,1,0:T(8,128)S(1)}, u32[]{:S(2)}, u32[]{:S(2)}) collective-permute-start(f32[2,4,40,256]{3,2,1,0:T(8,128)S(1)} %get-tuple-element.77), channel_id=1, source_target_pairs={{8,0},{16,8},{24,16},{9,1},{17,9},{25,17},{10,2},{18,10},{26,18},{... | collective-permute-start | bytes 983048 | tf_op jit(solution)/shard_map/ppermute | solution.py:614

commit v8 on v7

--- a/solution.py
+++ b/solution.py
@@ -12,7 +12,7 @@
 F32 = jnp.float32
 LIMIT = 24 * 1024 * 1024
 SCALE = 160.0
-CHUNKS = 4
+CHUNKS = 8
 FALLBACK = (0.72, -0.28)
 
 
@@ -573,7 +573,7 @@
     copies = []
     for k in range(CHUNKS):
         lo, hi = k * nx // CHUNKS, (k + 1) * nx // CHUNKS
-        lax.fori_loop(lo, hi, body, 0)
+        lax.fori_loop(lo, hi, body, 0, unroll=2)
         span = pl.ds(lo, hi - lo)
         for a, b in ((sol_ref, sol_any), (res_ref, res_any)):
             copies.append(

time: 80.4 us -> 80.3 us (level)
  no operation moved by 1% of the time
where the time goes in v8:
time: 80.3 us; the launch traced here: 79.9 us
  blocking collectives  29.9 us (37%)
  Pallas kernels  23.9 us (30%)
  starting transfers between devices  19.7 us (25%)
  waiting for transfers between devices  5.54 us (7%)
  between operations  0.81 us (1%)
    all_to_all x1, blocking collectives, local(): th = lax.all_to_all(th, AXES, 0, 0)  16.4 us
    pallas_call x7, Pallas kernels, call(): pl.pallas_call(kernel, out_shape=[jax.ShapeDtypeStruct(s, F32) for s in o...  15.5 us
    all_to_all x1, blocking collectives, local(): gram = lax.all_to_all(gram, AXES, 0, 0)  13.5 us
    ppermute x5, starting transfers between devices, both_ways(): lax.ppermute(to_upper, axis, up)  13.2 us
    ppermute x5, starting transfers between devices, both_ways(): lax.ppermute(to_lower, axis, down)  6.46 us
    pallas_call x2, Pallas kernels, edge_call(): pl.pallas_call(kernel, out_shape=[jax.ShapeDtypeStruct(s, F32) for s in o...  6.05 us
    ppermute x5, waiting for transfers between devices, both_ways(): lax.ppermute(to_lower, axis, down)  4.73 us
    pallas_call x1, Pallas kernels, local(): pl.pallas_call(final_kernel, out_shape=[jax.ShapeDtypeStruct(own, F32)] *...  2.4 us
  transfers between devices with their start and end apart: 10, of which 2 were waited for; matrix products, arithmetic and copies ran while one was open for 0% of the time, Pallas kernels for 17%

profile of v8, /device:TPU:0, one launch (start us, length us, event | category | flops | bytes accessed | tf_op | source)
XLA Modules:
  0.0 79.9 jit_solution(5103809277486627195)
XLA Ops:
  0.6 2.2 %shard_map.69 = (f32[5,4,32,256]{3,2,1,0:T(8,128)S(1)}, f32[5,4,32,256]{3,2,1,0:T(8,128)S(1)}, f32[40,8,256]{2,1,0:T(8,128)S(1)}, f32[40,8,256]{2,1,0:T(8,128)S(1)}) custom-call(f32[2,16,32,256]{3,2,1,0:T(8,128)} %b_ref.1, f32[16,32,256]{2,1,0:T(8,128)} %cf_ref.1, f32[16,32,256]{2,1,0:T(8,128)} %ct_ref.1, f32[16,32,256]{2,1,0:T(8,128)} %mr_ref.1, ...), custom_call_target="tpu_custom_call" | custom-call | tf_op jit(solution)/shard_map/pallas_call | solution.py:600
  2.8 2.4 %collective-permute-start.4 = (f32[5,4,32,256]{3,2,1,0:T(8,128)S(1)}, f32[5,4,32,256]{3,2,1,0:T(8,128)S(1)}, u32[]{:S(2)}, u32[]{:S(2)}) collective-permute-start(f32[5,4,32,256]{3,2,1,0:T(8,128)S(1)} %get-tuple-element.54), channel_id=1, source_target_pairs={{0,8},{8,16},{16,24},{1,9},{9,17},{17,25},{2,10},{10,18},{18,26},{... | collective-permute-start | bytes 1966088 | tf_op jit(solution)/shard_map/ppermute | solution.py:614
  5.2 1.3 %collective-permute-start.5 = (f32[5,4,32,256]{3,2,1,0:T(8,128)S(1)}, f32[5,4,32,256]{3,2,1,0:T(8,128)S(1)}, u32[]{:S(2)}, u32[]{:S(2)}) collective-permute-start(f32[5,4,32,256]{3,2,1,0:T(8,128)S(1)} %get-tuple-element.55), channel_id=1, source_target_pairs={{8,0},{16,8},{24,16},{9,1},{17,9},{25,17},{10,2},{18,10},{26,18},{... | collective-permute-start | bytes 1966088 | tf_op jit(solution)/shard_map/ppermute | solution.py:614
  6.5 4.2 %collective-permute-start = (f32[40,8,256]{2,1,0:T(8,128)S(1)}, f32[40,8,256]{2,1,0:T(8,128)S(1)}, u32[]{:S(2)}, u32[]{:S(2)}) collective-permute-start(f32[40,8,256]{2,1,0:T(8,128)S(1)} %get-tuple-element.50), channel_id=1, source_target_pairs={{0,1},{1,2},{2,3},{3,4},{4,5},{5,6},{6,7},{8,9},{9,10},{10,11},{11... | collective-permute-start | bytes 983048 | tf_op jit(solution)/shard_map/ppermute | solution.py:614
  10.8 1.3 %collective-permute-start.1 = (f32[40,8,256]{2,1,0:T(8,128)S(1)}, f32[40,8,256]{2,1,0:T(8,128)S(1)}, u32[]{:S(2)}, u32[]{:S(2)}) collective-permute-start(f32[40,8,256]{2,1,0:T(8,128)S(1)} %get-tuple-element.51), channel_id=1, source_target_pairs={{1,0},{2,1},{3,2},{4,3},{5,4},{6,5},{7,6},{9,8},{10,9},{11,10},{12... | collective-permute-start | bytes 983048 | tf_op jit(solution)/shard_map/ppermute | solution.py:614
  12.1 3.9 %shard_map.68 = (f32[2,24,40,256]{3,2,1,0:T(8,128)S(1)}, f32[2,24,40,256]{3,2,1,0:T(8,128)S(1)}, f32[2,24,40,256]{3,2,1,0:T(8,128)S(1)}, f32[2,24,40,256]{3,2,1,...) custom-call(f32[2,16,32,256]{3,2,1,0:T(8,128)} %b_ref.1, ...), custom_call_target="tpu_custom_call" | custom-call | tf_op jit(solution)/shard_map/pallas_call | solution.py:600
  16.0 16.4 %all_to_all.10.after_ref.th_ref = f32[32,1,128]{2,1,0:T(1,128)S(1)} all-to-all(f32[32,1,128]{2,1,0:T(1,128)S(1)} %get-tuple-element.47), channel_id=1, replica_groups=mesh['gx'=4,'gy'=8] {'gx','gy'}, dimensions={0} | all-to-all | bytes 32768 | tf_op jit(solution)/shard_map/all_to_all | solution.py:638
  32.4 0.0 collective-permute-done.1.yr_ref
  32.4 1.8 %collective-permute-start.2 = (f32[2,10,8,256]{3,2,1,0:T(8,128)S(1)}, f32[2,10,8,256]{3,2,1,0:T(8,128)S(1)}, u32[]{:S(2)}, u32[]{:S(2)}) collective-permute-start(f32[2,10,8,256]{3,2,1,0:T(8,128)S(1)} %get-tuple-element.52), channel_id=1, source_target_pairs={{0,8},{8,16},{16,24},{1,9},{9,17},{17,25},{2,10},{10,18},{18,26},{... | collective-permute-start | bytes 491528 | tf_op jit(solution)/shard_map/ppermute | solution.py:614
  34.2 1.3 %collective-permute-start.3 = (f32[2,10,8,256]{3,2,1,0:T(8,128)S(1)}, f32[2,10,8,256]{3,2,1,0:T(8,128)S(1)}, u32[]{:S(2)}, u32[]{:S(2)}) collective-permute-start(f32[2,10,8,256]{3,2,1,0:T(8,128)S(1)} %get-tuple-element.53), channel_id=1, source_target_pairs={{8,0},{16,8},{24,16},{9,1},{17,9},{25,17},{10,2},{18,10},{26,18},{... | collective-permute-start | bytes 491528 | tf_op jit(solution)/shard_map/ppermute | solution.py:614
  35.5 4.3 %shard_map.71 = (f32[2,24,40,256]{3,2,1,0:T(8,128)S(1)}, f32[2,24,40,256]{3,2,1,0:T(8,128)S(1)}, f32[2,24,40,256]{3,2,1,0:T(8,128)S(1)}, f32[2,24,40,256]{3,2,1,...) custom-call(f32[32,1,128]{2,1,0:T(1,128)S(1)} %all_to_all.10.after_r, ...), custom_call_target="tpu_custom_call", output_to_operand_aliasing={{0}: (5, {}), {1}: (6, {}), {2}: (7, {}), {3}: (8, {})} | custom-call | tf_op jit(solution)/shard_map/pallas_call | solution.py:588
  39.8 2.4 %shard_map.72 = (f32[2,24,40,256]{3,2,1,0:T(8,128)S(1)}, f32[2,24,40,256]{3,2,1,0:T(8,128)S(1)}, f32[2,24,40,256]{3,2,1,0:T(8,128)S(1)}, f32[2,24,40,256]{3,2,1,...) custom-call(f32[32,1,128]{2,1,0:T(1,128)S(1)} %all_to_all.10.after_r, ...), custom_call_target="tpu_custom_call", output_to_operand_aliasing={{0}: (3, {}), {1}: (4, {}), {2}: (5, {}), {3}: (6, {}), {4}... | custom-call | tf_op jit(solution)/shard_map/pallas_call | solution.py:588
  42.1 2.5 %collective-permute-start.6 = (f32[16,8,256]{2,1,0:T(8,128)S(1)}, f32[16,8,256]{2,1,0:T(8,128)S(1)}, u32[]{:S(2)}, u32[]{:S(2)}) collective-permute-start(f32[16,8,256]{2,1,0:T(8,128)S(1)} %get-tuple-element.72), channel_id=1, source_target_pairs={{0,1},{1,2},{2,3},{3,4},{4,5},{5,6},{6,7},{8,9},{9,10},{10,11},{11... | collective-permute-start | bytes 393224 | tf_op jit(solution)/shard_map/ppermute | solution.py:614
  44.7 1.3 %collective-permute-start.7 = (f32[16,8,256]{2,1,0:T(8,128)S(1)}, f32[16,8,256]{2,1,0:T(8,128)S(1)}, u32[]{:S(2)}, u32[]{:S(2)}) collective-permute-start(f32[16,8,256]{2,1,0:T(8,128)S(1)} %get-tuple-element.73), channel_id=1, source_target_pairs={{1,0},{2,1},{3,2},{4,3},{5,4},{6,5},{7,6},{9,8},{10,9},{11,10},{12... | collective-permute-start | bytes 393224 | tf_op jit(solution)/shard_map/ppermute | solution.py:614
  46.0 0.9 %shard_map.73.e_ref = f32[1,1,128]{2,1,0:T(1,128)S(1)} custom-call(f32[2,16,32,256]{3,2,1,0:T(8,128)S(1)} %get-tuple-element.48.b_ref, f32[16,32,256]{2,1,0:T(8,128)S(1)} %get-tuple-element.49.ct_ref, f32[2,24,40,256]{3,2,1,0:T(8,128)S(1)} %get-tuple-element.68.v1_ref, f32[2,24,40,256]{3,2,1,0:T(8,128)S(1)} %get-tuple-element.69.v2_ref._), custom_call_target="tpu_custom_call" | custom-call | tf_op jit(solution)/shard_map/pallas_call | solution.py:588
  46.8 0.8 %collective-permute-done.6.yl_ref = f32[16,8,256]{2,1,0:T(8,128)S(1)} collective-permute-done((f32[16,8,256]{2,1,0:T(8,128)S(1)}, f32[16,8,256]{2,1,0:T(8,128)S(1)}, u32[]{:S(2)}, u32[]{:S(2)}) %collective-permute-start.6) | collective-permute-done | bytes 131104 | tf_op jit(solution)/shard_map/ppermute | solution.py:614
  47.6 4.7 %collective-permute-done.7.yr_ref = f32[16,8,256]{2,1,0:T(8,128)S(1)} collective-permute-done((f32[16,8,256]{2,1,0:T(8,128)S(1)}, f32[16,8,256]{2,1,0:T(8,128)S(1)}, u32[]{:S(2)}, u32[]{:S(2)}) %collective-permute-start.7) | collective-permute-done | bytes 131104 | tf_op jit(solution)/shard_map/ppermute | solution.py:614
  52.4 0.1 shard_map.74
  52.4 2.3 %collective-permute-start.8 = (f32[2,4,40,256]{3,2,1,0:T(8,128)S(1)}, f32[2,4,40,256]{3,2,1,0:T(8,128)S(1)}, u32[]{:S(2)}, u32[]{:S(2)}) collective-permute-start(f32[2,4,40,256]{3,2,1,0:T(8,128)S(1)} %get-tuple-element.76), channel_id=1, source_target_pairs={{0,8},{8,16},{16,24},{1,9},{9,17},{17,25},{2,10},{10,18},{18,26},{... | collective-permute-start | bytes 983048 | tf_op jit(solution)/shard_map/ppermute | solution.py:614
  54.8 1.3 %collective-permute-start.9 = (f32[2,4,40,256]{3,2,1,0:T(8,128)S(1)}, f32[2,4,40,256]{3,2,1,0:T(8,128)S(1)}, u32[]{:S(2)}, u32[]{:S(2)}) collective-permute-start(f32[2,4,40,256]{3,2,1,0:T(8,128)S(1)} %get-tuple-element.77), channel_id=1, source_target_pairs={{8,0},{16,8},{24,16},{9,1},{17,9},{25,17},{10,2},{18,10},{26,18},{... | collective-permute-start | bytes 983048 | tf_op jit(solution)/shard_map/ppermute | solution.py:614
  56.1 4.7 %shard_map.75 = (f32[2,24,40,256]{3,2,1,0:T(8,128)S(1)}, f32[2,24,40,256]{3,2,1,0:T(8,128)S(1)}, f32[2,24,40,256]{3,2,1,0:T(8,128)S(1)}, f32[2,24,40,256]{3,2,1,...) custom-call(f32[32,1,128]{2,1,0:T(1,128)S(1)} %all_to_all.10.after_ref.th_ref, ...), custom_call_target="tpu_custom_call" | custom-call | tf_op jit(solution)/shard_map/pallas_call | solution.py:588
  60.9 3.1 %shard_map.76 = (f32[2,24,40,256]{3,2,1,0:T(8,128)S(1)}, f32[2,24,40,256]{3,2,1,0:T(8,128)S(1)}, f32[2,24,40,256]{3,2,1,0:T(8,128)S(1)}, f32[2,24,40,256]{3,2,1,...) custom-call(f32[32,1,128]{2,1,0:T(1,128)S(1)} %all_to_all.10.after_r, ...), custom_call_target="tpu_custom_call", output_to_operand_aliasing={{0}: (9, {}), {1}: (10, {}), {2}: (11, {}), {3}: (12, {}), ... | custom-call | tf_op jit(solution)/shard_map/pallas_call | solution.py:588
  64.0 13.5 %all_to_all.11.g_ref = f32[32,1,128]{2,1,0:T(1,128)S(1)} all-to-all(f32[32,1,128]{2,1,0:T(1,128)S(1)} %get-tuple-element.83), channel_id=1, replica_groups=mesh['gx'=4,'gy'=8] {'gx','gy'}, dimensions={0} | all-to-all | bytes 32768 | tf_op jit(solution)/shard_map/all_to_all | solution.py:661
  77.5 2.4 %shard_map.77 = (f32[2,16,32,256]{3,2,1,0:T(8,128)}, f32[2,16,32,256]{3,2,1,0:T(8,128)}) custom-call(f32[32,1,128]{2,1,0:T(1,128)S(1)} %all_to_all.10.after_ref.th_ref, f32[32,1,128]{2,1,0:T(1,128)S(1)} %all_to_all.11.g_ref, f32[2,16,32,256]{3,2,1,0:T(8,128)S(1)} %get-tuple-element.48.b_ref, f32[16,32,256]{2,1,0:T(8,128)S(1)} %get-tuple-element.84.cf_ref, ...), custom_call_target="tpu_custom_call" | custom-call | tf_op jit(solution)/shard_map/pallas_call | solution.py:664
  (8 shorter events, 0.0 us)
Async XLA Ops:
  2.8 32.7 %collective-permute-start.4 = (f32[5,4,32,256]{3,2,1,0:T(8,128)S(1)}, f32[5,4,32,256]{3,2,1,0:T(8,128)S(1)}, u32[]{:S(2)}, u32[]{:S(2)}) collective-permute-start(f32[5,4,32,256]{3,2,1,0:T(8,128)S(1)} %get-tuple-element.54), channel_id=1, source_target_pairs={{0,8},{8,16},{16,24},{1,9},{9,17},{17,25},{2,10},{10,18},{18,26},{... | collective-permute-start | bytes 1966088 | tf_op jit(solution)/shard_map/ppermute | solution.py:614
  5.2 30.3 %collective-permute-start.5 = (f32[5,4,32,256]{3,2,1,0:T(8,128)S(1)}, f32[5,4,32,256]{3,2,1,0:T(8,128)S(1)}, u32[]{:S(2)}, u32[]{:S(2)}) collective-permute-start(f32[5,4,32,256]{3,2,1,0:T(8,128)S(1)} %get-tuple-element.55), channel_id=1, source_target_pairs={{8,0},{16,8},{24,16},{9,1},{17,9},{25,17},{10,2},{18,10},{26,18},{... | collective-permute-start | bytes 1966088 | tf_op jit(solution)/shard_map/ppermute | solution.py:614
  6.5 25.9 %collective-permute-start = (f32[40,8,256]{2,1,0:T(8,128)S(1)}, f32[40,8,256]{2,1,0:T(8,128)S(1)}, u32[]{:S(2)}, u32[]{:S(2)}) collective-permute-start(f32[40,8,256]{2,1,0:T(8,128)S(1)} %get-tuple-element.50), channel_id=1, source_target_pairs={{0,1},{1,2},{2,3},{3,4},{4,5},{5,6},{6,7},{8,9},{9,10},{10,11},{11... | collective-permute-start | bytes 983048 | tf_op jit(solution)/shard_map/ppermute | solution.py:614
  10.8 21.6 %collective-permute-start.1 = (f32[40,8,256]{2,1,0:T(8,128)S(1)}, f32[40,8,256]{2,1,0:T(8,128)S(1)}, u32[]{:S(2)}, u32[]{:S(2)}) collective-permute-start(f32[40,8,256]{2,1,0:T(8,128)S(1)} %get-tuple-element.51), channel_id=1, source_target_pairs={{1,0},{2,1},{3,2},{4,3},{5,4},{6,5},{7,6},{9,8},{10,9},{11,10},{12... | collective-permute-start | bytes 983048 | tf_op jit(solution)/shard_map/ppermute | solution.py:614
  32.4 7.4 %collective-permute-start.2 = (f32[2,10,8,256]{3,2,1,0:T(8,128)S(1)}, f32[2,10,8,256]{3,2,1,0:T(8,128)S(1)}, u32[]{:S(2)}, u32[]{:S(2)}) collective-permute-start(f32[2,10,8,256]{3,2,1,0:T(8,128)S(1)} %get-tuple-element.52), channel_id=1, source_target_pairs={{0,8},{8,16},{16,24},{1,9},{9,17},{17,25},{2,10},{10,18},{18,26},{... | collective-permute-start | bytes 491528 | tf_op jit(solution)/shard_map/ppermute | solution.py:614
  34.2 5.6 %collective-permute-start.3 = (f32[2,10,8,256]{3,2,1,0:T(8,128)S(1)}, f32[2,10,8,256]{3,2,1,0:T(8,128)S(1)}, u32[]{:S(2)}, u32[]{:S(2)}) collective-permute-start(f32[2,10,8,256]{3,2,1,0:T(8,128)S(1)} %get-tuple-element.53), channel_id=1, source_target_pairs={{8,0},{16,8},{24,16},{9,1},{17,9},{25,17},{10,2},{18,10},{26,18},{... | collective-permute-start | bytes 491528 | tf_op jit(solution)/shard_map/ppermute | solution.py:614
  42.1 5.5 %collective-permute-start.6 = (f32[16,8,256]{2,1,0:T(8,128)S(1)}, f32[16,8,256]{2,1,0:T(8,128)S(1)}, u32[]{:S(2)}, u32[]{:S(2)}) collective-permute-start(f32[16,8,256]{2,1,0:T(8,128)S(1)} %get-tuple-element.72), channel_id=1, source_target_pairs={{0,1},{1,2},{2,3},{3,4},{4,5},{5,6},{6,7},{8,9},{9,10},{10,11},{11... | collective-permute-start | bytes 393224 | tf_op jit(solution)/shard_map/ppermute | solution.py:614
  44.7 7.7 %collective-permute-start.7 = (f32[16,8,256]{2,1,0:T(8,128)S(1)}, f32[16,8,256]{2,1,0:T(8,128)S(1)}, u32[]{:S(2)}, u32[]{:S(2)}) collective-permute-start(f32[16,8,256]{2,1,0:T(8,128)S(1)} %get-tuple-element.73), channel_id=1, source_target_pairs={{1,0},{2,1},{3,2},{4,3},{5,4},{6,5},{7,6},{9,8},{10,9},{11,10},{12... | collective-permute-start | bytes 393224 | tf_op jit(solution)/shard_map/ppermute | solution.py:614
  52.4 8.4 %collective-permute-start.8 = (f32[2,4,40,256]{3,2,1,0:T(8,128)S(1)}, f32[2,4,40,256]{3,2,1,0:T(8,128)S(1)}, u32[]{:S(2)}, u32[]{:S(2)}) collective-permute-start(f32[2,4,40,256]{3,2,1,0:T(8,128)S(1)} %get-tuple-element.76), channel_id=1, source_target_pairs={{0,8},{8,16},{16,24},{1,9},{9,17},{17,25},{2,10},{10,18},{18,26},{... | collective-permute-start | bytes 983048 | tf_op jit(solution)/shard_map/ppermute | solution.py:614
  54.8 6.1 %collective-permute-start.9 = (f32[2,4,40,256]{3,2,1,0:T(8,128)S(1)}, f32[2,4,40,256]{3,2,1,0:T(8,128)S(1)}, u32[]{:S(2)}, u32[]{:S(2)}) collective-permute-start(f32[2,4,40,256]{3,2,1,0:T(8,128)S(1)} %get-tuple-element.77), channel_id=1, source_target_pairs={{8,0},{16,8},{24,16},{9,1},{17,9},{25,17},{10,2},{18,10},{26,18},{... | collective-permute-start | bytes 983048 | tf_op jit(solution)/shard_map/ppermute | solution.py:614
